TPU v7x, 512 devices: a whole 4x8x8 slice. The times are simulated.
512 devices in a mesh: seq: 128 (over z, y, core), grp: 4 (over x).
Axes of the slice: x: 4, y: 8, z: 8, core: 2. Of those that a mesh axis runs over, the one named last changes fastest.
Arguments:
- q_pre: bfloat16 [8192, 4096], P('seq', 'grp'), may hold values from -180 to 180, as said below
- k_pre: bfloat16 [8192, 1024], P('seq', 'grp'), may hold values from -6 to 6
- v_pre: bfloat16 [8192, 1024], P('seq', 'grp'), may hold values from -6 to 6
- old_k: bfloat16 [128, 40, 16, 1024], P('seq', 'grp'), may hold values from -6 to 6
- old_v: bfloat16 [128, 40, 16, 1024], P('seq', 'grp'), may hold values from -6 to 6
- src_page: int32 [128, 8], P('seq'), may hold values from 0 to 511
- page_row: int32 [128, 48], P('seq', 'grp'), may hold values from 0 to 31
- page_len: int32 [128, 48], P('seq', 'grp'), may hold values from 1 to 16
- q_dec: bfloat16 [32, 4, 4096], replicated, may hold values from -180 to 180, as said below
- dec_k: bfloat16 [32, 4, 1024], replicated, may hold values from -6 to 6
- dec_v: bfloat16 [32, 4, 1024], replicated, may hold values from -6 to 6
Outputs:
- attn_pre: bfloat16 [8192, 4096], P('seq', 'grp')
- dec_out: bfloat16 [4096, 128], P(('seq', 'grp'))
Inputs may be any that keep to these rules, and one draw needn't show every extreme that they name: `q_pre`: queries of the prefill block. `q_dec`: queries of the decode rows.
All inputs are finite; a program needn't handle non-finite values.
Results may differ from a plain program's by a relative error of at most 0.01025.
Values may be sent and summed in bfloat16 or wider, within the bound.
No kernel may reach another device: no remote copies, remote signals or barrier semaphores. Data moves between devices by JAX's collectives and lax.ppermute only.
A program may use at most 64 MiB of HBM per device.

v0:
```python
import math

import jax
import jax.numpy as jnp
from jax import lax
from jax.sharding import PartitionSpec as P

HEAD = 128
QH = 32
PAGE = 16
ROWS = 32
STEPS = 4


NEG = -1e30


def attend_block(state, q_block, keys, values, q_pos, k_pos, scale):
    m_run, l_run, o_run = state
    scores = jnp.einsum("tgjd,ugd->tgju", q_block, keys, preferred_element_type=jnp.float32) * scale
    allowed = (k_pos[None, :] <= q_pos[:, None])[:, None, None, :]
    scores = jnp.where(allowed, scores, NEG)
    m_new = jnp.maximum(m_run, jnp.max(scores, axis=-1))
    weights = jnp.where(allowed, jnp.exp(scores - m_new[..., None]), 0.0).astype(jnp.bfloat16)
    factor = jnp.exp(m_run - m_new)
    l_new = l_run * factor + jnp.sum(weights.astype(jnp.float32), axis=-1)
    o_new = o_run * factor[..., None] + jnp.einsum(
        "tgju,ugd->tgjd", weights, values, preferred_element_type=jnp.float32
    )
    return (m_new, l_new, o_new)


def pick_tokens(source, token_idx, begin):
    local = token_idx - begin
    inside = (local >= 0) & (local < source.shape[0])
    taken = source[jnp.clip(local, 0, source.shape[0] - 1)]
    return (inside, taken)


def empty_state(count, kv_local, gqa, head):
    return (
        jnp.full((count, kv_local, gqa), NEG, jnp.float32),
        jnp.zeros((count, kv_local, gqa), jnp.float32),
        jnp.zeros((count, kv_local, gqa, head), jnp.float32),
    )


def body(q_pre, k_pre, v_pre, old_k, old_v, src_page, page_row, page_len, q_dec, dec_k, dec_v):
    rows = q_pre.shape[0]
    head = HEAD
    kv_local = k_pre.shape[1] // head
    gqa = q_pre.shape[1] // (kv_local * head)
    scale = 1.0 / HEAD**0.5
    seq_count = lax.axis_size("seq")
    seq_index = lax.axis_index("seq")
    grp_count = lax.axis_size("grp")
    newp = src_page.shape[1] // grp_count
    q_sets = (
        q_pre.reshape(rows, kv_local, gqa, head),
        seq_index * rows + jnp.arange(rows, dtype=jnp.int32),
    )
    wanted = src_page[0].reshape(grp_count, newp).T
    token_idx = wanted[:, None, :] * PAGE + jnp.arange(PAGE, dtype=jnp.int32)[None, :, None]
    keys_all, values_all = (
        lax.all_gather(k_pre, "seq", axis=0, tiled=True),
        lax.all_gather(v_pre, "seq", axis=0, tiled=True),
    )
    total_rows = keys_all.shape[0]
    power = 2 ** (max(1, 1024 // rows).bit_length() - 1)
    span = rows * math.gcd(seq_count, power)
    keys4 = keys_all.reshape(total_rows, kv_local, head)
    values4 = values_all.reshape(total_rows, kv_local, head)
    q_block, q_pos = q_sets
    needed = (jnp.max(q_pos) + span) // span

    def step(count, carry, q_block=q_block, q_pos=q_pos):
        begin = count * span
        keys = lax.dynamic_slice_in_dim(keys4, begin, span, 0)
        values = lax.dynamic_slice_in_dim(values4, begin, span, 0)
        k_pos = begin + jnp.arange(span, dtype=jnp.int32)
        return attend_block(carry, q_block, keys, values, q_pos, k_pos, scale)

    states = lax.fori_loop(0, needed, step, empty_state(q_block.shape[0], kv_local, gqa, head))
    inside, pages_k = pick_tokens(keys_all, token_idx, 0)
    inside, pages_v = pick_tokens(values_all, token_idx, 0)
    m_run, l_run, o_run = states
    outputs = (o_run / l_run[..., None]).astype(jnp.bfloat16).reshape(m_run.shape[0], -1)
    fresh_k, fresh_v = (
        lax.all_to_all(pages_k, "grp", split_axis=2, concat_axis=2, tiled=True),
        lax.all_to_all(pages_v, "grp", split_axis=2, concat_axis=2, tiled=True),
    )
    pool_k = jnp.concatenate([old_k[0], fresh_k.reshape(newp, PAGE, -1)], axis=0)
    pool_v = jnp.concatenate([old_v[0], fresh_v.reshape(newp, PAGE, -1)], axis=0)
    kv_full = pool_k.shape[-1] // head
    owners = page_row[0]
    lengths = page_len[0]
    pool_count = owners.shape[0]
    q_page = q_dec[owners].reshape(pool_count, STEPS, kv_full, gqa, head)
    k_page = pool_k.reshape(pool_count, PAGE, kv_full, head)
    v_page = pool_v.reshape(pool_count, PAGE, kv_full, head)
    scores = (
        jnp.einsum("psgjd,ptgd->psgjt", q_page, k_page, preferred_element_type=jnp.float32) * scale
    )
    valid = (jnp.arange(PAGE, dtype=jnp.int32)[None, :] < lengths[:, None])[:, None, None, None, :]
    scores = jnp.where(valid, scores, NEG)
    page_top = jnp.max(scores, axis=-1)
    hit = owners[None, :] == jnp.arange(ROWS, dtype=jnp.int32)[:, None]
    row_top = jnp.max(jnp.where(hit[:, :, None, None, None], page_top[None], NEG), axis=1)
    items = ROWS * STEPS * QH
    per = items // lax.axis_size(("seq", "grp"))
    first = lax.axis_index(("seq", "grp")) * per
    top_all = lax.pmax(row_top, ("seq", "grp"))
    weights = jnp.where(valid, jnp.exp(scores - top_all[owners][..., None]), 0.0).astype(
        jnp.bfloat16
    )
    page_mix = jnp.einsum("psgjt,ptgd->psgjd", weights, v_page, preferred_element_type=jnp.float32)
    total = jax.ops.segment_sum(jnp.sum(weights.astype(jnp.float32), axis=-1), owners, ROWS)
    mixed = jax.ops.segment_sum(page_mix, owners, ROWS)
    total, mixed = (total, mixed)
    total_mine, mixed_mine = (
        lax.psum_scatter(total.reshape(items), ("seq", "grp"), scatter_dimension=0, tiled=True),
        lax.psum_scatter(
            mixed.reshape(items, head), ("seq", "grp"), scatter_dimension=0, tiled=True
        ),
    )
    top_mine = lax.dynamic_slice_in_dim(top_all.reshape(items), first, per, 0)
    item_ids = first + jnp.arange(per, dtype=jnp.int32)
    row_of = item_ids // (STEPS * QH)
    step_of = item_ids // QH % STEPS
    kv_of = item_ids % QH // gqa
    q_items = lax.dynamic_slice_in_dim(q_dec.reshape(items, head), first, per, 0)
    own_keys = dec_k.reshape(ROWS, STEPS, kv_full, head)[row_of, :, kv_of]
    own_vals = dec_v.reshape(ROWS, STEPS, kv_full, head)[row_of, :, kv_of]
    own_scores = (
        jnp.einsum("nd,nud->nu", q_items, own_keys, preferred_element_type=jnp.float32) * scale
    )
    causal = jnp.arange(STEPS, dtype=jnp.int32)[None, :] <= step_of[:, None]
    own_scores = jnp.where(causal, own_scores, NEG)
    top = jnp.maximum(top_mine, jnp.max(own_scores, axis=-1))
    own_w = jnp.where(causal, jnp.exp(own_scores - top[:, None]), 0.0).astype(jnp.bfloat16)
    factor = jnp.exp(top_mine - top)
    total_all_terms = total_mine * factor + jnp.sum(own_w.astype(jnp.float32), axis=-1)
    mixed_all_terms = mixed_mine * factor[:, None] + jnp.einsum(
        "nu,nud->nd", own_w, own_vals, preferred_element_type=jnp.float32
    )
    dec_out = (mixed_all_terms / total_all_terms[:, None]).astype(jnp.bfloat16)
    return (outputs, dec_out)


def solution(mesh):
    return jax.shard_map(
        body,
        mesh=mesh,
        in_specs=(
            P("seq", "grp"),
            P("seq", "grp"),
            P("seq", "grp"),
            P("seq", "grp", None, None),
            P("seq", "grp", None, None),
            P("seq", None),
            P("seq", "grp"),
            P("seq", "grp"),
            P(),
            P(),
            P(),
        ),
        out_specs=(P("seq", "grp"), P(("seq", "grp"), None)),
        check_vma=False,
    )
```

profile of v0, /device:TPU:1, one launch (start us, length us, event | category | flops | bytes accessed | tf_op | source)
XLA Modules:
  0.0 623.8 jit_solution(108940886322527567)
XLA Ops:
  11.5 1.5 gather_fusion.4
  13.1 1.0 reshape.341
  14.8 1.0 copy.88
  16.8 1.1 reshape.347
  19.7 82.1 %all-gather.3.cloned.1.call-done = bf16[8192,256]{1,0:T(8,128)(2,1)} async-done(((bf16[64,256]{1,0:T(8,128)(2,1)}), bf16[8192,256]{1,0:T(8,128)(2,1)}) %all-gather.3.cloned.1.call-update) | async-done | bytes 4194320 | tf_op jit(solution)/shard_map/all_gather | solution.py:65
  101.8 3.5 gather_fusion.1
  105.9 4.0 all-to-all-start.1
  109.9 6.9 %reshape.340 = bf16[8192,2,128]{2,1,0:T(2,128)(2,1)} reshape(bf16[8192,256]{1,0:T(8,128)(2,1)} %all-gather.3.cloned.1.call-done) | data formatting | bytes 8388608 | tf_op jit(solution)/shard_map/reshape | solution.py:71
  116.8 69.6 %all-gather.5.cloned.1.call-done = bf16[8192,256]{1,0:T(8,128)(2,1)} async-done(((bf16[64,256]{1,0:T(8,128)(2,1)}), bf16[8192,256]{1,0:T(8,128)(2,1)}) %all-gather.5.cloned.1.call-update) | async-done | bytes 4194320 | tf_op jit(solution)/shard_map/all_gather | solution.py:66
  186.4 6.9 %reshape.342 = bf16[8192,2,128]{2,1,0:T(2,128)(2,1)} reshape(bf16[8192,256]{1,0:T(8,128)(2,1)} %all-gather.5.cloned.1.call-done) | data formatting | bytes 8388608 | tf_op jit(solution)/shard_map/reshape | solution.py:72
  193.4 4.2 while.15
  193.6 1.9 constant_dynamic-slice_fusion.3
  197.8 3.5 gather_fusion
  202.8 4.0 all-to-all-start
  208.5 126.7 %pmax.7 = f32[32,4,8,4]{2,3,1,0:T(4,128)S(1)} all-reduce(f32[32,4,8,4]{2,3,1,0:T(4,128)S(1)} %copy.70), channel_id=1, replica_groups=mesh['seq'=128,'grp'=4] {'seq','grp'}, use_global_device_ids=true, to_apply=%region_7.8 | all-reduce | flops 4096 | bytes 32768 | tf_op jit(solution)/shard_map/pmax | solution.py:112
  335.8 1.6 copy.74
  339.0 1.4 scatter_fusion
  340.4 1.9 copy.73
  342.3 1.1 copy-done.4
  343.4 1.1 convert_reduce_fusion.1
  345.0 1.1 scatter_fusion.1
  347.6 95.1 %all-reduce.1 = f32[4096]{0:T(1024)S(1)} all-reduce(f32[4096]{0:T(1024)S(1)} %reshape.350), channel_id=3, replica_groups=mesh['seq'=128,'grp'=4] {'seq','grp'}, use_global_device_ids=true, to_apply=%region_13.14.clone | all-reduce | flops 4096 | bytes 32768
  442.9 173.1 %all-reduce.4.cloned.1.call-done = f32[4096,128]{1,0:T(8,128)} async-done(((f32[4096,128]{1,0:T(8,128)}), f32[4096,128]{1,0:T(8,128)}) %all-reduce.4.cloned.1.call-update) | async-done | bytes 2097168
  616.0 1.3 fusion.14
  (95 shorter events, 17.6 us)
Async XLA Ops:
  7.2 3.7 copy-start
  7.2 8.7 %copy-start.5 = (bf16[1,10,16,1024]{3,2,1,0:T(8,128)(2,1)S(1)}, bf16[1,10,16,1024]{3,2,1,0:T(8,128)(2,1)}, u32[]{:S(2)}) copy-start(bf16[1,10,16,1024]{3,2,1,0:T(8,128)(2,1)} %param.17) | copy-start | bytes 983044
  7.2 9.6 %copy-start.2 = (bf16[32,4,4096]{2,1,0:T(4,128)(2,1)S(1)}, bf16[32,4,4096]{2,1,0:T(4,128)(2,1)}, u32[]{:S(2)}) copy-start(bf16[32,4,4096]{2,1,0:T(4,128)(2,1)} %param.21) | copy-start | bytes 3145732
  7.2 94.6 %all-gather.3.cloned.1.call-start = ((), (), s32[]{:S(2)}) async-start(), calls=%async_computation.2 | async-start | bytes 4227072 | tf_op jit(solution)/shard_map/all_gather | solution.py:65
  7.9 178.5 %all-gather.5.cloned.1.call-start = ((), (), s32[]{:S(2)}) async-start(), calls=%async_computation.3 | async-start | bytes 4227072 | tf_op jit(solution)/shard_map/all_gather | solution.py:66
  15.8 2.1 copy-start.8
  16.0 3.5 copy-start.9
  105.9 96.9 %all-to-all-start.1 = ((bf16[2,16,4,256]{3,1,0,2:T(8,128)(2,1)}), bf16[2,16,4,256]{3,1,0,2:T(8,128)(2,1)S(1)}, u32[]{:S(2)}, u32[]{:S(2)}) async-start(bf16[2,16,4,256]{3,1,0,2:T(8,128)(2,1)} %copy.64), calls=%async_computation.1 | async-start | bytes 131072 | tf_op jit(solution)/shard_map/all_to_all | solution.py:89
  116.8 76.6 %copy-start.7 = (bf16[64,2,4,128]{3,0,2,1:T(8,128)(2,1)S(1)}, bf16[64,2,4,128]{3,0,2,1:T(8,128)(2,1)}, u32[]{:S(2)}) copy-start(bf16[64,2,4,128]{3,0,2,1:T(8,128)(2,1)} %copy.56) | copy-start | bytes 393220
  202.8 134.7 %all-to-all-start = ((bf16[2,16,4,256]{3,1,0,2:T(8,128)(2,1)}), bf16[2,16,4,256]{3,1,0,2:T(8,128)(2,1)S(1)}, u32[]{:S(2)}, u32[]{:S(2)}) async-start(bf16[2,16,4,256]{3,1,0,2:T(8,128)(2,1)} %copy.60), calls=%async_computation | async-start | bytes 131072 | tf_op jit(solution)/shard_map/all_to_all | solution.py:90
  206.7 409.2 %all-reduce.4.cloned.1.call-start = ((), (), s32[]{:S(2)}) async-start(), calls=%async_computation.4 | async-start | bytes 4194304
  207.6 130.9 %copy-start.3 = (f32[12,4,8,4,16]{4,3,1,2,0:T(4,128)}, f32[12,4,8,4,16]{4,3,1,2,0:T(4,128)S(1)}, u32[]{:S(2)}) copy-start(f32[12,4,8,4,16]{4,3,1,2,0:T(4,128)S(1)} %get-tuple-element.140) | copy-start | bytes 294916
  207.6 130.3 %copy-start.6 = (bf16[10,16,8,128]{3,1,2,0:T(8,128)(2,1)S(1)}, bf16[10,16,8,128]{3,1,2,0:T(8,128)(2,1)}, u32[]{:S(2)}) copy-start(bf16[10,16,8,128]{3,1,2,0:T(8,128)(2,1)} %copy.62) | copy-start | bytes 983044
  342.3 1.1 copy-start.4
  343.4 3.7 copy-start.1
Sparse Core Ops, SparseCore 0:
  11.2 90.5 all-gather.2
  104.9 81.4 all-gather.4
  342.5 273.4 all-reduce.3
where the time goes:
time: 625 us; the launch traced here: 624 us
  waiting for transfers between devices  326 us (52%)
  blocking collectives  222 us (36%)
  local copies, waits for them, and re-layouts  42.1 us (7%)
  between operations  14.8 us (2%)
  starting transfers between devices  8.01 us (1%)
  other arithmetic  7.86 us (1%)
    unnamed x4, waiting for transfers between devices  174 us
    pmax x1, blocking collectives, body(): top_all = lax.pmax(row_top, ('seq', 'grp'))  127 us
    unnamed x1, blocking collectives  95.1 us
    all_gather x1, waiting for transfers between devices, body(): lax.all_gather(k_pre, 'seq', axis=0, tiled=True)  82.1 us
    all_gather x1, waiting for transfers between devices, body(): lax.all_gather(v_pre, 'seq', axis=0, tiled=True)  69.6 us
  transfers between devices with their start and end apart: 5, of which 3 were waited for; matrix products, arithmetic and copies ran while one was open for 7% of the time, Pallas kernels for 0%

commit v1 on v0

v1 whole, which is shorter than its diff:
```python
import functools
import math

import jax
import jax.numpy as jnp
from jax import lax
from jax.experimental import pallas as pl
from jax.experimental.pallas import tpu as pltpu
from jax.sharding import PartitionSpec as P

HEAD = 128
PAGE = 16
OLD = 10
NEWP = 2
ROWS = 32
STEPS = 4
ITEMS = ROWS * STEPS
SIDE = 8
NG = 4
TOK = 64
BLK = 2 * TOK
KEYS = SIDE * BLK
QROWS = 4 * BLK
HEADS = 8
TWO = 2 * HEAD
EXP2_SCALE = math.log2(math.e) / math.sqrt(HEAD)
NEG = -(2.0**100)
HIDE = -(2.0**80)
LOWEST = -(2.0**60)
META = 16
KV_MSG = 2 * BLK + META
Q_MSG = QROWS + META
PAIR_MSG = 6 * TOK + META
HALF = OLD * PAGE
X_MSG = 2 * HALF + META
OLD_TOK = NG * HALF
DEC_TOK = OLD_TOK + 128
PER = ITEMS // SIDE
DEC_MSG = HEADS * PER + PER
O_MSG = Q_MSG + DEC_MSG
LAST_MSG = 4 * TOK + 16
NT = (((1,), (1,)), ((), ()))
F32 = jnp.float32
BF16 = jnp.bfloat16


def seq_of(z, y, core):
    return (z * SIDE + y) * 2 + core


ALONG_Z = [[[seq_of(i, j, c) for i in range(SIDE)] for j in range(SIDE)] for c in range(2)]
ALONG_Y = [[[seq_of(j, i, c) for i in range(SIDE)] for j in range(SIDE)] for c in range(2)]
KEY_GROUPS = ALONG_Z[0] + ALONG_Y[1]
QUERY_GROUPS = ALONG_Y[0] + ALONG_Z[1]


def iota(shape, dim):
    return lax.broadcasted_iota(jnp.int32, shape, dim)


def spot():
    seq, grp = lax.axis_index("seq"), lax.axis_index("grp")
    core = seq & 1
    y = (seq >> 1) & (SIDE - 1)
    z = seq >> 4
    even = core == 0
    return seq, grp, z, y, core, jnp.where(even, z, y), jnp.where(even, y, z)


def aligned(x, by):
    return pl.multiple_of(x, by)


def call(kernel, outs, args, scratch=(), limit=32, specs=None, out_specs=None, cost=None, alias=None):
    whole = pl.BlockSpec(memory_space=pltpu.VMEM)
    name = kernel.__name__.removesuffix("_kernel")
    return pl.pallas_call(
        kernel,
        out_shape=[jax.ShapeDtypeStruct(s, t) for s, t in outs],
        in_specs=[specs.get(n, whole) if specs else whole for n in range(len(args))],
        out_specs=out_specs or [whole] * len(outs),
        scratch_shapes=list(scratch),
        compiler_params=pltpu.CompilerParams(vmem_limit_bytes=limit * 1024 * 1024),
        cost_estimate=cost,
        input_output_aliases=alias or {},
        name=name,
    )(*args)


SMEM = pl.BlockSpec(memory_space=pltpu.SMEM)


def split_kernel(q, k, v, src_page, page_row, page_len, keep, send, src_s, row_s, len_s, sems):
    _, grp, z, y, core, w, u = spot()
    pairs = [(src_page, src_s), (page_row, row_s), (page_len, len_s)]
    for dst, head in ((keep, core), (send, 1 - core)):
        one = pl.ds(aligned(head * HEAD, HEAD), HEAD)
        pairs.append((k.at[:, one], dst.at[pl.ds(0, TOK), :]))
        pairs.append((v.at[:, one], dst.at[pl.ds(TOK, TOK), :]))
        for h in range(4):
            cols = pl.ds(aligned((head * 4 + h) * HEAD, HEAD), HEAD)
            pairs.append((q.at[:, cols], dst.at[pl.ds((2 + h) * TOK, TOK), :]))
    copies = [pltpu.make_async_copy(a, b, sems.at[n]) for n, (a, b) in enumerate(pairs)]
    for copy in copies:
        copy.start()
    for copy in copies[:3]:
        copy.wait()
    sub, lane = iota((META, 128), 0), iota((META, 128), 1)
    for dst, at in ((keep, w), (send, u)):
        tile = jnp.zeros((META, 128), F32)
        for n in range(NEWP):
            src = src_s[0, grp * NEWP + n]
            values = (src >> 2, src & 3, row_s[0, OLD + n], len_s[0, OLD + n])
            for m, value in enumerate(values):
                here = (lane == at * 4 + core * 2 + n) & ((sub & 3) == m) & (sub < 8)
                tile = jnp.where(here, value.astype(F32), tile)
        dst[6 * TOK :, :] = tile.astype(BF16)
    for copy in copies[3:]:
        copy.wait()


def keys_kernel(keep, got, kv_send, q_blk):
    core = spot()[4]
    for src, start in ((keep, core * TOK), (got, (1 - core) * TOK)):
        for n in range(2):
            kv_send[0, pl.ds(aligned(n * BLK + start, TOK), TOK), :] = src[n * TOK : (n + 1) * TOK, :]
        for h in range(4):
            q_blk[pl.ds(aligned(h * BLK + start, TOK), TOK), :] = src[
                (2 + h) * TOK : (3 + h) * TOK, :
            ]
    meta = keep[6 * TOK :, :].astype(F32) + got[6 * TOK :, :].astype(F32)
    kv_send[0, 2 * BLK :, :] = meta.astype(BF16)
    for n in range(1, SIDE):
        kv_send[n] = kv_send[0]


def queries_kernel(q_blk, kv, q_send):
    u = spot()[6]
    tile = sum(kv[n, 2 * BLK :, :].astype(F32) for n in range(SIDE))
    tile = pltpu.roll(tile, (u & 3) * 32, 1)
    tile = jnp.where(iota((META, 128), 0) >> 2 == u >> 2, tile, 0.0).astype(BF16)
    for n in range(SIDE):
        q_send[n, :QROWS, :] = q_blk[...]
        q_send[n, QROWS:, :] = tile


def pages_kernel(qs_far, old_k, old_v, page_row, page_len, x_send, qs, sem):
    copy = pltpu.make_async_copy(qs_far.at[:, pl.ds(QROWS, META), :], qs, sem)
    copy.start()
    copy.wait()
    sub, lane = iota((META, 128), 0), iota((META, 128), 1)
    tile = sum(qs[n].astype(F32) for n in range(SIDE))
    for n in range(OLD):
        tile = jnp.where((sub == 8) & (lane == n), page_row[0, n].astype(F32), tile)
        tile = jnp.where((sub == 9) & (lane == n), page_len[0, n].astype(F32), tile)
    for n in range(NG):
        x_send[n, :HALF, :] = old_k[:, n * TWO : (n + 1) * TWO]
        x_send[n, HALF : 2 * HALF, :] = old_v[:, n * TWO : (n + 1) * TWO]
        x_send[n, 2 * HALF :, :HEAD] = tile.astype(BF16)
        x_send[n, 2 * HALF :, HEAD:] = jnp.zeros((META, HEAD), BF16)


def attend_kernel(qs_far, kv_far, out, qs, kv, vs, tri, qx_a, qx_b, kx_a, kx_b, s_a, s_b, sems):
    _, _, z, y, core, _, _ = spot()
    load_kv = pltpu.make_async_copy(kv_far, kv, sems.at[0])
    load_q = pltpu.make_async_copy(qs_far, qs, sems.at[1])
    load_kv.start()
    load_q.start()
    row, col = iota((BLK, BLK), 0), iota((BLK, BLK), 1)
    tri[...] = jnp.where(col > row, HIDE, 0.0)
    same = jnp.where(row == col, 1.0, 0.0).astype(BF16)
    for h in range(4):
        qx_a[h * BLK : (h + 1) * BLK, HEAD:] = same
        qx_b[h * BLK : (h + 1) * BLK, HEAD:] = same
    vs[:, HEAD:] = jnp.where(iota((KEYS, HEAD), 1) == 0, 1.0, 0.0).astype(BF16)
    load_kv.wait()
    for n in range(SIDE):
        at = slice(n * BLK, (n + 1) * BLK)
        flipped = jnp.transpose(kv[n, :BLK, :].astype(F32)).astype(BF16)
        kx_a[:HEAD, at] = flipped
        kx_b[:HEAD, at] = flipped
        vs[at, :HEAD] = kv[n, BLK : 2 * BLK, :]
    load_q.wait()

    def score(n, qx, kx, s):
        even = core == 0
        full = jnp.where(
            even,
            z + jnp.where(y < n, 1, 0),
            jnp.where(z < n, SIDE, jnp.where(z == n, y, 0)),
        )
        edge = jnp.where(jnp.where(even, y, z) == n, full, SIDE)
        for m in range(SIDE):
            hidden = jnp.where(m == edge, tri[...], HIDE)
            kx[HEAD:, m * BLK : (m + 1) * BLK] = jnp.where(m < full, 0.0, hidden).astype(BF16)
        qx[:, :HEAD] = qs[n, :QROWS, :]
        s[...] = jnp.dot(qx[...], kx[...], preferred_element_type=F32)

    def mix(n, s):
        lane = iota((BLK, 128), 1)
        stats = jnp.zeros((BLK, 128), F32)
        for part in range(2):
            rows = slice(part * 2 * BLK, (part + 1) * 2 * BLK)
            scores = s[rows, :]
            top = EXP2_SCALE * jnp.max(scores, axis=1, keepdims=True)
            top = jnp.maximum(top, LOWEST).astype(BF16).astype(F32)
            weights = jnp.exp2(scores * EXP2_SCALE - top).astype(BF16)
            mixed = jnp.dot(weights, vs[...], preferred_element_type=F32)
            out[n, rows, :] = mixed[:, :HEAD].astype(BF16)
            total = mixed[:, HEAD : HEAD + 1]
            high = total.astype(BF16).astype(F32)
            for h in range(2):
                one = slice(h * BLK, (h + 1) * BLK)
                at = part * 2 + h
                stats = jnp.where(lane == at, top[one], stats)
                stats = jnp.where(lane == 4 + at, high[one], stats)
                stats = jnp.where(lane == 8 + at, (total - high)[one], stats)
        out[n, QROWS:Q_MSG, :] = jnp.transpose(stats)[:META].astype(BF16)

    score(0, qx_a, kx_a, s_a)

    def two(i, _):
        score(2 * i + 1, qx_b, kx_b, s_b)
        mix(2 * i, s_a)
        score(jnp.minimum(2 * i + 2, SIDE - 1), qx_a, kx_a, s_a)
        mix(2 * i + 1, s_b)

    lax.fori_loop(0, SIDE // 2, two, None)


def decode_kernel(q, xr, k_own, v_own, k_dec, v_dec, _, out, ks, vs, cs, ds, sem):
    seq, _, _, _, core, _, _ = spot()
    for n in range(NG):
        ks[n * HALF : (n + 1) * HALF, :] = xr[n, :HALF, :]
        vs[n * HALF : (n + 1) * HALF, :] = xr[n, HALF : 2 * HALF, :]
    for dst, own, dec in ((ks, k_own, k_dec), (vs, v_own, v_dec)):
        dst[OLD_TOK : OLD_TOK + TOK, :] = own[...]
        dst[OLD_TOK + TOK :, :] = dec[...]

    def hot(flag):
        return jnp.where(flag, 1.0, 0.0).astype(BF16)

    def item(shape):
        i = iota(shape, 0)
        swapped = ((i >> 1) & 7) * 16 + (i >> 4) * 2 + (i & 1)
        return jnp.where(core == 0, swapped, i)

    which = item((ITEMS, 128))
    lane = iota((ITEMS, 128), 1)
    row = (which >> 2).astype(F32)
    count = jnp.where((which == seq) & (lane >= TOK) & (lane - TOK <= (seq & 3)), 1.0, 0.0)
    token = iota((128, 128), 0)
    page, at = (token >> 4).astype(F32), (token & 15).astype(F32)
    place_f = seq.astype(F32)
    old_token = iota((OLD_TOK, 128), 0)
    old_at = (old_token & 15).astype(F32)
    old_page = (old_token >> 4) - iota((OLD_TOK, 128), 1)
    old_count = 0.0
    for n in range(NG):
        meta = xr[n, 2 * HALF :, :HEAD].astype(F32)
        for part in (0, 4):
            high, low, owner, length = (meta[part + m : part + m + 1, :] for m in range(4))
            inside = (high == place_f) & (low == page) & (at < length) & (token < TOK)
            count = count + lax.dot_general(
                hot(row == owner), hot(inside), NT, preferred_element_type=F32
            )
        owner, length = meta[8:9, :], meta[9:10, :]
        inside = (old_page == n * OLD) & (old_at < length)
        old_count = old_count + lax.dot_general(
            hot(row == owner), hot(inside), NT, preferred_element_type=F32
        )
    cs[:, :OLD_TOK] = old_count
    cs[:, OLD_TOK:] = count

    order = hot(which == lane)
    stats = jnp.zeros((ITEMS, 128), F32)
    for h in range(HEADS):
        kv = slice(h // 4 * HEAD, (h // 4 + 1) * HEAD)
        query = jnp.dot(order, q[:, h * HEAD : (h + 1) * HEAD], preferred_element_type=F32).astype(BF16)
        scores = EXP2_SCALE * lax.dot_general(query, ks[:, kv], NT, preferred_element_type=F32)
        terms = cs[...]
        scores = jnp.where(terms > 0.5, scores, NEG)
        top = jnp.max(scores, axis=1, keepdims=True).astype(BF16).astype(F32)
        weights = (jnp.exp2(scores - top) * terms).astype(BF16)
        total = jnp.sum(weights.astype(F32), axis=1, keepdims=True)
        mixed = jnp.dot(weights, vs[:, kv], preferred_element_type=F32)
        ds[:, h * PER : (h + 1) * PER, :] = mixed.astype(BF16).reshape(SIDE, PER, HEAD)
        high = total.astype(BF16).astype(F32)
        stats = jnp.where(lane == h, top, stats)
        stats = jnp.where(lane == HEADS + h, high, stats)
        stats = jnp.where(lane == 2 * HEADS + h, total - high, stats)
    ds[:, HEADS * PER :, :] = stats.astype(BF16).reshape(SIDE, PER, 128)
    copy = pltpu.make_async_copy(ds, out.at[:, pl.ds(Q_MSG, DEC_MSG), :], sem)
    copy.start()
    copy.wait()


def combine(values, stats, split):
    mixes, tops, totals = [], [], []
    for h in range(HEADS):
        top_of = [s[:, h : h + 1] for s in stats]
        top = functools.reduce(jnp.maximum, top_of)
        total, mixed = 0.0, 0.0
        for value, s, t in zip(values, stats, top_of):
            factor = jnp.exp2(t - top)
            each = s[:, HEADS + h : HEADS + h + 1]
            if split:
                each = each + s[:, 2 * HEADS + h : 2 * HEADS + h + 1]
            total = total + each * factor
            mixed = mixed + value(h) * factor
        mixes.append(mixed)
        tops.append(top)
        totals.append(total)
    return mixes, tops, totals


def stat_tile(tops, totals, split=False):
    lane = iota((tops[0].shape[0], 128), 1)
    tile = jnp.zeros(lane.shape, F32)
    for h in range(HEADS):
        tile = jnp.where(lane == h, tops[h], tile)
        if split:
            high = totals[h].astype(BF16).astype(F32)
            tile = jnp.where(lane == HEADS + h, high, tile)
            tile = jnp.where(lane == 2 * HEADS + h, totals[h] - high, tile)
        else:
            tile = jnp.where(lane == HEADS + h, totals[h], tile)
    return tile


def merge_kernel(got, attn, dec_send):
    stats = [got[n, QROWS:Q_MSG, :].astype(F32) for n in range(SIDE)]
    tops = [s[0:4] for s in stats]
    top = functools.reduce(jnp.maximum, tops)
    factors = [jnp.exp2(t - top) for t in tops]
    total = sum(f * (s[4:8] + s[8:12]) for f, s in zip(factors, stats))
    shares = jnp.concatenate([f / total for f in factors] + [jnp.zeros((96, 128), F32)], 0)
    shares = jnp.transpose(shares)
    for h in range(4):
        rows = slice(h * BLK, (h + 1) * BLK)
        out = 0.0
        for n in range(SIDE):
            out = out + got[n, rows, :].astype(F32) * shares[:, n * 4 + h : n * 4 + h + 1]
        attn[rows, :] = out.astype(BF16)

    def values(n):
        return lambda h: got[n, Q_MSG + h * PER : Q_MSG + (h + 1) * PER, :].astype(F32)

    mixes, tops, totals = combine(
        [values(n) for n in range(SIDE)],
        [got[n, O_MSG - PER :, :].astype(F32) for n in range(SIDE)],
        True,
    )
    for m, piece in enumerate(mixes + [stat_tile(tops, totals)]):
        for n in range(SIDE):
            dec_send[n, 2 * m : 2 * m + 2, :] = piece[2 * n : 2 * n + 2, :]


def pair_kernel(got, attn, attn_keep, dec_keep, send):
    core = spot()[4]
    even = core == 0

    def values(n):
        return lambda h: got[n, 2 * h : 2 * h + 2, :]

    mixes, tops, totals = combine(
        [values(n) for n in range(SIDE)], [got[n, 16:18, :] for n in range(SIDE)], False
    )
    keep_stats = stat_tile(tops, totals)
    send_stats = stat_tile(tops, totals, True)
    dec_keep[8:, :] = jnp.broadcast_to(jnp.where(even, keep_stats[0:1], keep_stats[1:2]), (8, 128))
    sent = []
    for h in range(HEADS):
        dec_keep[h : h + 1, :] = jnp.where(even, mixes[h][0:1], mixes[h][1:2])
        sent.append(jnp.where(even, mixes[h][1:2], mixes[h][0:1]))
    sent.append(jnp.where(even, send_stats[1:2], send_stats[0:1]))
    sent.append(jnp.zeros((7, 128), F32))
    send[4 * TOK :, :] = jnp.concatenate(sent, 0).astype(BF16)
    for h in range(4):
        rows = slice(h * TOK, (h + 1) * TOK)
        attn_keep[rows, :] = attn[pl.ds(aligned(h * BLK + core * TOK, TOK), TOK), :]
        send[rows, :] = attn[pl.ds(aligned(h * BLK + (1 - core) * TOK, TOK), TOK), :]


def final_kernel(attn_keep, dec_keep, got, attn_out, dec_out):
    core = spot()[4]
    for h in range(4):
        rows = slice(h * TOK, (h + 1) * TOK)
        for src, head in ((attn_keep, core), (got, 1 - core)):
            attn_out[:, pl.ds(aligned((head * 4 + h) * HEAD, HEAD), HEAD)] = src[rows, :]
    theirs = got[4 * TOK :, :].astype(F32)
    other = theirs[8:9, :]
    for h in range(HEADS):
        top_a, top_b = dec_keep[8:9, h : h + 1], other[:, h : h + 1]
        total_a = dec_keep[8:9, HEADS + h : HEADS + h + 1]
        total_b = other[:, HEADS + h : HEADS + h + 1] + other[:, 2 * HEADS + h : 2 * HEADS + h + 1]
        top = jnp.maximum(top_a, top_b)
        scale_a, scale_b = jnp.exp2(top_a - top), jnp.exp2(top_b - top)
        mixed = dec_keep[h : h + 1, :] * scale_a + theirs[h : h + 1, :] * scale_b
        dec_out[h : h + 1, :] = (mixed / (total_a * scale_a + total_b * scale_b)).astype(BF16)


def exchange(x, groups):
    return lax.all_to_all(x, "seq", 0, 0, axis_index_groups=groups, tiled=True)


def to_other_core(x):
    return lax.ppermute(x, "seq", [(n, n ^ 1) for n in range(2 * SIDE * SIDE)])


def body(q_pre, k_pre, v_pre, old_k, old_v, src_page, page_row, page_len, q_dec, dec_k, dec_v):
    seq, grp = lax.axis_index("seq"), lax.axis_index("grp")
    far = pl.BlockSpec(memory_space=pltpu.HBM)
    anywhere = pl.BlockSpec(memory_space=pl.ANY)
    counts = page_row.shape[1]
    keep, send = call(
        split_kernel,
        [((PAIR_MSG, 128), BF16)] * 2,
        (q_pre, k_pre, v_pre, src_page, page_row, page_len),
        scratch=(
            pltpu.SMEM(src_page.shape, jnp.int32),
            pltpu.SMEM((1, counts), jnp.int32),
            pltpu.SMEM((1, counts), jnp.int32),
            pltpu.SemaphoreType.DMA((15,)),
        ),
        specs={n: far for n in range(6)},
    )
    got = to_other_core(send)
    kv_send, q_blk = call(
        keys_kernel,
        [((SIDE, KV_MSG, 128), BF16), ((QROWS, 128), BF16)],
        (keep, got),
    )
    kv = exchange(kv_send, KEY_GROUPS)
    (q_send,) = call(queries_kernel, [((SIDE, Q_MSG, 128), BF16)], (q_blk, kv))
    qs = exchange(q_send, QUERY_GROUPS)
    (x_send,) = call(
        pages_kernel,
        [((NG, X_MSG, TWO), BF16)],
        (qs, old_k.reshape(HALF, -1), old_v.reshape(HALF, -1), page_row, page_len),
        scratch=(pltpu.VMEM((SIDE, META, 128), BF16), pltpu.SemaphoreType.DMA),
        specs={0: far, 3: SMEM, 4: SMEM},
    )
    xr = lax.all_to_all(x_send, "grp", 0, 0, tiled=True)
    work = QROWS * SIDE * KEYS
    (o_send,) = call(
        attend_kernel,
        [((SIDE, O_MSG, 128), BF16)],
        (qs, kv),
        scratch=(
            pltpu.VMEM((SIDE, Q_MSG, 128), BF16),
            pltpu.VMEM((SIDE, KV_MSG, 128), BF16),
            pltpu.VMEM((KEYS, TWO), BF16),
            pltpu.VMEM((BLK, BLK), F32),
            pltpu.VMEM((QROWS, TWO), BF16),
            pltpu.VMEM((QROWS, TWO), BF16),
            pltpu.VMEM((TWO, KEYS), BF16),
            pltpu.VMEM((TWO, KEYS), BF16),
            pltpu.VMEM((QROWS, KEYS), F32),
            pltpu.VMEM((QROWS, KEYS), F32),
            pltpu.SemaphoreType.DMA((2,)),
        ),
        specs={0: far, 1: far},
        cost=pl.CostEstimate(flops=work * 512, bytes_accessed=4 * 1024 * 1024, transcendentals=work),
    )

    q_mine = lax.dynamic_slice_in_dim(q_dec, grp * HEADS * HEAD, HEADS * HEAD, 2)
    q_mine = q_mine.reshape(ITEMS, HEADS * HEAD)

    def own_tokens(x):
        part = lax.dynamic_slice(x, (seq // STEPS, 0, grp * TWO), (1, STEPS, TWO))[0]
        return jnp.pad(part, ((0, TOK - STEPS), (0, 0)))

    (o_send,) = call(
        decode_kernel,
        [((SIDE, O_MSG, 128), BF16)],
        (q_mine, xr, k_pre, v_pre, own_tokens(dec_k), own_tokens(dec_v), o_send),
        scratch=(
            pltpu.VMEM((DEC_TOK, TWO), BF16),
            pltpu.VMEM((DEC_TOK, TWO), BF16),
            pltpu.VMEM((ITEMS, DEC_TOK), F32),
            pltpu.VMEM((SIDE, DEC_MSG, 128), BF16),
            pltpu.SemaphoreType.DMA,
        ),
        specs={6: anywhere},
        out_specs=[anywhere],
        alias={6: 0},
    )
    attn, dec_send = call(
        merge_kernel,
        [((QROWS, 128), BF16), ((SIDE, 18, 128), F32)],
        (exchange(o_send, QUERY_GROUPS),),
    )
    attn_keep, dec_keep, last = call(
        pair_kernel,
        [((4 * TOK, 128), BF16), ((16, 128), F32), ((LAST_MSG, 128), BF16)],
        (exchange(dec_send, KEY_GROUPS), attn),
    )
    attn_out, dec_out = call(
        final_kernel,
        [((TOK, HEADS * HEAD), BF16), ((HEADS, HEAD), BF16)],
        (attn_keep, dec_keep, to_other_core(last)),
    )
    return attn_out, dec_out


def solution(mesh):
    return jax.shard_map(
        body,
        mesh=mesh,
        in_specs=(
            P("seq", "grp"),
            P("seq", "grp"),
            P("seq", "grp"),
            P("seq", "grp", None, None),
            P("seq", "grp", None, None),
            P("seq", None),
            P("seq", "grp"),
            P("seq", "grp"),
            P(),
            P(),
            P(),
        ),
        out_specs=(P("seq", "grp"), P(("seq", "grp"), None)),
        check_vma=False,
    )
```

time: 625 us -> 128 us (0.20)
  waiting for transfers between devices: 326 us -> 1.82 us
  blocking collectives: 222 us -> 75.6 us
  local copies, waits for them, and re-layouts: 42.1 us -> 11 us
  Pallas kernels: 0 us -> 18 us
  between operations: 14.8 us -> 0.84 us
  starting transfers between devices: 8.01 us -> 20.3 us
  other arithmetic: 7.86 us -> 0 us
    unnamed x4 -> x0, waiting for transfers between devices: 174 us -> none
    all_gather x2 -> x0, waiting for transfers between devices: 152 us -> none  [the longest x1 82.1 us: body(): lax.all_gather(k_pre, 'seq', axis=0, tiled=True)]
    pmax x1 -> x0, blocking collectives: 127 us -> none  [body(): top_all = lax.pmax(row_top, ('seq', 'grp'))]
    unnamed x1 -> x0, blocking collectives: 95.1 us -> none
    all_to_all x0 -> x4, blocking collectives: none -> 75.6 us  [exchange(): return lax.all_to_all(x, 'seq', 0, 0, axis_index_groups=groups, tiled=True)]
    pallas_call x0 -> x9, Pallas kernels: none -> 18 us  [call(): pl.pallas_call(kernel, out_shape=[jax.ShapeDtypeStruct(s, t) for s, t in...]
    reshape x8 -> x1, local copies, waits for them, and re-layouts: 17.6 us -> 0.77 us  [body(): q_mine = q_mine.reshape(ITEMS, HEADS * HEAD)]
    ppermute x0 -> x2, starting transfers between devices: none -> 16.1 us  [to_other_core(): return lax.ppermute(x, 'seq', [(n, n ^ 1) for n in range(2 * SIDE * SIDE)])]
  transfers between devices with their start and end apart: 5 -> 3, of which waited for: 3 -> 2; matrix products, arithmetic and copies ran while one was open for 7% -> 2% of each run, Pallas kernels for 0% -> 6%
where the time goes in v1:
time: 128 us
  blocking collectives  75.6 us (59%)
  starting transfers between devices  20.3 us (16%)
  Pallas kernels  18 us (14%)
  local copies, waits for them, and re-layouts  11 us (9%)
  waiting for transfers between devices  1.82 us (1%)
    all_to_all x4, blocking collectives, exchange(): return lax.all_to_all(x, 'seq', 0, 0, axis_index_groups=groups, tiled=True)  75.6 us
    pallas_call x9, Pallas kernels, call(): pl.pallas_call(kernel, out_shape=[jax.ShapeDtypeStruct(s, t) for s, t in...  18 us
    ppermute x2, starting transfers between devices, to_other_core(): return lax.ppermute(x, 'seq', [(n, n ^ 1) for n in range(2 * SIDE * SIDE)])  16.1 us
    unnamed x34, local copies, waits for them, and re-layouts  8.77 us
    all_to_all x1, starting transfers between devices, body(): xr = lax.all_to_all(x_send, 'grp', 0, 0, tiled=True)  4.19 us
  transfers between devices with their start and end apart: 3, of which 2 were waited for; matrix products, arithmetic and copies ran while one was open for 2% of the time, Pallas kernels for 6%

profile of v1, /device:TPU:1, one launch (start us, length us, event | category | flops | bytes accessed | tf_op | source)
XLA Modules:
  0.0 127.5 jit_solution(10543398550700989325)
XLA Ops:
  0.7 0.8 copy-done.7
  1.5 0.8 copy-done.9
  2.3 0.9 copy-done.11
  5.1 0.7 split.1
  5.9 8.8 %collective-permute-start = (bf16[400,128]{1,0:T(8,128)(2,1)S(1)}, bf16[400,128]{1,0:T(8,128)(2,1)S(1)}, u32[]{:S(2)}, u32[]{:S(2)}) collective-permute-start(bf16[400,128]{1,0:T(8,128)(2,1)S(1)} %get-tuple-element.12), channel_id=1, source_target_pairs={{0,4},{4,0},{8,12},{12,8},{16,20},{20,16},{24,28},{28,24},{32,36},... | collective-permute-start | bytes 307208 | tf_op jit(solution)/shard_map/ppermute | solution.py:408
  14.7 0.9 collective-permute-done.got
  15.7 14.9 %all_to_all.25.kv.kv_far = bf16[8,272,128]{2,1,0:T(8,128)(2,1)S(1)} all-to-all(bf16[8,272,128]{2,1,0:T(8,128)(2,1)S(1)} %get-tuple-element.14), channel_id=1, replica_groups={{0,64,128,192,256,320,384,448},{8,72,136,200,264,328,392,456},{16,80,14..., dimensions={0} | all-to-all | bytes 1114112 | tf_op jit(solution)/shard_map/all_to_all | solution.py:404
  30.7 26.9 %all_to_all.26.qs_far = bf16[8,528,128]{2,1,0:T(8,128)(2,1)S(1)} all-to-all(bf16[8,528,128]{2,1,0:T(8,128)(2,1)S(1)} %queries.1), channel_id=1, replica_groups={{0,8,16,24,32,40,48,56},{64,72,80,88,96,104,112,120},{128,136,144,152,1..., dimensions={0} | all-to-all | bytes 2162688 | tf_op jit(solution)/shard_map/all_to_all | solution.py:404
  57.7 1.5 %pages.1 = bf16[4,336,256]{2,1,0:T(8,128)(2,1)} custom-call(bf16[8,528,128]{2,1,0:T(8,128)(2,1)S(1)} %all_to_all.26.qs_far, bf16[160,1024]{1,0:T(8,128)(2,1)S(1)} %bitcast.6, bf16[160,1024]{1,0:T(8,128)(2,1)S(1)} %bitcast.7, s32[1,12]{1,0:T(1,128)S(1)} %copy-done.13, s32[1,12]{1,0:T(1,128)S(1)} %copy-done.15), custom_call_target="tpu_custom_call" | custom-call | tf_op jit(solution)/shard_map/pages/pallas_call | solution.py:77
  59.2 4.2 %all-to-all-start.2 = ((bf16[4,336,256]{2,1,0:T(8,128)(2,1)}), bf16[4,336,256]{2,1,0:T(8,128)(2,1)}, u32[]{:S(2)}, u32[]{:S(2)}) async-start(bf16[4,336,256]{2,1,0:T(8,128)(2,1)} %pages.1), calls=%async_computation.2 | async-start | bytes 1376256 | tf_op jit(solution)/shard_map/all_to_all | solution.py:444
  64.9 0.8 reshape.13.q
  65.7 1.1 copy-done.2
  66.7 8.2 %attend.1._ = bf16[8,672,128]{2,1,0:T(8,128)(2,1)S(1)} custom-call(bf16[8,528,128]{2,1,0:T(8,128)(2,1)S(1)} %all_to_all.26.qs_far, bf16[8,272,128]{2,1,0:T(8,128)(2,1)S(1)} %copy-done.2), custom_call_target="tpu_custom_call" | custom-call | flops 2147483648 | bytes 4194304 | tf_op jit(solution)/shard_map/attend/pallas_call | solution.py:77
  74.9 0.9 copy-done.3
  75.9 0.8 copy-done.6
  76.6 0.8 copy-done.8
  77.4 0.8 copy-done.10
  78.1 5.2 %decode.1 = bf16[8,672,128]{2,1,0:T(8,128)(2,1)S(1)} custom-call(bf16[128,1024]{1,0:T(8,128)(2,1)S(1)} %copy-done.3, bf16[4,336,256]{2,1,0:T(8,128)(2,1)} %all-to-all-done.2.xr, bf16[64,256]{1,0:T(8,128)(2,1)S(1)} %copy-done.8, bf16[64,256]{1,0:T(8,128)(2,1)S(1)} %copy-done.10, bf16[64,256]{1,0:T(8,128)(2,1)S(1)} %pad.7.k_dec, ...), custom_call_target="tpu_custom_call", output_to_operand_aliasing={{}: (6, {})} | custom-call | tf_op jit(solution)/shard_map/decode/pallas_call | solution.py:77
  83.4 23.8 %all_to_all.27.got = bf16[8,672,128]{2,1,0:T(8,128)(2,1)S(1)} all-to-all(bf16[8,672,128]{2,1,0:T(8,128)(2,1)S(1)} %decode.1), channel_id=1, replica_groups={{0,8,16,24,32,40,48,56},{64,72,80,88,96,104,112,120},{128,136,144,152,1..., dimensions={0} | all-to-all | bytes 2752512 | tf_op jit(solution)/shard_map/all_to_all | solution.py:404
  107.2 1.1 merge.1
  108.3 10.0 %all_to_all.28.got = f32[8,18,128]{2,1,0:T(8,128)S(1)} all-to-all(f32[8,18,128]{2,1,0:T(8,128)S(1)} %get-tuple-element.15), channel_id=1, replica_groups={{0,64,128,192,256,320,384,448},{8,72,136,200,264,328,392,456},{16,80,14..., dimensions={0} | all-to-all | bytes 147456 | tf_op jit(solution)/shard_map/all_to_all | solution.py:404
  118.5 7.3 %collective-permute-start.1 = (bf16[272,128]{1,0:T(8,128)(2,1)S(1)}, bf16[272,128]{1,0:T(8,128)(2,1)S(1)}, u32[]{:S(2)}, u32[]{:S(2)}) collective-permute-start(bf16[272,128]{1,0:T(8,128)(2,1)S(1)} %get-tuple-element.19), channel_id=1, source_target_pairs={{0,4},{4,0},{8,12},{12,8},{16,20},{20,16},{24,28},{28,24},{32,36},... | collective-permute-start | bytes 208904 | tf_op jit(solution)/shard_map/ppermute | solution.py:408
  125.8 0.9 collective-permute-done.1.got
  126.7 0.8 final.1
  (34 shorter events, 3.9 us)
Async XLA Ops:
  0.6 64.2 %copy-start = (bf16[32,4,4096]{2,1,0:T(4,128)(2,1)S(1)}, bf16[32,4,4096]{2,1,0:T(4,128)(2,1)}, u32[]{:S(2)}) copy-start(bf16[32,4,4096]{2,1,0:T(4,128)(2,1)} %param.19) | copy-start | bytes 3145732
  0.6 0.8 copy-start.7
  1.5 0.8 copy-start.9
  2.3 0.9 copy-start.11
  3.2 0.7 copy-start.12
  3.8 0.7 copy-start.14
  4.5 0.7 copy-start.16
  5.9 9.7 %collective-permute-start = (bf16[400,128]{1,0:T(8,128)(2,1)S(1)}, bf16[400,128]{1,0:T(8,128)(2,1)S(1)}, u32[]{:S(2)}, u32[]{:S(2)}) collective-permute-start(bf16[400,128]{1,0:T(8,128)(2,1)S(1)} %get-tuple-element.12), channel_id=1, source_target_pairs={{0,4},{4,0},{8,12},{12,8},{16,20},{20,16},{24,28},{28,24},{32,36},... | collective-permute-start | bytes 307208 | tf_op jit(solution)/shard_map/ppermute | solution.py:408
  30.5 27.1 %copy-start.1 = (bf16[8,272,128]{2,1,0:T(8,128)(2,1)}, bf16[8,272,128]{2,1,0:T(8,128)(2,1)S(1)}, u32[]{:S(2)}) copy-start(bf16[8,272,128]{2,1,0:T(8,128)(2,1)S(1)} %all_to_all.25.kv.kv_far) | copy-start | bytes 1671172
  30.7 27.0 %copy-start.4 = (bf16[1,10,16,1024]{3,2,1,0:T(8,128)(2,1)S(1)}, bf16[1,10,16,1024]{3,2,1,0:T(8,128)(2,1)}, u32[]{:S(2)}) copy-start(bf16[1,10,16,1024]{3,2,1,0:T(8,128)(2,1)} %param.14) | copy-start | bytes 983044
  30.7 27.0 %copy-start.5 = (bf16[1,10,16,1024]{3,2,1,0:T(8,128)(2,1)S(1)}, bf16[1,10,16,1024]{3,2,1,0:T(8,128)(2,1)}, u32[]{:S(2)}) copy-start(bf16[1,10,16,1024]{3,2,1,0:T(8,128)(2,1)} %param.15) | copy-start | bytes 983044
  30.7 27.0 %copy-start.13 = (s32[1,12]{1,0:T(1,128)S(1)}, s32[1,12]{1,0:T(1,128)}, u32[]{:S(2)}) copy-start(s32[1,12]{1,0:T(1,128)} %page_row.3) | copy-start | bytes 148
  30.7 27.0 %copy-start.15 = (s32[1,12]{1,0:T(1,128)S(1)}, s32[1,12]{1,0:T(1,128)}, u32[]{:S(2)}) copy-start(s32[1,12]{1,0:T(1,128)} %page_len.3) | copy-start | bytes 148
  59.2 15.7 %all-to-all-start.2 = ((bf16[4,336,256]{2,1,0:T(8,128)(2,1)}), bf16[4,336,256]{2,1,0:T(8,128)(2,1)}, u32[]{:S(2)}, u32[]{:S(2)}) async-start(bf16[4,336,256]{2,1,0:T(8,128)(2,1)} %pages.1), calls=%async_computation.2 | async-start | bytes 1376256 | tf_op jit(solution)/shard_map/all_to_all | solution.py:444
  65.7 1.1 copy-start.2
  74.9 1.0 copy-start.3
  75.9 0.8 copy-start.6
  76.6 0.8 copy-start.8
  77.4 0.8 copy-start.10
  118.5 8.2 %collective-permute-start.1 = (bf16[272,128]{1,0:T(8,128)(2,1)S(1)}, bf16[272,128]{1,0:T(8,128)(2,1)S(1)}, u32[]{:S(2)}, u32[]{:S(2)}) collective-permute-start(bf16[272,128]{1,0:T(8,128)(2,1)S(1)} %get-tuple-element.19), channel_id=1, source_target_pairs={{0,4},{4,0},{8,12},{12,8},{16,20},{20,16},{24,28},{28,24},{32,36},... | collective-permute-start | bytes 208904 | tf_op jit(solution)/shard_map/ppermute | solution.py:408

commit v2 on v1

v2 whole, which is shorter than its diff:
```python
import functools
import math

import jax
import jax.numpy as jnp
from jax import lax
from jax.experimental import pallas as pl
from jax.experimental.pallas import tpu as pltpu
from jax.sharding import PartitionSpec as P

HEAD = 128
PAGE = 16
OLD = 10
NEWP = 2
ROWS = 32
STEPS = 4
ITEMS = ROWS * STEPS
SIDE = 8
NG = 4
TOK = 64
BLK = 2 * TOK
KEYS = SIDE * BLK
QROWS = 4 * BLK
HEADS = 8
TWO = 2 * HEAD
EXP2_SCALE = math.log2(math.e) / math.sqrt(HEAD)
NEG = -(2.0**100)
HIDE = -(2.0**80)
LOWEST = -(2.0**60)
META = 16
PAIR_MSG = 6 * TOK + META
HALF = OLD * PAGE
X_MSG = 2 * HALF + META
OLD_TOK = NG * HALF
DEC_TOK = OLD_TOK + 128
PER = ITEMS // SIDE
DEC_MSG = HEADS * PER + PER
KV_DEC = 2 * BLK + META
KV_MSG = KV_DEC + DEC_MSG
FRONT = META + KEYS
CHUNK = FRONT + KEYS
PAGES = KEYS // PAGE
LAST_MSG = 4 * TOK + 16
FRESH = 16
NT = (((1,), (1,)), ((), ()))
F32 = jnp.float32
BF16 = jnp.bfloat16


def seq_of(z, y, core):
    return (z * SIDE + y) * 2 + core


ALONG_Z = [[[seq_of(i, j, c) for i in range(SIDE)] for j in range(SIDE)] for c in range(2)]
ALONG_Y = [[[seq_of(j, i, c) for i in range(SIDE)] for j in range(SIDE)] for c in range(2)]
KEY_GROUPS = ALONG_Z[0] + ALONG_Y[1]
QUERY_GROUPS = ALONG_Y[0] + ALONG_Z[1]


def iota(shape, dim):
    return lax.broadcasted_iota(jnp.int32, shape, dim)


def spot():
    seq, grp = lax.axis_index("seq"), lax.axis_index("grp")
    core = seq & 1
    y = (seq >> 1) & (SIDE - 1)
    z = seq >> 4
    even = core == 0
    return seq, grp, z, y, core, jnp.where(even, z, y), jnp.where(even, y, z)


def aligned(x, by):
    return pl.multiple_of(x, by)


def call(kernel, outs, args, scratch=(), limit=32, specs=None, out_specs=None, cost=None, alias=None):
    whole = pl.BlockSpec(memory_space=pltpu.VMEM)
    name = kernel.__name__.removesuffix("_kernel")
    return pl.pallas_call(
        kernel,
        out_shape=[jax.ShapeDtypeStruct(s, t) for s, t in outs],
        in_specs=[specs.get(n, whole) if specs else whole for n in range(len(args))],
        out_specs=out_specs or [whole] * len(outs),
        scratch_shapes=list(scratch),
        compiler_params=pltpu.CompilerParams(vmem_limit_bytes=limit * 1024 * 1024),
        cost_estimate=cost,
        input_output_aliases=alias or {},
        name=name,
    )(*args)


SMEM = pl.BlockSpec(memory_space=pltpu.SMEM)


def pages_kernel(old_k, old_v, src_page, page_row, page_len, *rest):
    outs, (src_s, row_s, len_s, sems) = rest[:NG], rest[NG:]
    grp = spot()[1]
    pairs = [(src_page, src_s), (page_row, row_s), (page_len, len_s)]
    for d in range(NG):
        cols = pl.ds(aligned(((grp + d) % NG) * TWO, TWO), TWO)
        pairs.append((old_k.at[:, cols], outs[d].at[pl.ds(0, HALF), :]))
        pairs.append((old_v.at[:, cols], outs[d].at[pl.ds(HALF, HALF), :]))
    copies = [pltpu.make_async_copy(a, b, sems.at[n]) for n, (a, b) in enumerate(pairs)]
    for copy in copies:
        copy.start()
    for copy in copies[:3]:
        copy.wait()
    sub, lane = iota((META, TWO), 0), iota((META, TWO), 1)
    tile = jnp.zeros((META, TWO), F32)
    for n in range(NEWP):
        src = src_s[0, grp * NEWP + n]
        values = (src >> 2, src & 3, row_s[0, OLD + n], len_s[0, OLD + n])
        for m, value in enumerate(values):
            tile = jnp.where((lane == n) & (sub == m), value.astype(F32), tile)
    for n in range(OLD):
        tile = jnp.where((sub == 8) & (lane == n), row_s[0, n].astype(F32), tile)
        tile = jnp.where((sub == 9) & (lane == n), len_s[0, n].astype(F32), tile)
    for d in range(NG):
        outs[d][2 * HALF :, :] = tile.astype(BF16)
    for copy in copies[3:]:
        copy.wait()


def split_kernel(q, k, v, x0, x1, x2, x3, keep, send, sems):
    _, _, _, _, core, w, u = spot()
    pairs = []
    for dst, head in ((keep, core), (send, 1 - core)):
        one = pl.ds(aligned(head * HEAD, HEAD), HEAD)
        pairs.append((k.at[:, one], dst.at[pl.ds(0, TOK), :]))
        pairs.append((v.at[:, one], dst.at[pl.ds(TOK, TOK), :]))
        for h in range(4):
            cols = pl.ds(aligned((head * 4 + h) * HEAD, HEAD), HEAD)
            pairs.append((q.at[:, cols], dst.at[pl.ds((2 + h) * TOK, TOK), :]))
    copies = [pltpu.make_async_copy(a, b, sems.at[n]) for n, (a, b) in enumerate(pairs)]
    for copy in copies:
        copy.start()
    fresh = (iota((META, 128), 0) < 4) & (iota((META, 128), 1) < NEWP)
    for dst, at in ((keep, w), (send, u)):
        tile = jnp.zeros((META, 128), F32)
        for d, x in enumerate((x0, x1, x2, x3)):
            part = jnp.where(fresh, x[2 * HALF :, :HEAD].astype(F32), 0.0)
            tile = tile + pltpu.roll(part, at * 16 + core * 8 + d * NEWP, 1)
        dst[6 * TOK :, :] = tile.astype(BF16)
    for copy in copies:
        copy.wait()


def local_kernel(keep, got, q, x0, x1, x2, x3, k_dec, v_dec, kv_send, q_blk, ks, vs, cs, kb):
    seq, _, _, _, core, _, _ = spot()
    for src, start in ((keep, core * TOK), (got, (1 - core) * TOK)):
        kb[pl.ds(aligned(start, TOK), TOK), :] = src[:TOK, :].astype(F32)
        kv_send[0, pl.ds(aligned(BLK + start, TOK), TOK), :] = src[TOK : 2 * TOK, :]
        for h in range(4):
            q_blk[pl.ds(aligned(h * BLK + start, TOK), TOK), :] = src[
                (2 + h) * TOK : (3 + h) * TOK, :
            ]
    kv_send[0, :BLK, :] = jnp.transpose(kb[...]).astype(BF16)
    meta = keep[6 * TOK :, :].astype(F32) + got[6 * TOK :, :].astype(F32)
    kv_send[0, 2 * BLK : KV_DEC, :] = meta.astype(BF16)
    for n in range(1, SIDE):
        kv_send[n, :KV_DEC, :] = kv_send[0, :KV_DEC, :]

    parts = (x0, x1, x2, x3)
    for n, part in enumerate(parts):
        ks[n * HALF : (n + 1) * HALF, :] = part[:HALF, :]
        vs[n * HALF : (n + 1) * HALF, :] = part[HALF : 2 * HALF, :]
    ks[OLD_TOK:, :] = k_dec[...]
    vs[OLD_TOK:, :] = v_dec[...]

    def hot(flag):
        return jnp.where(flag, 1.0, 0.0).astype(BF16)

    i = iota((ITEMS, 128), 0)
    swapped = ((i >> 1) & 7) * 16 + (i >> 4) * 2 + (i & 1)
    which = jnp.where(core == 0, i, swapped)
    lane = iota((ITEMS, 128), 1)
    row = (which >> 2).astype(F32)
    token = iota((OLD_TOK, 128), 0)
    at = (token & 15).astype(F32)
    page = (token >> 4) - iota((OLD_TOK, 128), 1)
    count = 0.0
    for n, part in enumerate(parts):
        numbers = part[2 * HALF :, :HEAD].astype(F32)
        owner, length = numbers[8:9, :], numbers[9:10, :]
        inside = (page == n * OLD) & (at < length)
        count = count + lax.dot_general(
            hot(row == owner), hot(inside), NT, preferred_element_type=F32
        )
    cs[:, :OLD_TOK] = count
    cs[:, OLD_TOK:] = jnp.where((which == seq) & (lane <= (seq & 3)), 1.0, 0.0)

    order = hot(which == lane)
    stats = jnp.zeros((ITEMS, 128), F32)
    for h in range(HEADS):
        kv = slice(h // 4 * HEAD, (h // 4 + 1) * HEAD)
        query = jnp.dot(order, q[:, h * HEAD : (h + 1) * HEAD], preferred_element_type=F32).astype(BF16)
        scores = EXP2_SCALE * lax.dot_general(query, ks[:, kv], NT, preferred_element_type=F32)
        terms = cs[...]
        scores = jnp.where(terms > 0.5, scores, NEG)
        top = jnp.max(scores, axis=1, keepdims=True).astype(BF16).astype(F32)
        weights = (jnp.exp2(scores - top) * terms).astype(BF16)
        total = jnp.sum(weights.astype(F32), axis=1, keepdims=True)
        mixed = jnp.dot(weights, vs[:, kv], preferred_element_type=F32)
        rows = slice(KV_DEC + h * PER, KV_DEC + (h + 1) * PER)
        kv_send[:, rows, :] = mixed.astype(BF16).reshape(SIDE, PER, HEAD)
        high = total.astype(BF16).astype(F32)
        stats = jnp.where(lane == h, top, stats)
        stats = jnp.where(lane == HEADS + h, high, stats)
        stats = jnp.where(lane == 2 * HEADS + h, total - high, stats)
    kv_send[:, KV_DEC + HEADS * PER :, :] = stats.astype(BF16).reshape(SIDE, PER, 128)


def attend_kernel(q, q_dec, *refs):
    bufs = refs[:9]
    attn, fresh_o, fresh_s = refs[9:12]
    vs_a, vs_b, tri, qx, kx_a, kx_b, s_a, s_b, acc, tops = refs[12:]
    seq, _, z, y, core, _, u = spot()
    even = core == 0
    keys_at = [bufs[d] if d < 5 else bufs[d + 1] for d in range(SIDE)]
    row, col = iota((BLK, BLK), 0), iota((BLK, BLK), 1)
    tri[...] = jnp.where(col > row, HIDE, 0.0)
    same = jnp.where(row == col, 1.0, 0.0).astype(BF16)
    qx[:, :HEAD] = q[...]
    for h in range(4):
        qx[h * BLK : (h + 1) * BLK, HEAD:] = same
    first = jnp.where(iota((KEYS, HEAD), 1) == 0, 1.0, 0.0).astype(BF16)
    vs_a[:, HEAD:] = first
    vs_b[:, HEAD:] = first
    acc[...] = jnp.zeros_like(acc)
    tops[...] = jnp.full_like(tops, LOWEST)

    numbers = jnp.concatenate([ref[:META, :].astype(F32) for ref in keys_at], axis=1)
    source = numbers[0:1, :] * 4.0 + numbers[1:2, :]
    mine = numbers[2:3, :] == (seq >> 2).astype(F32)
    slots = source.shape[1]
    live = mine & (iota((PAGE, slots), 0).astype(F32) < numbers[3:4, :])
    live = jnp.where(live, 1.0, 0.0).astype(BF16)
    spread = iota((PAGES, KEYS), 1) >> 4 == iota((PAGES, KEYS), 0)
    spread = jnp.where(spread, 1.0, 0.0).astype(BF16)
    at = (iota((PAGE, KEYS), 1) & 15) == iota((PAGE, KEYS), 0)

    def far(d):
        return (u - d + SIDE) & (SIDE - 1)

    def score(d, kx, vs, s):
        n = far(d)
        full = jnp.where(
            even,
            z + jnp.where(n < y, 1, 0),
            jnp.where(n < z, SIDE, jnp.where(n == z, y, 0)),
        )
        edge = jnp.where(n == u, full, SIDE)
        for m in range(SIDE):
            cols = slice(m * BLK, (m + 1) * BLK)
            kx[:HEAD, cols] = keys_at[d][META + m * BLK : META + (m + 1) * BLK, :]
            hidden = jnp.where(m == edge, tri[...], HIDE)
            kx[HEAD:, cols] = jnp.where(m < full, 0.0, hidden).astype(BF16)
        vs[:, :HEAD] = bufs[5][...] if d == 4 else keys_at[d][FRONT:, :]
        s[...] = jnp.dot(qx[...], kx[...], preferred_element_type=F32)

    def mix(s, vs):
        for part in range(2):
            rows = slice(part * 2 * BLK, (part + 1) * 2 * BLK)
            scores = s[rows, :]
            before = tops[rows, :]
            top = jnp.maximum(before, EXP2_SCALE * jnp.max(scores, axis=1, keepdims=True))
            tops[rows, :] = top
            weights = jnp.exp2(scores * EXP2_SCALE - top[:, :1]).astype(BF16)
            mixed = jnp.dot(weights, vs[...], preferred_element_type=F32)
            acc[rows, :] = acc[rows, :] * jnp.exp2(before - top)[:, :1] + mixed

    def copied(d, kx, vs, state):
        before, mixed = state
        n = far(d)
        page = iota((PAGES, slots), 0)
        w = page >> 3
        chip = jnp.where(even, w * SIDE + n, n * SIDE + w)
        page = (chip * SIDE + (page & 7)).astype(F32)
        there = jnp.where(source == page, 1.0, 0.0).astype(BF16)
        count = lax.dot_general(live, there, NT, preferred_element_type=F32)
        high = count.astype(BF16)
        low = (count - high.astype(F32)).astype(BF16)
        count = jnp.dot(high, spread, preferred_element_type=F32) + jnp.dot(
            low, spread, preferred_element_type=F32
        )
        terms = jnp.sum(jnp.where(at, count, 0.0), axis=0, keepdims=True)
        scores = EXP2_SCALE * jnp.dot(q_dec[...], kx[:HEAD, :], preferred_element_type=F32)
        scores = jnp.where(terms > 0.5, scores, NEG)
        top = jnp.max(scores, axis=1, keepdims=True).astype(BF16).astype(F32)
        top = jnp.maximum(before, top)
        weights = (jnp.exp2(scores - top) * terms).astype(BF16)
        mixed = mixed * jnp.exp2(before - top)
        return top, mixed + jnp.dot(weights, vs[...], preferred_element_type=F32)

    sides = ((kx_a, vs_a, s_a), (kx_b, vs_b, s_b))
    state = (jnp.full((FRESH, 1), NEG, F32), jnp.zeros((FRESH, TWO), F32))
    score(0, *sides[0])
    for d in range(SIDE):
        kx, vs, s = sides[d % 2]
        if d + 1 < SIDE:
            score(d + 1, *sides[(d + 1) % 2])
        mix(s, vs)
        state = copied(d, kx, vs, state)
    attn[...] = (acc[:, :HEAD] / acc[:, HEAD : HEAD + 1]).astype(BF16)
    top, mixed = state
    fresh_o[...] = mixed[:, :HEAD]
    lane = iota((FRESH, 128), 1)
    fresh_s[...] = jnp.where(lane == 0, top, jnp.where(lane == 1, mixed[:, HEAD : HEAD + 1], 0.0))


def combine(values, stats, split):
    mixes, tops, totals = [], [], []
    for h in range(HEADS):
        top_of = [s[:, h : h + 1] for s in stats]
        top = functools.reduce(jnp.maximum, top_of)
        total, mixed = 0.0, 0.0
        for value, s, t in zip(values, stats, top_of):
            factor = jnp.exp2(t - top)
            each = s[:, HEADS + h : HEADS + h + 1]
            if split:
                each = each + s[:, 2 * HEADS + h : 2 * HEADS + h + 1]
            total = total + each * factor
            mixed = mixed + value(h) * factor
        mixes.append(mixed)
        tops.append(top)
        totals.append(total)
    return mixes, tops, totals


def stat_tile(tops, totals, split=False):
    lane = iota((tops[0].shape[0], 128), 1)
    tile = jnp.zeros(lane.shape, F32)
    for h in range(HEADS):
        tile = jnp.where(lane == h, tops[h], tile)
        if split:
            high = totals[h].astype(BF16).astype(F32)
            tile = jnp.where(lane == HEADS + h, high, tile)
            tile = jnp.where(lane == 2 * HEADS + h, totals[h] - high, tile)
        else:
            tile = jnp.where(lane == HEADS + h, totals[h], tile)
    return tile


def merge_kernel(got, chunk, dec_send):
    chunk[:META, :] = sum(got[n, 2 * BLK : KV_DEC, :].astype(F32) for n in range(SIDE)).astype(BF16)
    for n in range(SIDE):
        chunk[META + n * BLK : META + (n + 1) * BLK, :] = got[n, :BLK, :]
        chunk[FRONT + n * BLK : FRONT + (n + 1) * BLK, :] = got[n, BLK : 2 * BLK, :]

    def values(n):
        return lambda h: got[n, KV_DEC + h * PER : KV_DEC + (h + 1) * PER, :].astype(F32)

    mixes, tops, totals = combine(
        [values(n) for n in range(SIDE)],
        [got[n, KV_MSG - PER :, :].astype(F32) for n in range(SIDE)],
        True,
    )
    for m, piece in enumerate(mixes + [stat_tile(tops, totals)]):
        for n in range(SIDE):
            dec_send[n, 2 * m : 2 * m + 2, :] = piece[2 * n : 2 * n + 2, :]


def pair_kernel(got, attn, fresh_o, fresh_s, attn_keep, dec_keep, send):
    core = spot()[4]
    even = core == 0

    def values(n):
        return lambda h: got[n, 2 * h : 2 * h + 2, :]

    def fresh(h):
        return jnp.concatenate([fresh_o[h % 4 : h % 4 + 1, :], fresh_o[4 + h % 4 : 5 + h % 4, :]], 0)

    lane = iota((2, 128), 1)
    stats = jnp.zeros((2, 128), F32)
    for h in range(HEADS):
        both = jnp.concatenate([fresh_s[h % 4 : h % 4 + 1, :], fresh_s[4 + h % 4 : 5 + h % 4, :]], 0)
        here = core == h // 4
        stats = jnp.where(lane == h, jnp.where(here, both[:, 0:1], NEG), stats)
        stats = jnp.where(lane == HEADS + h, jnp.where(here, both[:, 1:2], 0.0), stats)
    mixes, tops, totals = combine(
        [values(n) for n in range(SIDE)] + [fresh],
        [got[n, 16:18, :] for n in range(SIDE)] + [stats],
        False,
    )
    keep_stats = stat_tile(tops, totals)
    send_stats = stat_tile(tops, totals, True)
    dec_keep[8:, :] = jnp.broadcast_to(jnp.where(even, keep_stats[0:1], keep_stats[1:2]), (8, 128))
    sent = []
    for h in range(HEADS):
        dec_keep[h : h + 1, :] = jnp.where(even, mixes[h][0:1], mixes[h][1:2])
        sent.append(jnp.where(even, mixes[h][1:2], mixes[h][0:1]))
    sent.append(jnp.where(even, send_stats[1:2], send_stats[0:1]))
    sent.append(jnp.zeros((7, 128), F32))
    send[4 * TOK :, :] = jnp.concatenate(sent, 0).astype(BF16)
    for h in range(4):
        rows = slice(h * TOK, (h + 1) * TOK)
        attn_keep[rows, :] = attn[pl.ds(aligned(h * BLK + core * TOK, TOK), TOK), :]
        send[rows, :] = attn[pl.ds(aligned(h * BLK + (1 - core) * TOK, TOK), TOK), :]


def final_kernel(attn_keep, dec_keep, got, attn_out, dec_out):
    core = spot()[4]
    for h in range(4):
        rows = slice(h * TOK, (h + 1) * TOK)
        for src, head in ((attn_keep, core), (got, 1 - core)):
            attn_out[:, pl.ds(aligned((head * 4 + h) * HEAD, HEAD), HEAD)] = src[rows, :]
    theirs = got[4 * TOK :, :].astype(F32)
    other = theirs[8:9, :]
    for h in range(HEADS):
        top_a, top_b = dec_keep[8:9, h : h + 1], other[:, h : h + 1]
        total_a = dec_keep[8:9, HEADS + h : HEADS + h + 1]
        total_b = other[:, HEADS + h : HEADS + h + 1] + other[:, 2 * HEADS + h : 2 * HEADS + h + 1]
        top = jnp.maximum(top_a, top_b)
        scale_a, scale_b = jnp.exp2(top_a - top), jnp.exp2(top_b - top)
        mixed = dec_keep[h : h + 1, :] * scale_a + theirs[h : h + 1, :] * scale_b
        dec_out[h : h + 1, :] = (mixed / (total_a * scale_a + total_b * scale_b)).astype(BF16)


def exchange(x, groups):
    return lax.all_to_all(x, "seq", 0, 0, axis_index_groups=groups, tiled=True)


def to_other_core(x):
    return lax.ppermute(x, "seq", [(n, n ^ 1) for n in range(2 * SIDE * SIDE)])


def along_queries(x, by):
    pairs = []
    for group in QUERY_GROUPS:
        pairs += [(group[n], group[(n + by) % SIDE]) for n in range(SIDE)]
    return lax.ppermute(x, "seq", pairs)


def ring(block):
    ahead, back = [block], [block]
    for _ in range(SIDE // 2 - 1):
        ahead.append(along_queries(ahead[-1], 1))
        back.append(along_queries(back[-1], -1))
    front = along_queries(ahead[-1][:FRONT], 1)
    rest = along_queries(back[-1][FRONT:], -1)
    return ahead + [front, rest] + back[:0:-1]


def body(q_pre, k_pre, v_pre, old_k, old_v, src_page, page_row, page_len, q_dec, dec_k, dec_v):
    seq, grp = lax.axis_index("seq"), lax.axis_index("grp")
    core = seq & 1
    far = pl.BlockSpec(memory_space=pltpu.HBM)
    counts = page_row.shape[1]
    xs = call(
        pages_kernel,
        [((X_MSG, TWO), BF16)] * NG,
        (old_k.reshape(HALF, -1), old_v.reshape(HALF, -1), src_page, page_row, page_len),
        scratch=(
            pltpu.SMEM(src_page.shape, jnp.int32),
            pltpu.SMEM((1, counts), jnp.int32),
            pltpu.SMEM((1, counts), jnp.int32),
            pltpu.SemaphoreType.DMA((3 + 2 * NG,)),
        ),
        specs={n: far for n in range(5)},
    )
    xs = [xs[0]] + [
        lax.ppermute(xs[d], "grp", [(n, (n + d) % NG) for n in range(NG)]) for d in range(1, NG)
    ]
    keep, send = call(
        split_kernel,
        [((PAIR_MSG, 128), BF16)] * 2,
        (q_pre, k_pre, v_pre, *xs),
        scratch=(pltpu.SemaphoreType.DMA((12,)),),
        specs={n: far for n in range(3)},
    )
    q_mine = lax.dynamic_slice_in_dim(q_dec, grp * HEADS * HEAD, HEADS * HEAD, 2)
    q_mine = q_mine.reshape(ITEMS, HEADS * HEAD)

    def own_tokens(x):
        part = lax.dynamic_slice(x, (seq // STEPS, 0, grp * TWO), (1, STEPS, TWO))[0]
        return jnp.pad(part, ((0, 128 - STEPS), (0, 0)))

    kv_send, q_blk = call(
        local_kernel,
        [((SIDE, KV_MSG, 128), BF16), ((QROWS, 128), BF16)],
        (keep, to_other_core(send), q_mine, *xs, own_tokens(dec_k), own_tokens(dec_v)),
        scratch=(
            pltpu.VMEM((DEC_TOK, TWO), BF16),
            pltpu.VMEM((DEC_TOK, TWO), BF16),
            pltpu.VMEM((ITEMS, DEC_TOK), F32),
            pltpu.VMEM((BLK, HEAD), F32),
        ),
    )
    chunk, dec_send = call(
        merge_kernel,
        [((CHUNK, 128), BF16), ((SIDE, 18, 128), F32)],
        (exchange(kv_send, KEY_GROUPS),),
    )
    reduced = exchange(dec_send, QUERY_GROUPS)
    q_last = lax.dynamic_slice(
        q_dec,
        (seq // STEPS, seq % STEPS // 2 * 2, (grp * HEADS + core * 4) * HEAD),
        (1, 2, 4 * HEAD),
    )
    q_last = jnp.pad(q_last.reshape(HEADS, HEAD), ((0, FRESH - HEADS), (0, 0)))
    work = QROWS * SIDE * KEYS
    attn, fresh_o, fresh_s = call(
        attend_kernel,
        [((QROWS, HEAD), BF16), ((FRESH, 128), F32), ((FRESH, 128), F32)],
        (q_blk, q_last, *ring(chunk)),
        scratch=(
            pltpu.VMEM((KEYS, TWO), BF16),
            pltpu.VMEM((KEYS, TWO), BF16),
            pltpu.VMEM((BLK, BLK), F32),
            pltpu.VMEM((QROWS, TWO), BF16),
            pltpu.VMEM((TWO, KEYS), BF16),
            pltpu.VMEM((TWO, KEYS), BF16),
            pltpu.VMEM((QROWS, KEYS), F32),
            pltpu.VMEM((QROWS, KEYS), F32),
            pltpu.VMEM((QROWS, TWO), F32),
            pltpu.VMEM((QROWS, 128), F32),
        ),
        cost=pl.CostEstimate(flops=work * 512, bytes_accessed=4 * 1024 * 1024, transcendentals=work),
    )
    attn_keep, dec_keep, last = call(
        pair_kernel,
        [((4 * TOK, 128), BF16), ((16, 128), F32), ((LAST_MSG, 128), BF16)],
        (reduced, attn, fresh_o, fresh_s),
    )
    attn_out, dec_out = call(
        final_kernel,
        [((TOK, HEADS * HEAD), BF16), ((HEADS, HEAD), BF16)],
        (attn_keep, dec_keep, to_other_core(last)),
    )
    return attn_out, dec_out


def solution(mesh):
    return jax.shard_map(
        body,
        mesh=mesh,
        in_specs=(
            P("seq", "grp"),
            P("seq", "grp"),
            P("seq", "grp"),
            P("seq", "grp", None, None),
            P("seq", "grp", None, None),
            P("seq", None),
            P("seq", "grp"),
            P("seq", "grp"),
            P(),
            P(),
            P(),
        ),
        out_specs=(P("seq", "grp"), P(("seq", "grp"), None)),
        check_vma=False,
    )
```

time: 128 us -> 127 us (level)
  blocking collectives: 75.6 us -> 19.5 us
  starting transfers between devices: 20.3 us -> 61.6 us
  waiting for transfers between devices: 1.82 us -> 18.1 us
  local copies, waits for them, and re-layouts: 11 us -> 7.75 us
    all_to_all x4 -> x1, blocking collectives: 75.6 us -> 19.5 us  [exchange(): return lax.all_to_all(x, 'seq', 0, 0, axis_index_groups=groups, tiled=True)]
    ppermute x0 -> x11, starting transfers between devices: none -> 43.2 us  [the longest x8 31.7 us: along_queries(): return lax.ppermute(x, 'seq', pairs)]
    ppermute x0 -> x11, waiting for transfers between devices: none -> 17.2 us  [the longest x8 14.6 us: along_queries(): return lax.ppermute(x, 'seq', pairs)]
    unnamed x34 -> x20, local copies, waits for them, and re-layouts: 8.77 us -> 3.67 us
    slice x0 -> x2, local copies, waits for them, and re-layouts: none -> 1.45 us  [the longest x1 0.74 us: ring(): front = along_queries(ahead[-1][:FRONT], 1)]
    ppermute x2, starting transfers between devices: 16.1 us -> 14.8 us  [to_other_core(): return lax.ppermute(x, 'seq', [(n, n ^ 1) for n in range(2 * SIDE * SIDE)])]
    pallas_call x9 -> x7, Pallas kernels: 18 us -> 17.4 us  [call(): pl.pallas_call(kernel, out_shape=[jax.ShapeDtypeStruct(s, t) for s, t in...]
  transfers between devices with their start and end apart: 3 -> 14, of which waited for: 2 -> 6; matrix products, arithmetic and copies ran while one was open for 2% -> 3% of each run, Pallas kernels for 6% -> 8%
where the time goes in v2:
time: 127 us; the launch traced here: 125 us
  starting transfers between devices  61.6 us (49%)
  blocking collectives  19.5 us (15%)
  waiting for transfers between devices  18.1 us (14%)
  Pallas kernels  17.4 us (14%)
  local copies, waits for them, and re-layouts  7.75 us (6%)
    ppermute x8, starting transfers between devices, along_queries(): return lax.ppermute(x, 'seq', pairs)  31.7 us
    all_to_all x1, blocking collectives, exchange(): return lax.all_to_all(x, 'seq', 0, 0, axis_index_groups=groups, tiled=True)  19.5 us
    pallas_call x7, Pallas kernels, call(): pl.pallas_call(kernel, out_shape=[jax.ShapeDtypeStruct(s, t) for s, t in...  17.4 us
    ppermute x2, starting transfers between devices, to_other_core(): return lax.ppermute(x, 'seq', [(n, n ^ 1) for n in range(2 * SIDE * SIDE)])  14.8 us
    ppermute x8, waiting for transfers between devices, along_queries(): return lax.ppermute(x, 'seq', pairs)  14.6 us
    ppermute x3, starting transfers between devices, body(): lax.ppermute(xs[d], 'grp', [(n, (n + d) % NG) for n in range(NG)])  11.5 us
    unnamed x20, local copies, waits for them, and re-layouts  3.67 us
    all_to_all x1, starting transfers between devices, exchange(): return lax.all_to_all(x, 'seq', 0, 0, axis_index_groups=groups, tiled=True)  3.55 us
  transfers between devices with their start and end apart: 14, of which 6 were waited for; matrix products, arithmetic and copies ran while one was open for 3% of the time, Pallas kernels for 8%

profile of v2, /device:TPU:1, one launch (start us, length us, event | category | flops | bytes accessed | tf_op | source)
XLA Modules:
  0.0 125.3 jit_solution(14504804999516762958)
XLA Ops:
  1.3 1.0 copy-done
  4.0 4.1 %collective-permute-start = (bf16[336,256]{1,0:T(8,128)(2,1)S(1)}, bf16[336,256]{1,0:T(8,128)(2,1)S(1)}, u32[]{:S(2)}, u32[]{:S(2)}) collective-permute-start(bf16[336,256]{1,0:T(8,128)(2,1)S(1)} %get-tuple-element.19), channel_id=1, source_target_pairs={{0,1},{1,2},{2,3},{3,0},{4,5},{5,6},{6,7},{7,4},{8,9},{9,10},{10,1... | collective-permute-start | bytes 516104 | tf_op jit(solution)/shard_map/ppermute | solution.py:463
  8.1 4.4 %collective-permute-start.1 = (bf16[336,256]{1,0:T(8,128)(2,1)S(1)}, bf16[336,256]{1,0:T(8,128)(2,1)S(1)}, u32[]{:S(2)}, u32[]{:S(2)}) collective-permute-start(bf16[336,256]{1,0:T(8,128)(2,1)S(1)} %get-tuple-element.20), channel_id=1, source_target_pairs={{0,2},{1,3},{2,0},{3,1},{4,6},{5,7},{6,4},{7,5},{8,10},{9,11},{10,... | collective-permute-start | bytes 516104 | tf_op jit(solution)/shard_map/ppermute | solution.py:463
  12.4 3.1 %collective-permute-start.2 = (bf16[336,256]{1,0:T(8,128)(2,1)S(1)}, bf16[336,256]{1,0:T(8,128)(2,1)S(1)}, u32[]{:S(2)}, u32[]{:S(2)}) collective-permute-start(bf16[336,256]{1,0:T(8,128)(2,1)S(1)} %get-tuple-element.21), channel_id=1, source_target_pairs={{0,3},{1,0},{2,1},{3,2},{4,7},{5,4},{6,5},{7,6},{8,11},{9,8},{10,9... | collective-permute-start | bytes 516104 | tf_op jit(solution)/shard_map/ppermute | solution.py:463
  17.0 1.9 %collective-permute-done.2.x3 = bf16[336,256]{1,0:T(8,128)(2,1)S(1)} collective-permute-done((bf16[336,256]{1,0:T(8,128)(2,1)S(1)}, bf16[336,256]{1,0:T(8,128)(2,1)S(1)}, u32[]{:S(2)}, u32[]{:S(2)}) %collective-permute-start.2) | collective-permute-done | bytes 172064 | tf_op jit(solution)/shard_map/ppermute | solution.py:463
  19.2 7.2 %collective-permute-start.3 = (bf16[400,128]{1,0:T(8,128)(2,1)S(1)}, bf16[400,128]{1,0:T(8,128)(2,1)S(1)}, u32[]{:S(2)}, u32[]{:S(2)}) collective-permute-start(bf16[400,128]{1,0:T(8,128)(2,1)S(1)} %get-tuple-element.23), channel_id=1, source_target_pairs={{0,4},{4,0},{8,12},{12,8},{16,20},{20,16},{24,28},{28,24},{32,36},... | collective-permute-start | bytes 307208 | tf_op jit(solution)/shard_map/ppermute | solution.py:425
  26.4 1.1 constant_dynamic-slice_fusion
  27.6 4.1 %local.1 = (bf16[8,416,128]{2,1,0:T(8,128)(2,1)S(1)}, bf16[512,128]{1,0:T(8,128)(2,1)S(1)}) custom-call(bf16[400,128]{1,0:T(8,128)(2,1)S(1)} %get-tuple-element.22.keep, bf16[400,128]{1,0:T(8,128)(2,1)S(1)} %collective-permute-done.3.got, bf16[128,1024]{1,0:T(8,128)(2,1)S(1)} %reshape.18.q, bf16[336,256]{1,0:T(8,128)(2,1)S(1)} %get-tuple-element.18.x0, ...), custom_call_target="tpu_custom_call" | custom-call | tf_op jit(solution)/shard_map/local/pallas_call | solution.py:80
  31.7 19.5 %all_to_all.10.got = bf16[8,416,128]{2,1,0:T(8,128)(2,1)S(1)} all-to-all(bf16[8,416,128]{2,1,0:T(8,128)(2,1)S(1)} %get-tuple-element.24), channel_id=1, replica_groups={{0,64,128,192,256,320,384,448},{8,72,136,200,264,328,392,456},{16,80,14..., dimensions={0} | all-to-all | bytes 1703936 | tf_op jit(solution)/shard_map/all_to_all | solution.py:421
  52.1 3.7 %collective-permute-start.4 = (bf16[2064,128]{1,0:T(8,128)(2,1)S(1)}, bf16[2064,128]{1,0:T(8,128)(2,1)S(1)}, u32[]{:S(2)}, u32[]{:S(2)}) collective-permute-start(bf16[2064,128]{1,0:T(8,128)(2,1)S(1)} %get-tuple-element.27.refs_0_), channel_id=1, source_target_pairs={{0,8},{8,16},{16,24},{24,32},{32,40},{40,48},{48,56},{56,0},{64,72... | collective-permute-start | bytes 1585160 | tf_op jit(solution)/shard_map/ppermute | solution.py:432
  55.8 8.6 %collective-permute-start.8 = (bf16[2064,128]{1,0:T(8,128)(2,1)S(1)}, bf16[2064,128]{1,0:T(8,128)(2,1)S(1)}, u32[]{:S(2)}, u32[]{:S(2)}) collective-permute-start(bf16[2064,128]{1,0:T(8,128)(2,1)S(1)} %get-tuple-element.27.refs_0_), channel_id=1, source_target_pairs={{0,56},{8,0},{16,8},{24,16},{32,24},{40,32},{48,40},{56,48},{64,12... | collective-permute-start | bytes 1585160 | tf_op jit(solution)/shard_map/ppermute | solution.py:432
  64.4 4.7 %collective-permute-done.4.refs_1_ = bf16[2064,128]{1,0:T(8,128)(2,1)S(1)} collective-permute-done((bf16[2064,128]{1,0:T(8,128)(2,1)S(1)}, bf16[2064,128]{1,0:T(8,128)(2,1)S(1)}, u32[]{:S(2)}, u32[]{:S(2)}) %collective-permute-start.4) | collective-permute-done | bytes 528416 | tf_op jit(solution)/shard_map/ppermute | solution.py:432
  69.0 1.9 %collective-permute-start.5 = (bf16[2064,128]{1,0:T(8,128)(2,1)S(1)}, bf16[2064,128]{1,0:T(8,128)(2,1)S(1)}, u32[]{:S(2)}, u32[]{:S(2)}) collective-permute-start(bf16[2064,128]{1,0:T(8,128)(2,1)S(1)} %collective-permute-done.4.refs_1_), channel_id=1, source_target_pairs={{0,8},{8,16},{16,24},{24,32},{32,40},{40,48},{48,56},{56,0},{64,72... | collective-permute-start | bytes 1585160 | tf_op jit(solution)/shard_map/ppermute | solution.py:432
  71.0 4.6 %collective-permute-start.9 = (bf16[2064,128]{1,0:T(8,128)(2,1)S(1)}, bf16[2064,128]{1,0:T(8,128)(2,1)S(1)}, u32[]{:S(2)}, u32[]{:S(2)}) collective-permute-start(bf16[2064,128]{1,0:T(8,128)(2,1)S(1)} %collective-permute-done.8.refs_8_), channel_id=1, source_target_pairs={{0,56},{8,0},{16,8},{24,16},{32,24},{40,32},{48,40},{56,48},{64,12... | collective-permute-start | bytes 1585160 | tf_op jit(solution)/shard_map/ppermute | solution.py:432
  75.6 5.0 %collective-permute-done.5.refs_2_ = bf16[2064,128]{1,0:T(8,128)(2,1)S(1)} collective-permute-done((bf16[2064,128]{1,0:T(8,128)(2,1)S(1)}, bf16[2064,128]{1,0:T(8,128)(2,1)S(1)}, u32[]{:S(2)}, u32[]{:S(2)}) %collective-permute-start.5) | collective-permute-done | bytes 528416 | tf_op jit(solution)/shard_map/ppermute | solution.py:432
  80.5 1.9 %collective-permute-start.6 = (bf16[2064,128]{1,0:T(8,128)(2,1)S(1)}, bf16[2064,128]{1,0:T(8,128)(2,1)S(1)}, u32[]{:S(2)}, u32[]{:S(2)}) collective-permute-start(bf16[2064,128]{1,0:T(8,128)(2,1)S(1)} %collective-permute-done.5.refs_2_), channel_id=1, source_target_pairs={{0,8},{8,16},{16,24},{24,32},{32,40},{40,48},{48,56},{56,0},{64,72... | collective-permute-start | bytes 1585160 | tf_op jit(solution)/shard_map/ppermute | solution.py:432
  82.4 4.6 %collective-permute-start.10 = (bf16[2064,128]{1,0:T(8,128)(2,1)S(1)}, bf16[2064,128]{1,0:T(8,128)(2,1)S(1)}, u32[]{:S(2)}, u32[]{:S(2)}) collective-permute-start(bf16[2064,128]{1,0:T(8,128)(2,1)S(1)} %collective-permute-done.9.refs_7_), channel_id=1, source_target_pairs={{0,56},{8,0},{16,8},{24,16},{32,24},{40,32},{48,40},{56,48},{64,12... | collective-permute-start | bytes 1585160 | tf_op jit(solution)/shard_map/ppermute | solution.py:432
  87.0 4.9 %collective-permute-done.6.refs_3_ = bf16[2064,128]{1,0:T(8,128)(2,1)S(1)} collective-permute-done((bf16[2064,128]{1,0:T(8,128)(2,1)S(1)}, bf16[2064,128]{1,0:T(8,128)(2,1)S(1)}, u32[]{:S(2)}, u32[]{:S(2)}) %collective-permute-start.6) | collective-permute-done | bytes 528416 | tf_op jit(solution)/shard_map/ppermute | solution.py:432
  92.7 1.9 %collective-permute-start.7 = (bf16[1040,128]{1,0:T(8,128)(2,1)}, bf16[1040,128]{1,0:T(8,128)(2,1)}, u32[]{:S(2)}, u32[]{:S(2)}) collective-permute-start(bf16[1040,128]{1,0:T(8,128)(2,1)} %slice.8), channel_id=1, source_target_pairs={{0,8},{8,16},{16,24},{24,32},{32,40},{40,48},{48,56},{56,0},{64,72... | collective-permute-start | bytes 798728 | tf_op jit(solution)/shard_map/ppermute | solution.py:432
  95.4 4.6 %collective-permute-start.11 = (bf16[1024,128]{1,0:T(8,128)(2,1)}, bf16[1024,128]{1,0:T(8,128)(2,1)}, u32[]{:S(2)}, u32[]{:S(2)}) collective-permute-start(bf16[1024,128]{1,0:T(8,128)(2,1)} %slice.9), channel_id=1, source_target_pairs={{0,56},{8,0},{16,8},{24,16},{32,24},{40,32},{48,40},{56,48},{64,12... | collective-permute-start | bytes 786440 | tf_op jit(solution)/shard_map/ppermute | solution.py:432
  100.8 3.5 %all-to-all-start.1 = ((f32[8,18,128]{2,1,0:T(8,128)}), f32[8,18,128]{2,1,0:T(8,128)S(1)}, u32[]{:S(2)}, u32[]{:S(2)}) async-start(f32[8,18,128]{2,1,0:T(8,128)} %get-tuple-element.25), calls=%async_computation.1 | async-start | bytes 196608 | tf_op jit(solution)/shard_map/all_to_all | solution.py:421
  104.3 1.0 copy-done.9
  105.4 10.3 %attend.1 = (bf16[512,128]{1,0:T(8,128)(2,1)S(1)}, f32[16,128]{1,0:T(8,128)S(1)}, f32[16,128]{1,0:T(8,128)S(1)}) custom-call(bf16[512,128]{1,0:T(8,128)(2,1)S(1)} %get-tuple-element.26.q, bf16[16,128]{1,0:T(8,128)(2,1)S(1)} %pad.13.q_dec, bf16[2064,128]{1,0:T(8,128)(2,1)S(1)} %get-tuple-element.27.refs_0_, ...), custom_call_target="tpu_custom_call" | custom-call | flops 2147483648 | bytes 4194304 | tf_op jit(solution)/shard_map/attend/pallas_call | solution.py:80
  116.0 7.6 %collective-permute-start.12 = (bf16[272,128]{1,0:T(8,128)(2,1)S(1)}, bf16[272,128]{1,0:T(8,128)(2,1)S(1)}, u32[]{:S(2)}, u32[]{:S(2)}) collective-permute-start(bf16[272,128]{1,0:T(8,128)(2,1)S(1)} %get-tuple-element.33), channel_id=1, source_target_pairs={{0,4},{4,0},{8,12},{12,8},{16,20},{20,16},{24,28},{28,24},{32,36},... | collective-permute-start | bytes 208904 | tf_op jit(solution)/shard_map/ppermute | solution.py:425
  (42 shorter events, 9.3 us)
Async XLA Ops:
  0.6 0.7 copy-start.5
  0.6 0.7 copy-start.6
  0.7 0.7 copy-start.7
  1.3 1.0 copy-start
  2.3 1.0 copy-start.1
  4.0 14.9 %copy-start.2 = (bf16[64,1024]{1,0:T(8,128)(2,1)S(1)}, bf16[64,1024]{1,0:T(8,128)(2,1)}, u32[]{:S(2)}) copy-start(bf16[64,1024]{1,0:T(8,128)(2,1)} %q.1) | copy-start | bytes 393220
  4.0 12.3 %collective-permute-start = (bf16[336,256]{1,0:T(8,128)(2,1)S(1)}, bf16[336,256]{1,0:T(8,128)(2,1)S(1)}, u32[]{:S(2)}, u32[]{:S(2)}) collective-permute-start(bf16[336,256]{1,0:T(8,128)(2,1)S(1)} %get-tuple-element.19), channel_id=1, source_target_pairs={{0,1},{1,2},{2,3},{3,0},{4,5},{5,6},{6,7},{7,4},{8,9},{9,10},{10,1... | collective-permute-start | bytes 516104 | tf_op jit(solution)/shard_map/ppermute | solution.py:463
  8.1 8.9 %collective-permute-start.1 = (bf16[336,256]{1,0:T(8,128)(2,1)S(1)}, bf16[336,256]{1,0:T(8,128)(2,1)S(1)}, u32[]{:S(2)}, u32[]{:S(2)}) collective-permute-start(bf16[336,256]{1,0:T(8,128)(2,1)S(1)} %get-tuple-element.20), channel_id=1, source_target_pairs={{0,2},{1,3},{2,0},{3,1},{4,6},{5,7},{6,4},{7,5},{8,10},{9,11},{10,... | collective-permute-start | bytes 516104 | tf_op jit(solution)/shard_map/ppermute | solution.py:463
  12.4 6.4 %collective-permute-start.2 = (bf16[336,256]{1,0:T(8,128)(2,1)S(1)}, bf16[336,256]{1,0:T(8,128)(2,1)S(1)}, u32[]{:S(2)}, u32[]{:S(2)}) collective-permute-start(bf16[336,256]{1,0:T(8,128)(2,1)S(1)} %get-tuple-element.21), channel_id=1, source_target_pairs={{0,3},{1,0},{2,1},{3,2},{4,7},{5,4},{6,5},{7,6},{8,11},{9,8},{10,9... | collective-permute-start | bytes 516104 | tf_op jit(solution)/shard_map/ppermute | solution.py:463
  16.3 2.6 %copy-start.3 = (bf16[64,256]{1,0:T(8,128)(2,1)S(1)}, bf16[64,256]{1,0:T(8,128)(2,1)}, u32[]{:S(2)}) copy-start(bf16[64,256]{1,0:T(8,128)(2,1)} %k.1) | copy-start | bytes 98308
  16.3 2.6 %copy-start.4 = (bf16[64,256]{1,0:T(8,128)(2,1)S(1)}, bf16[64,256]{1,0:T(8,128)(2,1)}, u32[]{:S(2)}) copy-start(bf16[64,256]{1,0:T(8,128)(2,1)} %v.1) | copy-start | bytes 98308
  19.2 8.4 %collective-permute-start.3 = (bf16[400,128]{1,0:T(8,128)(2,1)S(1)}, bf16[400,128]{1,0:T(8,128)(2,1)S(1)}, u32[]{:S(2)}, u32[]{:S(2)}) collective-permute-start(bf16[400,128]{1,0:T(8,128)(2,1)S(1)} %get-tuple-element.23), channel_id=1, source_target_pairs={{0,4},{4,0},{8,12},{12,8},{16,20},{20,16},{24,28},{28,24},{32,36},... | collective-permute-start | bytes 307208 | tf_op jit(solution)/shard_map/ppermute | solution.py:425
  52.1 17.0 %collective-permute-start.4 = (bf16[2064,128]{1,0:T(8,128)(2,1)S(1)}, bf16[2064,128]{1,0:T(8,128)(2,1)S(1)}, u32[]{:S(2)}, u32[]{:S(2)}) collective-permute-start(bf16[2064,128]{1,0:T(8,128)(2,1)S(1)} %get-tuple-element.27.refs_0_), channel_id=1, source_target_pairs={{0,8},{8,16},{16,24},{24,32},{32,40},{40,48},{48,56},{56,0},{64,72... | collective-permute-start | bytes 1585160 | tf_op jit(solution)/shard_map/ppermute | solution.py:432
  55.8 15.2 %collective-permute-start.8 = (bf16[2064,128]{1,0:T(8,128)(2,1)S(1)}, bf16[2064,128]{1,0:T(8,128)(2,1)S(1)}, u32[]{:S(2)}, u32[]{:S(2)}) collective-permute-start(bf16[2064,128]{1,0:T(8,128)(2,1)S(1)} %get-tuple-element.27.refs_0_), channel_id=1, source_target_pairs={{0,56},{8,0},{16,8},{24,16},{32,24},{40,32},{48,40},{56,48},{64,12... | collective-permute-start | bytes 1585160 | tf_op jit(solution)/shard_map/ppermute | solution.py:432
  69.0 11.5 %collective-permute-start.5 = (bf16[2064,128]{1,0:T(8,128)(2,1)S(1)}, bf16[2064,128]{1,0:T(8,128)(2,1)S(1)}, u32[]{:S(2)}, u32[]{:S(2)}) collective-permute-start(bf16[2064,128]{1,0:T(8,128)(2,1)S(1)} %collective-permute-done.4.refs_1_), channel_id=1, source_target_pairs={{0,8},{8,16},{16,24},{24,32},{32,40},{40,48},{48,56},{56,0},{64,72... | collective-permute-start | bytes 1585160 | tf_op jit(solution)/shard_map/ppermute | solution.py:432
  71.0 11.5 %collective-permute-start.9 = (bf16[2064,128]{1,0:T(8,128)(2,1)S(1)}, bf16[2064,128]{1,0:T(8,128)(2,1)S(1)}, u32[]{:S(2)}, u32[]{:S(2)}) collective-permute-start(bf16[2064,128]{1,0:T(8,128)(2,1)S(1)} %collective-permute-done.8.refs_8_), channel_id=1, source_target_pairs={{0,56},{8,0},{16,8},{24,16},{32,24},{40,32},{48,40},{56,48},{64,12... | collective-permute-start | bytes 1585160 | tf_op jit(solution)/shard_map/ppermute | solution.py:432
  80.5 11.5 %collective-permute-start.6 = (bf16[2064,128]{1,0:T(8,128)(2,1)S(1)}, bf16[2064,128]{1,0:T(8,128)(2,1)S(1)}, u32[]{:S(2)}, u32[]{:S(2)}) collective-permute-start(bf16[2064,128]{1,0:T(8,128)(2,1)S(1)} %collective-permute-done.5.refs_2_), channel_id=1, source_target_pairs={{0,8},{8,16},{16,24},{24,32},{32,40},{40,48},{48,56},{56,0},{64,72... | collective-permute-start | bytes 1585160 | tf_op jit(solution)/shard_map/ppermute | solution.py:432
  82.4 12.2 %copy-start.8 = (bf16[2064,128]{1,0:T(8,128)(2,1)}, bf16[2064,128]{1,0:T(8,128)(2,1)S(1)}, u32[]{:S(2)}) copy-start(bf16[2064,128]{1,0:T(8,128)(2,1)S(1)} %collective-permute-done.9.refs_7_) | copy-start | bytes 1585156
  82.4 12.2 %collective-permute-start.10 = (bf16[2064,128]{1,0:T(8,128)(2,1)S(1)}, bf16[2064,128]{1,0:T(8,128)(2,1)S(1)}, u32[]{:S(2)}, u32[]{:S(2)}) collective-permute-start(bf16[2064,128]{1,0:T(8,128)(2,1)S(1)} %collective-permute-done.9.refs_7_), channel_id=1, source_target_pairs={{0,56},{8,0},{16,8},{24,16},{32,24},{40,32},{48,40},{56,48},{64,12... | collective-permute-start | bytes 1585160 | tf_op jit(solution)/shard_map/ppermute | solution.py:432
  92.7 11.6 %collective-permute-start.7 = (bf16[1040,128]{1,0:T(8,128)(2,1)}, bf16[1040,128]{1,0:T(8,128)(2,1)}, u32[]{:S(2)}, u32[]{:S(2)}) collective-permute-start(bf16[1040,128]{1,0:T(8,128)(2,1)} %slice.8), channel_id=1, source_target_pairs={{0,8},{8,16},{16,24},{24,32},{32,40},{40,48},{48,56},{56,0},{64,72... | collective-permute-start | bytes 798728 | tf_op jit(solution)/shard_map/ppermute | solution.py:432
  95.4 9.0 %collective-permute-start.11 = (bf16[1024,128]{1,0:T(8,128)(2,1)}, bf16[1024,128]{1,0:T(8,128)(2,1)}, u32[]{:S(2)}, u32[]{:S(2)}) collective-permute-start(bf16[1024,128]{1,0:T(8,128)(2,1)} %slice.9), channel_id=1, source_target_pairs={{0,56},{8,0},{16,8},{24,16},{32,24},{40,32},{48,40},{56,48},{64,12... | collective-permute-start | bytes 786440 | tf_op jit(solution)/shard_map/ppermute | solution.py:432
  100.8 14.9 %all-to-all-start.1 = ((f32[8,18,128]{2,1,0:T(8,128)}), f32[8,18,128]{2,1,0:T(8,128)S(1)}, u32[]{:S(2)}, u32[]{:S(2)}) async-start(f32[8,18,128]{2,1,0:T(8,128)} %get-tuple-element.25), calls=%async_computation.1 | async-start | bytes 196608 | tf_op jit(solution)/shard_map/all_to_all | solution.py:421
  104.3 1.0 copy-start.9
  116.0 8.5 %collective-permute-start.12 = (bf16[272,128]{1,0:T(8,128)(2,1)S(1)}, bf16[272,128]{1,0:T(8,128)(2,1)S(1)}, u32[]{:S(2)}, u32[]{:S(2)}) collective-permute-start(bf16[272,128]{1,0:T(8,128)(2,1)S(1)} %get-tuple-element.33), channel_id=1, source_target_pairs={{0,4},{4,0},{8,12},{12,8},{16,20},{20,16},{24,28},{28,24},{32,36},... | collective-permute-start | bytes 208904 | tf_op jit(solution)/shard_map/ppermute | solution.py:425

commit v3 on v2

--- a/solution.py
+++ b/solution.py
@@ -41,7 +41,15 @@
 CHUNK = FRONT + KEYS
 PAGES = KEYS // PAGE
 LAST_MSG = 4 * TOK + 16
-FRESH = 16
+QUAD = 4
+PAIR_DEC = 80
+PAIR_ALL = CHUNK + PAIR_DEC
+Q_META = QROWS
+Q_DEC = QROWS + META
+Q_MSG = Q_DEC + 32
+O_FRESH = QROWS + META
+O_MSG = O_FRESH + 16
+FRESH = 4 * 16
 NT = (((1,), (1,)), ((), ()))
 F32 = jnp.float32
 BF16 = jnp.bfloat16
@@ -55,6 +63,8 @@
 ALONG_Y = [[[seq_of(j, i, c) for i in range(SIDE)] for j in range(SIDE)] for c in range(2)]
 KEY_GROUPS = ALONG_Z[0] + ALONG_Y[1]
 QUERY_GROUPS = ALONG_Y[0] + ALONG_Z[1]
+QUADS = [group[p::2] for group in QUERY_GROUPS for p in range(2)]
+NEIGHBOURS = [(group[n], group[n ^ 1]) for group in QUERY_GROUPS for n in range(SIDE)]
 
 
 def iota(shape, dim):
@@ -211,72 +221,105 @@
     kv_send[:, KV_DEC + HEADS * PER :, :] = stats.astype(BF16).reshape(SIDE, PER, 128)
 
 
-def attend_kernel(q, q_dec, *refs):
-    bufs = refs[:9]
-    attn, fresh_o, fresh_s = refs[9:12]
-    vs_a, vs_b, tri, qx, kx_a, kx_b, s_a, s_b, acc, tops = refs[12:]
-    seq, _, z, y, core, _, u = spot()
+def attend_kernel(qs, near, other, q_dec, out, *refs):
+    vs, tri, sel = refs[:3]
+    sides = (refs[3:8], refs[8:13])
+    seq, _, z, y, core, w, u = spot()
     even = core == 0
-    keys_at = [bufs[d] if d < 5 else bufs[d + 1] for d in range(SIDE)]
+    chunks = ((near, u), (other, u ^ 1))
     row, col = iota((BLK, BLK), 0), iota((BLK, BLK), 1)
     tri[...] = jnp.where(col > row, HIDE, 0.0)
     same = jnp.where(row == col, 1.0, 0.0).astype(BF16)
-    qx[:, :HEAD] = q[...]
-    for h in range(4):
-        qx[h * BLK : (h + 1) * BLK, HEAD:] = same
-    first = jnp.where(iota((KEYS, HEAD), 1) == 0, 1.0, 0.0).astype(BF16)
-    vs_a[:, HEAD:] = first
-    vs_b[:, HEAD:] = first
-    acc[...] = jnp.zeros_like(acc)
-    tops[...] = jnp.full_like(tops, LOWEST)
-
-    numbers = jnp.concatenate([ref[:META, :].astype(F32) for ref in keys_at], axis=1)
+    for side in sides:
+        for h in range(4):
+            side[0][h * BLK : (h + 1) * BLK, HEAD:] = same
+        for c, (chunk, _) in enumerate(chunks):
+            for m in range(SIDE):
+                cols = slice(m * BLK, (m + 1) * BLK)
+                side[1 + c][:HEAD, cols] = chunk[META + m * BLK : META + (m + 1) * BLK, :]
+    for c, (chunk, _) in enumerate(chunks):
+        vs[c * KEYS : (c + 1) * KEYS, :HEAD] = chunk[FRONT:CHUNK, :]
+    vs[:, HEAD:] = jnp.where(iota((2 * KEYS, HEAD), 1) == 0, 1.0, 0.0).astype(BF16)
+
+    def score(j, qx, kx_a, kx_b, s_a, s_b):
+        to = j * 2 + (u & 1)
+        qx[:, :HEAD] = qs[j, :QROWS, :]
+        for (_, n), kx, s in zip(chunks, (kx_a, kx_b), (s_a, s_b)):
+            full = jnp.where(
+                even,
+                w + jnp.where(n < to, 1, 0),
+                jnp.where(n < to, SIDE, jnp.where(n == to, w, 0)),
+            )
+            edge = jnp.where(n == to, w, SIDE)
+            for m in range(SIDE):
+                hidden = jnp.where(m == edge, tri[...], HIDE)
+                hidden = jnp.where(m < full, 0.0, hidden).astype(BF16)
+                kx[HEAD:, m * BLK : (m + 1) * BLK] = hidden
+            s[...] = jnp.dot(qx[...], kx[...], preferred_element_type=F32)
+
+    def mix(j, s_a, s_b):
+        lane = iota((BLK, 128), 1)
+        stats = jnp.zeros((BLK, 128), F32)
+        for part in range(2):
+            rows = slice(part * 2 * BLK, (part + 1) * 2 * BLK)
+            both = (s_a[rows, :], s_b[rows, :])
+            top = EXP2_SCALE * jnp.max(jnp.maximum(*both), axis=1, keepdims=True)
+            top = jnp.maximum(top, LOWEST).astype(BF16).astype(F32)
+            mixed = 0.0
+            for c in range(2):
+                weights = jnp.exp2(both[c] * EXP2_SCALE - top).astype(BF16)
+                mixed = mixed + jnp.dot(
+                    weights, vs[c * KEYS : (c + 1) * KEYS, :], preferred_element_type=F32
+                )
+            out[j, rows, :] = mixed[:, :HEAD].astype(BF16)
+            total = mixed[:, HEAD : HEAD + 1]
+            high = total.astype(BF16).astype(F32)
+            for h in range(2):
+                one = slice(h * BLK, (h + 1) * BLK)
+                at = part * 2 + h
+                stats = jnp.where(lane == at, top[one], stats)
+                stats = jnp.where(lane == 4 + at, high[one], stats)
+                stats = jnp.where(lane == 8 + at, (total - high)[one], stats)
+        out[j, QROWS:O_FRESH, :] = jnp.transpose(stats)[:META].astype(BF16)
+
+    score(0, *sides[0])
+    for j in range(QUAD):
+        if j + 1 < QUAD:
+            score(j + 1, *sides[(j + 1) % 2])
+        mix(j, *sides[j % 2][3:])
+
+    def chip_of(there, across):
+        return jnp.where(even, across * SIDE + there, there * SIDE + across)
+
+    numbers = jnp.concatenate(
+        [qs[j, Q_META : Q_META + 8, :].astype(F32) for j in range(QUAD)], axis=1
+    )
+    numbers = jnp.concatenate([numbers[0:4], numbers[4:8]], axis=1)
     source = numbers[0:1, :] * 4.0 + numbers[1:2, :]
-    mine = numbers[2:3, :] == (seq >> 2).astype(F32)
     slots = source.shape[1]
-    live = mine & (iota((PAGE, slots), 0).astype(F32) < numbers[3:4, :])
-    live = jnp.where(live, 1.0, 0.0).astype(BF16)
+    inside = iota((PAGE, slots), 0).astype(F32) < numbers[3:4, :]
+    live = []
+    for j in range(QUAD):
+        owner = (chip_of(j * 2 + (u & 1), w) >> 1).astype(F32)
+        live.append(jnp.where((numbers[2:3, :] == owner) & inside, 1.0, 0.0))
+    live = jnp.concatenate(live, axis=0).astype(BF16)
     spread = iota((PAGES, KEYS), 1) >> 4 == iota((PAGES, KEYS), 0)
     spread = jnp.where(spread, 1.0, 0.0).astype(BF16)
-    at = (iota((PAGE, KEYS), 1) & 15) == iota((PAGE, KEYS), 0)
-
-    def far(d):
-        return (u - d + SIDE) & (SIDE - 1)
-
-    def score(d, kx, vs, s):
-        n = far(d)
-        full = jnp.where(
-            even,
-            z + jnp.where(n < y, 1, 0),
-            jnp.where(n < z, SIDE, jnp.where(n == z, y, 0)),
-        )
-        edge = jnp.where(n == u, full, SIDE)
-        for m in range(SIDE):
-            cols = slice(m * BLK, (m + 1) * BLK)
-            kx[:HEAD, cols] = keys_at[d][META + m * BLK : META + (m + 1) * BLK, :]
-            hidden = jnp.where(m == edge, tri[...], HIDE)
-            kx[HEAD:, cols] = jnp.where(m < full, 0.0, hidden).astype(BF16)
-        vs[:, :HEAD] = bufs[5][...] if d == 4 else keys_at[d][FRONT:, :]
-        s[...] = jnp.dot(qx[...], kx[...], preferred_element_type=F32)
-
-    def mix(s, vs):
-        for part in range(2):
-            rows = slice(part * 2 * BLK, (part + 1) * 2 * BLK)
-            scores = s[rows, :]
-            before = tops[rows, :]
-            top = jnp.maximum(before, EXP2_SCALE * jnp.max(scores, axis=1, keepdims=True))
-            tops[rows, :] = top
-            weights = jnp.exp2(scores * EXP2_SCALE - top[:, :1]).astype(BF16)
-            mixed = jnp.dot(weights, vs[...], preferred_element_type=F32)
-            acc[rows, :] = acc[rows, :] * jnp.exp2(before - top)[:, :1] + mixed
-
-    def copied(d, kx, vs, state):
-        before, mixed = state
-        n = far(d)
+    at = (iota((PAGE * QUAD, KEYS), 1) & 15) == (iota((PAGE * QUAD, KEYS), 0) & 15)
+
+    pick = iota((16, ITEMS), 0)
+    item = chip_of((pick >> 1) * 2 + (u & 1), w) * 2 + (pick & 1)
+    pick = jnp.where((iota((16, ITEMS), 1) == item) & (pick < 8), 1.0, 0.0).astype(BF16)
+    for h in range(4):
+        cols = pl.ds(aligned((core * 4 + h) * HEAD, HEAD), HEAD)
+        sel[h * 16 : (h + 1) * 16, :] = jnp.dot(
+            pick, q_dec[:, cols], preferred_element_type=F32
+        ).astype(BF16)
+
+    all_scores, all_terms = [], []
+    for c, (_, n) in enumerate(chunks):
         page = iota((PAGES, slots), 0)
-        w = page >> 3
-        chip = jnp.where(even, w * SIDE + n, n * SIDE + w)
-        page = (chip * SIDE + (page & 7)).astype(F32)
+        page = (chip_of(n, page >> 3) * SIDE + (page & 7)).astype(F32)
         there = jnp.where(source == page, 1.0, 0.0).astype(BF16)
         count = lax.dot_general(live, there, NT, preferred_element_type=F32)
         high = count.astype(BF16)
@@ -284,29 +327,33 @@
         count = jnp.dot(high, spread, preferred_element_type=F32) + jnp.dot(
             low, spread, preferred_element_type=F32
         )
-        terms = jnp.sum(jnp.where(at, count, 0.0), axis=0, keepdims=True)
-        scores = EXP2_SCALE * jnp.dot(q_dec[...], kx[:HEAD, :], preferred_element_type=F32)
-        scores = jnp.where(terms > 0.5, scores, NEG)
-        top = jnp.max(scores, axis=1, keepdims=True).astype(BF16).astype(F32)
-        top = jnp.maximum(before, top)
-        weights = (jnp.exp2(scores - top) * terms).astype(BF16)
-        mixed = mixed * jnp.exp2(before - top)
-        return top, mixed + jnp.dot(weights, vs[...], preferred_element_type=F32)
-
-    sides = ((kx_a, vs_a, s_a), (kx_b, vs_b, s_b))
-    state = (jnp.full((FRESH, 1), NEG, F32), jnp.zeros((FRESH, TWO), F32))
-    score(0, *sides[0])
-    for d in range(SIDE):
-        kx, vs, s = sides[d % 2]
-        if d + 1 < SIDE:
-            score(d + 1, *sides[(d + 1) % 2])
-        mix(s, vs)
-        state = copied(d, kx, vs, state)
-    attn[...] = (acc[:, :HEAD] / acc[:, HEAD : HEAD + 1]).astype(BF16)
-    top, mixed = state
-    fresh_o[...] = mixed[:, :HEAD]
+        count = jnp.where(at, count, 0.0)
+        which = iota((16, KEYS), 0) >> 1
+        terms = jnp.zeros((16, KEYS), F32)
+        for j in range(QUAD):
+            one = jnp.sum(count[j * PAGE : (j + 1) * PAGE], axis=0, keepdims=True)
+            terms = jnp.where(which == j, one, terms)
+        terms = jnp.concatenate([terms] * 4, axis=0)
+        keys = sides[0][1 + c][:HEAD, :]
+        scores = EXP2_SCALE * jnp.dot(sel[...], keys, preferred_element_type=F32)
+        all_scores.append(jnp.where(terms > 0.5, scores, NEG))
+        all_terms.append(terms)
+    top = jnp.max(jnp.maximum(*all_scores), axis=1, keepdims=True).astype(BF16).astype(F32)
+    mixed = 0.0
+    for c in range(2):
+        weights = (jnp.exp2(all_scores[c] - top) * all_terms[c]).astype(BF16)
+        mixed = mixed + jnp.dot(
+            weights, vs[c * KEYS : (c + 1) * KEYS, :], preferred_element_type=F32
+        )
+    total = mixed[:, HEAD : HEAD + 1]
+    high = total.astype(BF16).astype(F32)
     lane = iota((FRESH, 128), 1)
-    fresh_s[...] = jnp.where(lane == 0, top, jnp.where(lane == 1, mixed[:, HEAD : HEAD + 1], 0.0))
+    stats = jnp.where(lane == 0, top, jnp.where(lane == 1, high, 0.0))
+    stats = jnp.where(lane == 2, total - high, stats)
+    for j in range(QUAD):
+        rows = [slice(h * 16 + 2 * j, h * 16 + 2 * j + 2) for h in range(4)]
+        pieces = [mixed[r, :HEAD] for r in rows] + [stats[r] for r in rows]
+        out[j, O_FRESH:, :] = jnp.concatenate(pieces, axis=0).astype(BF16)
 
 
 def combine(values, stats, split):
@@ -342,11 +389,11 @@
     return tile
 
 
-def merge_kernel(got, chunk, dec_send):
-    chunk[:META, :] = sum(got[n, 2 * BLK : KV_DEC, :].astype(F32) for n in range(SIDE)).astype(BF16)
+def merge_kernel(got, send, keep):
+    send[:META, :] = sum(got[n, 2 * BLK : KV_DEC, :].astype(F32) for n in range(SIDE)).astype(BF16)
     for n in range(SIDE):
-        chunk[META + n * BLK : META + (n + 1) * BLK, :] = got[n, :BLK, :]
-        chunk[FRONT + n * BLK : FRONT + (n + 1) * BLK, :] = got[n, BLK : 2 * BLK, :]
+        send[META + n * BLK : META + (n + 1) * BLK, :] = got[n, :BLK, :]
+        send[FRONT + n * BLK : FRONT + (n + 1) * BLK, :] = got[n, BLK : 2 * BLK, :]
 
     def values(n):
         return lambda h: got[n, KV_DEC + h * PER : KV_DEC + (h + 1) * PER, :].astype(F32)
@@ -356,32 +403,85 @@
         [got[n, KV_MSG - PER :, :].astype(F32) for n in range(SIDE)],
         True,
     )
-    for m, piece in enumerate(mixes + [stat_tile(tops, totals)]):
-        for n in range(SIDE):
-            dec_send[n, 2 * m : 2 * m + 2, :] = piece[2 * n : 2 * n + 2, :]
-
-
-def pair_kernel(got, attn, fresh_o, fresh_s, attn_keep, dec_keep, send):
+    even = spot()[6] & 1 == 0
+
+    def halves(x):
+        a = jnp.concatenate([x[4 * n : 4 * n + 2] for n in range(QUAD)], axis=0)
+        b = jnp.concatenate([x[4 * n + 2 : 4 * n + 4] for n in range(QUAD)], axis=0)
+        return jnp.where(even, a, b), jnp.where(even, b, a)
+
+    theirs = []
+    for h in range(HEADS):
+        mine, other = halves(mixes[h])
+        keep[8 * h : 8 * h + 8, :] = mine
+        theirs.append(other)
+    mine, other = halves(stat_tile(tops, totals, True))
+    keep[64:, :] = mine
+    theirs += [other, jnp.zeros((8, 128), F32)]
+    send[CHUNK:, :] = jnp.concatenate(theirs, axis=0).astype(BF16)
+
+
+def queries_kernel(q_blk, near, other, keep, send):
+    def kept(h):
+        return keep[8 * h : 8 * h + 8, :]
+
+    def came(h):
+        return other[CHUNK + 8 * h : CHUNK + 8 * h + 8, :].astype(F32)
+
+    mixes, tops, totals = combine(
+        [kept, came], [keep[64:, :], other[CHUNK + 64 : CHUNK + 72, :].astype(F32)], True
+    )
+    pieces = mixes + [stat_tile(tops, totals, True)]
+    numbers = jnp.concatenate(
+        [near[:META, :].astype(F32)[:4], other[:META, :].astype(F32)[:4], jnp.zeros((8, 128), F32)], 0
+    ).astype(BF16)
+    for n in range(QUAD):
+        send[n, :QROWS, :] = q_blk[...]
+        send[n, Q_META:Q_DEC, :] = numbers
+        rows = [piece[2 * n : 2 * n + 2] for piece in pieces] + [jnp.zeros((14, 128), F32)]
+        send[n, Q_DEC:, :] = jnp.concatenate(rows, axis=0).astype(BF16)
+
+
+def pair_kernel(got, qs, attn_keep, dec_keep, send, attn):
     core = spot()[4]
     even = core == 0
-
-    def values(n):
-        return lambda h: got[n, 2 * h : 2 * h + 2, :]
-
-    def fresh(h):
-        return jnp.concatenate([fresh_o[h % 4 : h % 4 + 1, :], fresh_o[4 + h % 4 : 5 + h % 4, :]], 0)
-
+    stats = [got[n, QROWS:O_FRESH, :].astype(F32) for n in range(QUAD)]
+    tops = [s[0:4] for s in stats]
+    top = functools.reduce(jnp.maximum, tops)
+    factors = [jnp.exp2(t - top) for t in tops]
+    total = sum(f * (s[4:8] + s[8:12]) for f, s in zip(factors, stats))
+    shares = jnp.concatenate([f / total for f in factors] + [jnp.zeros((112, 128), F32)], 0)
+    shares = jnp.transpose(shares)
+    for h in range(4):
+        rows = slice(h * BLK, (h + 1) * BLK)
+        out = 0.0
+        for n in range(QUAD):
+            out = out + got[n, rows, :].astype(F32) * shares[:, n * 4 + h : n * 4 + h + 1]
+        attn[rows, :] = out.astype(BF16)
+
+    def old(n):
+        return lambda h: qs[n, Q_DEC:, :].astype(F32)[2 * h : 2 * h + 2]
+
+    def fresh(n):
+        return lambda h: got[n, O_FRESH:, :].astype(F32)[2 * (h % 4) : 2 * (h % 4) + 2]
+
+    old_stats = [qs[n, Q_DEC:, :].astype(F32)[16:18] for n in range(QUAD)]
+    fresh_stats = []
     lane = iota((2, 128), 1)
-    stats = jnp.zeros((2, 128), F32)
-    for h in range(HEADS):
-        both = jnp.concatenate([fresh_s[h % 4 : h % 4 + 1, :], fresh_s[4 + h % 4 : 5 + h % 4, :]], 0)
-        here = core == h // 4
-        stats = jnp.where(lane == h, jnp.where(here, both[:, 0:1], NEG), stats)
-        stats = jnp.where(lane == HEADS + h, jnp.where(here, both[:, 1:2], 0.0), stats)
+    for n in range(QUAD):
+        tile = got[n, O_FRESH:, :].astype(F32)[8:]
+        placed = jnp.zeros((2, 128), F32)
+        for h in range(HEADS):
+            both = tile[2 * (h % 4) : 2 * (h % 4) + 2]
+            here = core == h // 4
+            placed = jnp.where(lane == h, jnp.where(here, both[:, 0:1], NEG), placed)
+            for m in (1, 2):
+                placed = jnp.where(lane == m * HEADS + h, jnp.where(here, both[:, m : m + 1], 0.0), placed)
+        fresh_stats.append(placed)
     mixes, tops, totals = combine(
-        [values(n) for n in range(SIDE)] + [fresh],
-        [got[n, 16:18, :] for n in range(SIDE)] + [stats],
-        False,
+        [old(n) for n in range(QUAD)] + [fresh(n) for n in range(QUAD)],
+        old_stats + fresh_stats,
+        True,
     )
     keep_stats = stat_tile(tops, totals)
     send_stats = stat_tile(tops, totals, True)
@@ -425,23 +525,6 @@
     return lax.ppermute(x, "seq", [(n, n ^ 1) for n in range(2 * SIDE * SIDE)])
 
 
-def along_queries(x, by):
-    pairs = []
-    for group in QUERY_GROUPS:
-        pairs += [(group[n], group[(n + by) % SIDE]) for n in range(SIDE)]
-    return lax.ppermute(x, "seq", pairs)
-
-
-def ring(block):
-    ahead, back = [block], [block]
-    for _ in range(SIDE // 2 - 1):
-        ahead.append(along_queries(ahead[-1], 1))
-        back.append(along_queries(back[-1], -1))
-    front = along_queries(ahead[-1][:FRONT], 1)
-    rest = along_queries(back[-1][FRONT:], -1)
-    return ahead + [front, rest] + back[:0:-1]
-
-
 def body(q_pre, k_pre, v_pre, old_k, old_v, src_page, page_row, page_len, q_dec, dec_k, dec_v):
     seq, grp = lax.axis_index("seq"), lax.axis_index("grp")
     core = seq & 1
@@ -487,41 +570,42 @@
             pltpu.VMEM((BLK, HEAD), F32),
         ),
     )
-    chunk, dec_send = call(
+    near, keep_dec = call(
         merge_kernel,
-        [((CHUNK, 128), BF16), ((SIDE, 18, 128), F32)],
+        [((PAIR_ALL, 128), BF16), ((72, 128), F32)],
         (exchange(kv_send, KEY_GROUPS),),
     )
-    reduced = exchange(dec_send, QUERY_GROUPS)
-    q_last = lax.dynamic_slice(
-        q_dec,
-        (seq // STEPS, seq % STEPS // 2 * 2, (grp * HEADS + core * 4) * HEAD),
-        (1, 2, 4 * HEAD),
-    )
-    q_last = jnp.pad(q_last.reshape(HEADS, HEAD), ((0, FRESH - HEADS), (0, 0)))
+    other = lax.ppermute(near, "seq", NEIGHBOURS)
+    (q_send,) = call(
+        queries_kernel, [((QUAD, Q_MSG, 128), BF16)], (q_blk, near, other, keep_dec)
+    )
+    qs = exchange(q_send, QUADS)
     work = QROWS * SIDE * KEYS
-    attn, fresh_o, fresh_s = call(
+    side = (
+        pltpu.VMEM((QROWS, TWO), BF16),
+        pltpu.VMEM((TWO, KEYS), BF16),
+        pltpu.VMEM((TWO, KEYS), BF16),
+        pltpu.VMEM((QROWS, KEYS), F32),
+        pltpu.VMEM((QROWS, KEYS), F32),
+    )
+    (o_send,) = call(
         attend_kernel,
-        [((QROWS, HEAD), BF16), ((FRESH, 128), F32), ((FRESH, 128), F32)],
-        (q_blk, q_last, *ring(chunk)),
+        [((QUAD, O_MSG, 128), BF16)],
+        (qs, near, other, q_mine),
         scratch=(
-            pltpu.VMEM((KEYS, TWO), BF16),
-            pltpu.VMEM((KEYS, TWO), BF16),
+            pltpu.VMEM((2 * KEYS, TWO), BF16),
             pltpu.VMEM((BLK, BLK), F32),
-            pltpu.VMEM((QROWS, TWO), BF16),
-            pltpu.VMEM((TWO, KEYS), BF16),
-            pltpu.VMEM((TWO, KEYS), BF16),
-            pltpu.VMEM((QROWS, KEYS), F32),
-            pltpu.VMEM((QROWS, KEYS), F32),
-            pltpu.VMEM((QROWS, TWO), F32),
-            pltpu.VMEM((QROWS, 128), F32),
+            pltpu.VMEM((FRESH, HEAD), BF16),
+            *side,
+            *side,
         ),
         cost=pl.CostEstimate(flops=work * 512, bytes_accessed=4 * 1024 * 1024, transcendentals=work),
     )
     attn_keep, dec_keep, last = call(
         pair_kernel,
         [((4 * TOK, 128), BF16), ((16, 128), F32), ((LAST_MSG, 128), BF16)],
-        (reduced, attn, fresh_o, fresh_s),
+        (exchange(o_send, QUADS), qs),
+        scratch=(pltpu.VMEM((QROWS, HEAD), BF16),),
     )
     attn_out, dec_out = call(
         final_kernel,

time: 127 us -> 116 us (0.913)
  blocking collectives: 19.5 us -> 54.9 us
  starting transfers between devices: 61.6 us -> 30.1 us
  waiting for transfers between devices: 18.1 us -> 11.3 us
  local copies, waits for them, and re-layouts: 7.75 us -> 3.62 us
  Pallas kernels: 17.4 us -> 14.4 us
    all_to_all x1 -> x3, blocking collectives: 19.5 us -> 54.9 us  [exchange(): return lax.all_to_all(x, 'seq', 0, 0, axis_index_groups=groups, tiled=True)]
    ppermute x8 -> x1, starting transfers between devices: 31.7 us -> 4 us  [body(): other = lax.ppermute(near, 'seq', NEIGHBOURS)]
    ppermute x8 -> x1, waiting for transfers between devices: 14.6 us -> 7.11 us  [body(): other = lax.ppermute(near, 'seq', NEIGHBOURS)]
    all_to_all x1 -> x0, starting transfers between devices: 3.55 us -> none  [exchange(): return lax.all_to_all(x, 'seq', 0, 0, axis_index_groups=groups, tiled=True)]
    pallas_call x7 -> x8, Pallas kernels: 17.4 us -> 14.4 us  [call(): pl.pallas_call(kernel, out_shape=[jax.ShapeDtypeStruct(s, t) for s, t in...]
    slice x2 -> x0, local copies, waits for them, and re-layouts: 1.45 us -> none  [the longest x1 0.74 us: ring(): front = along_queries(ahead[-1][:FRONT], 1)]
    unnamed x20 -> x18, local copies, waits for them, and re-layouts: 3.67 us -> 2.72 us
  transfers between devices with their start and end apart: 14 -> 6, of which waited for: 6 -> 5; matrix products, arithmetic and copies ran while one was open for 3% -> 1% of each run, Pallas kernels for 8% -> 0%
where the time goes in v3:
time: 116 us; the launch traced here: 115 us
  blocking collectives  54.9 us (47%)
  starting transfers between devices  30.1 us (26%)
  Pallas kernels  14.4 us (12%)
  waiting for transfers between devices  11.3 us (10%)
  local copies, waits for them, and re-layouts  3.62 us (3%)
    all_to_all x3, blocking collectives, exchange(): return lax.all_to_all(x, 'seq', 0, 0, axis_index_groups=groups, tiled=True)  54.9 us
    ppermute x2, starting transfers between devices, to_other_core(): return lax.ppermute(x, 'seq', [(n, n ^ 1) for n in range(2 * SIDE * SIDE)])  14.6 us
    pallas_call x8, Pallas kernels, call(): pl.pallas_call(kernel, out_shape=[jax.ShapeDtypeStruct(s, t) for s, t in...  14.4 us
    ppermute x3, starting transfers between devices, body(): lax.ppermute(xs[d], 'grp', [(n, (n + d) % NG) for n in range(NG)])  11.5 us
    ppermute x1, waiting for transfers between devices, body(): other = lax.ppermute(near, 'seq', NEIGHBOURS)  7.11 us
    ppermute x1, starting transfers between devices, body(): other = lax.ppermute(near, 'seq', NEIGHBOURS)  4 us
    unnamed x18, local copies, waits for them, and re-layouts  2.72 us
    ppermute x3, waiting for transfers between devices, body(): lax.ppermute(xs[d], 'grp', [(n, (n + d) % NG) for n in range(NG)])  2.59 us
  transfers between devices with their start and end apart: 6, of which 5 were waited for; matrix products, arithmetic and copies ran while one was open for 1% of the time, Pallas kernels for 0%

profile of v3, /device:TPU:1, one launch (start us, length us, event | category | flops | bytes accessed | tf_op | source)
XLA Modules:
  0.0 115.2 jit_solution(850325813398892866)
XLA Ops:
  0.7 0.7 copy-done.6
  1.4 1.0 copy-done.1
  2.4 1.0 copy-done.2
  3.4 0.7 pages.1
  4.1 4.1 %collective-permute-start = (bf16[336,256]{1,0:T(8,128)(2,1)S(1)}, bf16[336,256]{1,0:T(8,128)(2,1)S(1)}, u32[]{:S(2)}, u32[]{:S(2)}) collective-permute-start(bf16[336,256]{1,0:T(8,128)(2,1)S(1)} %get-tuple-element.16), channel_id=1, source_target_pairs={{0,1},{1,2},{2,3},{3,0},{4,5},{5,6},{6,7},{7,4},{8,9},{9,10},{10,1... | collective-permute-start | bytes 516104 | tf_op jit(solution)/shard_map/ppermute | solution.py:546
  8.2 4.4 %collective-permute-start.1 = (bf16[336,256]{1,0:T(8,128)(2,1)S(1)}, bf16[336,256]{1,0:T(8,128)(2,1)S(1)}, u32[]{:S(2)}, u32[]{:S(2)}) collective-permute-start(bf16[336,256]{1,0:T(8,128)(2,1)S(1)} %get-tuple-element.17), channel_id=1, source_target_pairs={{0,2},{1,3},{2,0},{3,1},{4,6},{5,7},{6,4},{7,5},{8,10},{9,11},{10,... | collective-permute-start | bytes 516104 | tf_op jit(solution)/shard_map/ppermute | solution.py:546
  12.5 3.1 %collective-permute-start.2 = (bf16[336,256]{1,0:T(8,128)(2,1)S(1)}, bf16[336,256]{1,0:T(8,128)(2,1)S(1)}, u32[]{:S(2)}, u32[]{:S(2)}) collective-permute-start(bf16[336,256]{1,0:T(8,128)(2,1)S(1)} %get-tuple-element.18), channel_id=1, source_target_pairs={{0,3},{1,0},{2,1},{3,2},{4,7},{5,4},{6,5},{7,6},{8,11},{9,8},{10,9... | collective-permute-start | bytes 516104 | tf_op jit(solution)/shard_map/ppermute | solution.py:546
  15.6 0.7 dynamic-slice_bitcast_fusion
  16.4 0.7 collective-permute-done.1.x2
  17.1 1.9 %collective-permute-done.2.x3 = bf16[336,256]{1,0:T(8,128)(2,1)S(1)} collective-permute-done((bf16[336,256]{1,0:T(8,128)(2,1)S(1)}, bf16[336,256]{1,0:T(8,128)(2,1)S(1)}, u32[]{:S(2)}, u32[]{:S(2)}) %collective-permute-start.2) | collective-permute-done | bytes 172064 | tf_op jit(solution)/shard_map/ppermute | solution.py:546
  19.3 7.2 %collective-permute-start.3 = (bf16[400,128]{1,0:T(8,128)(2,1)S(1)}, bf16[400,128]{1,0:T(8,128)(2,1)S(1)}, u32[]{:S(2)}, u32[]{:S(2)}) collective-permute-start(bf16[400,128]{1,0:T(8,128)(2,1)S(1)} %get-tuple-element.20), channel_id=1, source_target_pairs={{0,4},{4,0},{8,12},{12,8},{16,20},{20,16},{24,28},{28,24},{32,36},... | collective-permute-start | bytes 307208 | tf_op jit(solution)/shard_map/ppermute | solution.py:525
  26.7 0.7 collective-permute-done.3.got
  27.5 4.1 %local.1 = (bf16[8,416,128]{2,1,0:T(8,128)(2,1)S(1)}, bf16[512,128]{1,0:T(8,128)(2,1)S(1)}) custom-call(bf16[400,128]{1,0:T(8,128)(2,1)S(1)} %get-tuple-element.19.keep, bf16[400,128]{1,0:T(8,128)(2,1)S(1)} %collective-permute-done.3.got, bf16[128,1024]{1,0:T(8,128)(2,1)S(1)} %reshape.15.q.q_dec, bf16[336,256]{1,0:T(8,128)(2,1)S(1)} %get-tuple-element.15.x0, ...), custom_call_target="tpu_custom_call" | custom-call | tf_op jit(solution)/shard_map/local/pallas_call | solution.py:90
  31.5 19.2 %all_to_all.15.got = bf16[8,416,128]{2,1,0:T(8,128)(2,1)S(1)} all-to-all(bf16[8,416,128]{2,1,0:T(8,128)(2,1)S(1)} %get-tuple-element.22), channel_id=1, replica_groups={{0,64,128,192,256,320,384,448},{8,72,136,200,264,328,392,456},{16,80,14..., dimensions={0} | all-to-all | bytes 1703936 | tf_op jit(solution)/shard_map/all_to_all | solution.py:521
  50.7 0.3 merge.1
  51.0 4.0 %collective-permute-start.4 = (bf16[2144,128]{1,0:T(8,128)(2,1)S(1)}, bf16[2144,128]{1,0:T(8,128)(2,1)S(1)}, u32[]{:S(2)}, u32[]{:S(2)}) collective-permute-start(bf16[2144,128]{1,0:T(8,128)(2,1)S(1)} %get-tuple-element.23.near), channel_id=1, source_target_pairs={{0,8},{8,0},{16,24},{24,16},{32,40},{40,32},{48,56},{56,48},{64,72... | collective-permute-start | bytes 1646600 | tf_op jit(solution)/shard_map/ppermute | solution.py:578
  55.0 7.1 %collective-permute-done.4.other = bf16[2144,128]{1,0:T(8,128)(2,1)S(1)} collective-permute-done((bf16[2144,128]{1,0:T(8,128)(2,1)S(1)}, bf16[2144,128]{1,0:T(8,128)(2,1)S(1)}, u32[]{:S(2)}, u32[]{:S(2)}) %collective-permute-start.4) | collective-permute-done | bytes 548896 | tf_op jit(solution)/shard_map/ppermute | solution.py:578
  62.3 21.7 %all_to_all.16.qs = bf16[4,560,128]{2,1,0:T(8,128)(2,1)S(1)} all-to-all(bf16[4,560,128]{2,1,0:T(8,128)(2,1)S(1)} %queries.1), channel_id=1, replica_groups={{0,16,32,48},{8,24,40,56},{64,80,96,112},{72,88,104,120},{128,144,160,1..., dimensions={0} | all-to-all | bytes 1146880 | tf_op jit(solution)/shard_map/all_to_all | solution.py:521
  84.0 7.2 %attend.1 = bf16[4,544,128]{2,1,0:T(8,128)(2,1)S(1)} custom-call(bf16[4,560,128]{2,1,0:T(8,128)(2,1)S(1)} %all_to_all.16.qs, bf16[2144,128]{1,0:T(8,128)(2,1)S(1)} %get-tuple-element.23.near, bf16[2144,128]{1,0:T(8,128)(2,1)S(1)} %collective-permute-done.4.other, bf16[128,1024]{1,0:T(8,128)(2,1)S(1)} %reshape.15.q.q_dec), custom_call_target="tpu_custom_call" | custom-call | flops 2147483648 | bytes 4194304 | tf_op jit(solution)/shard_map/attend/pallas_call | solution.py:90
  91.3 14.0 %all_to_all.17.got = bf16[4,544,128]{2,1,0:T(8,128)(2,1)S(1)} all-to-all(bf16[4,544,128]{2,1,0:T(8,128)(2,1)S(1)} %attend.1), channel_id=1, replica_groups={{0,16,32,48},{8,24,40,56},{64,80,96,112},{72,88,104,120},{128,144,160,1..., dimensions={0} | all-to-all | bytes 1114112 | tf_op jit(solution)/shard_map/all_to_all | solution.py:521
  105.3 0.9 pair.1
  106.2 7.3 %collective-permute-start.5 = (bf16[272,128]{1,0:T(8,128)(2,1)S(1)}, bf16[272,128]{1,0:T(8,128)(2,1)S(1)}, u32[]{:S(2)}, u32[]{:S(2)}) collective-permute-start(bf16[272,128]{1,0:T(8,128)(2,1)S(1)} %get-tuple-element.27), channel_id=1, source_target_pairs={{0,4},{4,0},{8,12},{12,8},{16,20},{20,16},{24,28},{28,24},{32,36},... | collective-permute-start | bytes 208904 | tf_op jit(solution)/shard_map/ppermute | solution.py:525
  113.5 0.9 collective-permute-done.5.got
  114.4 0.8 final.1
  (22 shorter events, 0.7 us)
Async XLA Ops:
  0.6 25.9 %copy-start = (bf16[32,4,4096]{2,1,0:T(4,128)(2,1)S(1)}, bf16[32,4,4096]{2,1,0:T(4,128)(2,1)}, u32[]{:S(2)}) copy-start(bf16[32,4,4096]{2,1,0:T(4,128)(2,1)} %param.19) | copy-start | bytes 3145732
  0.6 0.7 copy-start.6
  0.7 0.7 copy-start.7
  0.7 0.8 copy-start.8
  1.4 1.0 copy-start.1
  2.4 1.0 copy-start.2
  4.1 14.9 %copy-start.3 = (bf16[64,1024]{1,0:T(8,128)(2,1)S(1)}, bf16[64,1024]{1,0:T(8,128)(2,1)}, u32[]{:S(2)}) copy-start(bf16[64,1024]{1,0:T(8,128)(2,1)} %q.1) | copy-start | bytes 393220
  4.1 12.3 %collective-permute-start = (bf16[336,256]{1,0:T(8,128)(2,1)S(1)}, bf16[336,256]{1,0:T(8,128)(2,1)S(1)}, u32[]{:S(2)}, u32[]{:S(2)}) collective-permute-start(bf16[336,256]{1,0:T(8,128)(2,1)S(1)} %get-tuple-element.16), channel_id=1, source_target_pairs={{0,1},{1,2},{2,3},{3,0},{4,5},{5,6},{6,7},{7,4},{8,9},{9,10},{10,1... | collective-permute-start | bytes 516104 | tf_op jit(solution)/shard_map/ppermute | solution.py:546
  8.2 8.9 %collective-permute-start.1 = (bf16[336,256]{1,0:T(8,128)(2,1)S(1)}, bf16[336,256]{1,0:T(8,128)(2,1)S(1)}, u32[]{:S(2)}, u32[]{:S(2)}) collective-permute-start(bf16[336,256]{1,0:T(8,128)(2,1)S(1)} %get-tuple-element.17), channel_id=1, source_target_pairs={{0,2},{1,3},{2,0},{3,1},{4,6},{5,7},{6,4},{7,5},{8,10},{9,11},{10,... | collective-permute-start | bytes 516104 | tf_op jit(solution)/shard_map/ppermute | solution.py:546
  12.5 6.4 %collective-permute-start.2 = (bf16[336,256]{1,0:T(8,128)(2,1)S(1)}, bf16[336,256]{1,0:T(8,128)(2,1)S(1)}, u32[]{:S(2)}, u32[]{:S(2)}) collective-permute-start(bf16[336,256]{1,0:T(8,128)(2,1)S(1)} %get-tuple-element.18), channel_id=1, source_target_pairs={{0,3},{1,0},{2,1},{3,2},{4,7},{5,4},{6,5},{7,6},{8,11},{9,8},{10,9... | collective-permute-start | bytes 516104 | tf_op jit(solution)/shard_map/ppermute | solution.py:546
  16.4 2.6 %copy-start.4 = (bf16[64,256]{1,0:T(8,128)(2,1)S(1)}, bf16[64,256]{1,0:T(8,128)(2,1)}, u32[]{:S(2)}) copy-start(bf16[64,256]{1,0:T(8,128)(2,1)} %k.1) | copy-start | bytes 98308
  16.4 2.6 %copy-start.5 = (bf16[64,256]{1,0:T(8,128)(2,1)S(1)}, bf16[64,256]{1,0:T(8,128)(2,1)}, u32[]{:S(2)}) copy-start(bf16[64,256]{1,0:T(8,128)(2,1)} %v.1) | copy-start | bytes 98308
  19.3 8.2 %collective-permute-start.3 = (bf16[400,128]{1,0:T(8,128)(2,1)S(1)}, bf16[400,128]{1,0:T(8,128)(2,1)S(1)}, u32[]{:S(2)}, u32[]{:S(2)}) collective-permute-start(bf16[400,128]{1,0:T(8,128)(2,1)S(1)} %get-tuple-element.20), channel_id=1, source_target_pairs={{0,4},{4,0},{8,12},{12,8},{16,20},{20,16},{24,28},{28,24},{32,36},... | collective-permute-start | bytes 307208 | tf_op jit(solution)/shard_map/ppermute | solution.py:525
  51.0 11.1 %collective-permute-start.4 = (bf16[2144,128]{1,0:T(8,128)(2,1)S(1)}, bf16[2144,128]{1,0:T(8,128)(2,1)S(1)}, u32[]{:S(2)}, u32[]{:S(2)}) collective-permute-start(bf16[2144,128]{1,0:T(8,128)(2,1)S(1)} %get-tuple-element.23.near), channel_id=1, source_target_pairs={{0,8},{8,0},{16,24},{24,16},{32,40},{40,32},{48,56},{56,48},{64,72... | collective-permute-start | bytes 1646600 | tf_op jit(solution)/shard_map/ppermute | solution.py:578
  106.2 8.2 %collective-permute-start.5 = (bf16[272,128]{1,0:T(8,128)(2,1)S(1)}, bf16[272,128]{1,0:T(8,128)(2,1)S(1)}, u32[]{:S(2)}, u32[]{:S(2)}) collective-permute-start(bf16[272,128]{1,0:T(8,128)(2,1)S(1)} %get-tuple-element.27), channel_id=1, source_target_pairs={{0,4},{4,0},{8,12},{12,8},{16,20},{20,16},{24,28},{28,24},{32,36},... | collective-permute-start | bytes 208904 | tf_op jit(solution)/shard_map/ppermute | solution.py:525

commit v4 on v3

--- a/solution.py
+++ b/solution.py
@@ -37,13 +37,12 @@
 DEC_MSG = HEADS * PER + PER
 KV_DEC = 2 * BLK + META
 KV_MSG = KV_DEC + DEC_MSG
-FRONT = META + KEYS
-CHUNK = FRONT + KEYS
+CHUNK = 2 * KEYS
 PAGES = KEYS // PAGE
 LAST_MSG = 4 * TOK + 16
 QUAD = 4
 PAIR_DEC = 80
-PAIR_ALL = CHUNK + PAIR_DEC
+PAIR_SMALL = META + PAIR_DEC
 Q_META = QROWS
 Q_DEC = QROWS + META
 Q_MSG = Q_DEC + 32
@@ -236,9 +235,9 @@
         for c, (chunk, _) in enumerate(chunks):
             for m in range(SIDE):
                 cols = slice(m * BLK, (m + 1) * BLK)
-                side[1 + c][:HEAD, cols] = chunk[META + m * BLK : META + (m + 1) * BLK, :]
+                side[1 + c][:HEAD, cols] = chunk[m * BLK : (m + 1) * BLK, :]
     for c, (chunk, _) in enumerate(chunks):
-        vs[c * KEYS : (c + 1) * KEYS, :HEAD] = chunk[FRONT:CHUNK, :]
+        vs[c * KEYS : (c + 1) * KEYS, :HEAD] = chunk[KEYS:, :]
     vs[:, HEAD:] = jnp.where(iota((2 * KEYS, HEAD), 1) == 0, 1.0, 0.0).astype(BF16)
 
     def score(j, qx, kx_a, kx_b, s_a, s_b):
@@ -389,11 +388,11 @@
     return tile
 
 
-def merge_kernel(got, send, keep):
+def merge_kernel(got, chunk, send, keep):
     send[:META, :] = sum(got[n, 2 * BLK : KV_DEC, :].astype(F32) for n in range(SIDE)).astype(BF16)
     for n in range(SIDE):
-        send[META + n * BLK : META + (n + 1) * BLK, :] = got[n, :BLK, :]
-        send[FRONT + n * BLK : FRONT + (n + 1) * BLK, :] = got[n, BLK : 2 * BLK, :]
+        chunk[n * BLK : (n + 1) * BLK, :] = got[n, :BLK, :]
+        chunk[KEYS + n * BLK : KEYS + (n + 1) * BLK, :] = got[n, BLK : 2 * BLK, :]
 
     def values(n):
         return lambda h: got[n, KV_DEC + h * PER : KV_DEC + (h + 1) * PER, :].astype(F32)
@@ -418,22 +417,22 @@
     mine, other = halves(stat_tile(tops, totals, True))
     keep[64:, :] = mine
     theirs += [other, jnp.zeros((8, 128), F32)]
-    send[CHUNK:, :] = jnp.concatenate(theirs, axis=0).astype(BF16)
-
-
-def queries_kernel(q_blk, near, other, keep, send):
+    send[META:, :] = jnp.concatenate(theirs, axis=0).astype(BF16)
+
+
+def queries_kernel(q_blk, mine, other, keep, send):
     def kept(h):
         return keep[8 * h : 8 * h + 8, :]
 
     def came(h):
-        return other[CHUNK + 8 * h : CHUNK + 8 * h + 8, :].astype(F32)
+        return other[META + 8 * h : META + 8 * h + 8, :].astype(F32)
 
     mixes, tops, totals = combine(
-        [kept, came], [keep[64:, :], other[CHUNK + 64 : CHUNK + 72, :].astype(F32)], True
+        [kept, came], [keep[64:, :], other[META + 64 : META + 72, :].astype(F32)], True
     )
     pieces = mixes + [stat_tile(tops, totals, True)]
     numbers = jnp.concatenate(
-        [near[:META, :].astype(F32)[:4], other[:META, :].astype(F32)[:4], jnp.zeros((8, 128), F32)], 0
+        [mine[:META, :].astype(F32)[:4], other[:META, :].astype(F32)[:4], jnp.zeros((8, 128), F32)], 0
     ).astype(BF16)
     for n in range(QUAD):
         send[n, :QROWS, :] = q_blk[...]
@@ -541,6 +540,7 @@
             pltpu.SemaphoreType.DMA((3 + 2 * NG,)),
         ),
         specs={n: far for n in range(5)},
+        limit=60,
     )
     xs = [xs[0]] + [
         lax.ppermute(xs[d], "grp", [(n, (n + d) % NG) for n in range(NG)]) for d in range(1, NG)
@@ -570,14 +570,16 @@
             pltpu.VMEM((BLK, HEAD), F32),
         ),
     )
-    near, keep_dec = call(
+    near, small, keep_dec = call(
         merge_kernel,
-        [((PAIR_ALL, 128), BF16), ((72, 128), F32)],
+        [((CHUNK, 128), BF16), ((PAIR_SMALL, 128), BF16), ((72, 128), F32)],
         (exchange(kv_send, KEY_GROUPS),),
     )
+    small_other = lax.ppermute(small, "seq", NEIGHBOURS)
+    near, small_other = lax.optimization_barrier((near, small_other))
     other = lax.ppermute(near, "seq", NEIGHBOURS)
     (q_send,) = call(
-        queries_kernel, [((QUAD, Q_MSG, 128), BF16)], (q_blk, near, other, keep_dec)
+        queries_kernel, [((QUAD, Q_MSG, 128), BF16)], (q_blk, small, small_other, keep_dec)
     )
     qs = exchange(q_send, QUADS)
     work = QROWS * SIDE * KEYS

time: 116 us -> 115 us (level)
  blocking collectives: 54.9 us -> 37 us
  starting transfers between devices: 30.1 us -> 42 us
  waiting for transfers between devices: 11.3 us -> 17 us
  local copies, waits for them, and re-layouts: 3.62 us -> 0.93 us
  Pallas kernels: 14.4 us -> 16.7 us
    all_to_all x3 -> x2, blocking collectives: 54.9 us -> 37 us  [exchange(): return lax.all_to_all(x, 'seq', 0, 0, axis_index_groups=groups, tiled=True)]
    all_to_all x0 -> x1, starting transfers between devices: none -> 9.38 us  [exchange(): return lax.all_to_all(x, 'seq', 0, 0, axis_index_groups=groups, tiled=True)]
    ppermute x1, waiting for transfers between devices: 7.11 us -> 11.4 us  [body(): other = lax.ppermute(near, 'seq', NEIGHBOURS)]
    ppermute x0 -> x1, starting transfers between devices: none -> 4 us  [body(): small_other = lax.ppermute(small, 'seq', NEIGHBOURS)]
    unnamed x18 -> x10, local copies, waits for them, and re-layouts: 2.72 us -> 0.03 us
    pallas_call x8, Pallas kernels: 14.4 us -> 16.7 us  [call(): pl.pallas_call(kernel, out_shape=[jax.ShapeDtypeStruct(s, t) for s, t in...]
    ppermute x0 -> x1, waiting for transfers between devices: none -> 1.2 us  [body(): small_other = lax.ppermute(small, 'seq', NEIGHBOURS)]
  transfers between devices with their start and end apart: 6 -> 8, of which waited for: 5 -> 6; matrix products, arithmetic and copies ran while one was open for 1% -> 1% of each run, Pallas kernels for 0% -> 0%
where the time goes in v4:
time: 115 us
  starting transfers between devices  42 us (37%)
  blocking collectives  37 us (32%)
  waiting for transfers between devices  17 us (15%)
  Pallas kernels  16.7 us (15%)
    all_to_all x2, blocking collectives, exchange(): return lax.all_to_all(x, 'seq', 0, 0, axis_index_groups=groups, tiled=True)  37 us
    pallas_call x8, Pallas kernels, call(): pl.pallas_call(kernel, out_shape=[jax.ShapeDtypeStruct(s, t) for s, t in...  16.7 us
    ppermute x2, starting transfers between devices, to_other_core(): return lax.ppermute(x, 'seq', [(n, n ^ 1) for n in range(2 * SIDE * SIDE)])  14.1 us
    ppermute x3, starting transfers between devices, body(): lax.ppermute(xs[d], 'grp', [(n, (n + d) % NG) for n in range(NG)])  11.5 us
    ppermute x1, waiting for transfers between devices, body(): other = lax.ppermute(near, 'seq', NEIGHBOURS)  11.4 us
    all_to_all x1, starting transfers between devices, exchange(): return lax.all_to_all(x, 'seq', 0, 0, axis_index_groups=groups, tiled=True)  9.38 us
    ppermute x1, starting transfers between devices, body(): small_other = lax.ppermute(small, 'seq', NEIGHBOURS)  4 us
    ppermute x1, starting transfers between devices, body(): other = lax.ppermute(near, 'seq', NEIGHBOURS)  3.09 us
  transfers between devices with their start and end apart: 8, of which 6 were waited for; matrix products, arithmetic and copies ran while one was open for 1% of the time, Pallas kernels for 0%

profile of v4, /device:TPU:1, one launch (start us, length us, event | category | flops | bytes accessed | tf_op | source)
XLA Modules:
  0.0 114.5 jit_solution(415126452279022255)
XLA Ops:
  0.7 2.2 %pages.1 = (bf16[336,256]{1,0:T(8,128)(2,1)}, bf16[336,256]{1,0:T(8,128)(2,1)}, bf16[336,256]{1,0:T(8,128)(2,1)}, bf16[336,256]{1,0:T(8,128)(2,1)}) custom-call(bf16[160,1024]{1,0:T(8,128)(2,1)} %bitcast.6, bf16[160,1024]{1,0:T(8,128)(2,1)} %bitcast.7, s32[1,8]{1,0:T(1,128)} %src_page.1, s32[1,12]{1,0:T(1,128)} %page_row.1, s32[1,12]{1,0:T(1,128)} %page_len.1), custom_call_target="tpu_custom_call" | custom-call | tf_op jit(solution)/shard_map/pages/pallas_call | solution.py:89
  2.9 4.1 %collective-permute-start = (bf16[336,256]{1,0:T(8,128)(2,1)}, bf16[336,256]{1,0:T(8,128)(2,1)S(1)}, u32[]{:S(2)}, u32[]{:S(2)}) collective-permute-start(bf16[336,256]{1,0:T(8,128)(2,1)} %get-tuple-element.19), channel_id=1, source_target_pairs={{0,1},{1,2},{2,3},{3,0},{4,5},{5,6},{6,7},{7,4},{8,9},{9,10},{10,1... | collective-permute-start | bytes 516104 | tf_op jit(solution)/shard_map/ppermute | solution.py:546
  7.0 4.4 %collective-permute-start.1 = (bf16[336,256]{1,0:T(8,128)(2,1)}, bf16[336,256]{1,0:T(8,128)(2,1)S(1)}, u32[]{:S(2)}, u32[]{:S(2)}) collective-permute-start(bf16[336,256]{1,0:T(8,128)(2,1)} %get-tuple-element.20), channel_id=1, source_target_pairs={{0,2},{1,3},{2,0},{3,1},{4,6},{5,7},{6,4},{7,5},{8,10},{9,11},{10,... | collective-permute-start | bytes 516104 | tf_op jit(solution)/shard_map/ppermute | solution.py:546
  11.4 3.1 %collective-permute-start.2 = (bf16[336,256]{1,0:T(8,128)(2,1)}, bf16[336,256]{1,0:T(8,128)(2,1)S(1)}, u32[]{:S(2)}, u32[]{:S(2)}) collective-permute-start(bf16[336,256]{1,0:T(8,128)(2,1)} %get-tuple-element.21), channel_id=1, source_target_pairs={{0,3},{1,0},{2,1},{3,2},{4,7},{5,4},{6,5},{7,6},{8,11},{9,8},{10,9... | collective-permute-start | bytes 516104 | tf_op jit(solution)/shard_map/ppermute | solution.py:546
  14.5 0.7 dynamic-slice_bitcast_fusion
  15.2 0.9 collective-permute-done.1.x2
  16.1 1.9 %collective-permute-done.2.x3 = bf16[336,256]{1,0:T(8,128)(2,1)S(1)} collective-permute-done((bf16[336,256]{1,0:T(8,128)(2,1)}, bf16[336,256]{1,0:T(8,128)(2,1)S(1)}, u32[]{:S(2)}, u32[]{:S(2)}) %collective-permute-start.2) | collective-permute-done | bytes 172064 | tf_op jit(solution)/shard_map/ppermute | solution.py:546
  18.3 7.2 %collective-permute-start.3 = (bf16[400,128]{1,0:T(8,128)(2,1)S(1)}, bf16[400,128]{1,0:T(8,128)(2,1)S(1)}, u32[]{:S(2)}, u32[]{:S(2)}) collective-permute-start(bf16[400,128]{1,0:T(8,128)(2,1)S(1)} %get-tuple-element.23), channel_id=1, source_target_pairs={{0,4},{4,0},{8,12},{12,8},{16,20},{20,16},{24,28},{28,24},{32,36},... | collective-permute-start | bytes 307208 | tf_op jit(solution)/shard_map/ppermute | solution.py:524
  25.8 0.7 collective-permute-done.3.got
  26.5 4.1 %local.1 = (bf16[8,416,128]{2,1,0:T(8,128)(2,1)S(1)}, bf16[512,128]{1,0:T(8,128)(2,1)S(1)}) custom-call(bf16[400,128]{1,0:T(8,128)(2,1)S(1)} %get-tuple-element.22.keep, bf16[400,128]{1,0:T(8,128)(2,1)S(1)} %collective-permute-done.3.got, bf16[128,1024]{1,0:T(8,128)(2,1)S(1)} %reshape.15.q.q_dec, bf16[336,256]{1,0:T(8,128)(2,1)S(1)} %copy-done.1, ...), custom_call_target="tpu_custom_call" | custom-call | tf_op jit(solution)/shard_map/local/pallas_call | solution.py:89
  30.6 19.2 %all_to_all.15.got = bf16[8,416,128]{2,1,0:T(8,128)(2,1)S(1)} all-to-all(bf16[8,416,128]{2,1,0:T(8,128)(2,1)S(1)} %get-tuple-element.25), channel_id=1, replica_groups={{0,64,128,192,256,320,384,448},{8,72,136,200,264,328,392,456},{16,80,14..., dimensions={0} | all-to-all | bytes 1703936 | tf_op jit(solution)/shard_map/all_to_all | solution.py:520
  49.8 0.3 merge.1
  50.1 4.0 %collective-permute-start.4 = (bf16[96,128]{1,0:T(8,128)(2,1)S(1)}, bf16[96,128]{1,0:T(8,128)(2,1)S(1)}, u32[]{:S(2)}, u32[]{:S(2)}) collective-permute-start(bf16[96,128]{1,0:T(8,128)(2,1)S(1)} %get-tuple-element.26.mine), channel_id=1, source_target_pairs={{0,8},{8,0},{16,24},{24,16},{32,40},{40,32},{48,56},{56,48},{64,72... | collective-permute-start | bytes 73736 | tf_op jit(solution)/shard_map/ppermute | solution.py:578
  54.1 1.2 %collective-permute-done.4.other = bf16[96,128]{1,0:T(8,128)(2,1)S(1)} collective-permute-done((bf16[96,128]{1,0:T(8,128)(2,1)S(1)}, bf16[96,128]{1,0:T(8,128)(2,1)S(1)}, u32[]{:S(2)}, u32[]{:S(2)}) %collective-permute-start.4) | collective-permute-done | bytes 24608 | tf_op jit(solution)/shard_map/ppermute | solution.py:578
  55.3 1.0 queries.1
  56.3 9.4 %all-to-all-start.1 = ((bf16[4,560,128]{2,1,0:T(8,128)(2,1)}), bf16[4,560,128]{2,1,0:T(8,128)(2,1)S(1)}, u32[]{:S(2)}, u32[]{:S(2)}) async-start(bf16[4,560,128]{2,1,0:T(8,128)(2,1)} %queries.1), calls=%async_computation.1 | async-start | bytes 1146880 | tf_op jit(solution)/shard_map/all_to_all | solution.py:520
  65.7 3.1 %collective-permute-start.5 = (bf16[2048,128]{1,0:T(8,128)(2,1)S(1)}, bf16[2048,128]{1,0:T(8,128)(2,1)S(1)}, u32[]{:S(2)}, u32[]{:S(2)}) collective-permute-start(bf16[2048,128]{1,0:T(8,128)(2,1)S(1)} %get-tuple-element.30.near), channel_id=1, source_target_pairs={{0,8},{8,0},{16,24},{24,16},{32,40},{40,32},{48,56},{56,48},{64,72... | collective-permute-start | bytes 1572872 | tf_op jit(solution)/shard_map/ppermute | solution.py:580
  68.8 11.4 %collective-permute-done.5.other = bf16[2048,128]{1,0:T(8,128)(2,1)S(1)} collective-permute-done((bf16[2048,128]{1,0:T(8,128)(2,1)S(1)}, bf16[2048,128]{1,0:T(8,128)(2,1)S(1)}, u32[]{:S(2)}, u32[]{:S(2)}) %collective-permute-start.5) | collective-permute-done | bytes 524320 | tf_op jit(solution)/shard_map/ppermute | solution.py:580
  80.1 7.2 %attend.1 = bf16[4,544,128]{2,1,0:T(8,128)(2,1)S(1)} custom-call(bf16[4,560,128]{2,1,0:T(8,128)(2,1)S(1)} %all-to-all-done.1.qs, bf16[2048,128]{1,0:T(8,128)(2,1)S(1)} %get-tuple-element.30.near, bf16[2048,128]{1,0:T(8,128)(2,1)S(1)} %collective-permute-done.5.other, bf16[128,1024]{1,0:T(8,128)(2,1)S(1)} %reshape.15.q.q_dec), custom_call_target="tpu_custom_call" | custom-call | flops 2147483648 | bytes 4194304 | tf_op jit(solution)/shard_map/attend/pallas_call | solution.py:89
  87.3 17.8 %all_to_all.16.got = bf16[4,544,128]{2,1,0:T(8,128)(2,1)S(1)} all-to-all(bf16[4,544,128]{2,1,0:T(8,128)(2,1)S(1)} %attend.1), channel_id=1, replica_groups={{0,16,32,48},{8,24,40,56},{64,80,96,112},{72,88,104,120},{128,144,160,1..., dimensions={0} | all-to-all | bytes 1114112 | tf_op jit(solution)/shard_map/all_to_all | solution.py:520
  105.2 0.9 pair.1
  106.0 6.8 %collective-permute-start.6 = (bf16[272,128]{1,0:T(8,128)(2,1)S(1)}, bf16[272,128]{1,0:T(8,128)(2,1)S(1)}, u32[]{:S(2)}, u32[]{:S(2)}) collective-permute-start(bf16[272,128]{1,0:T(8,128)(2,1)S(1)} %get-tuple-element.33), channel_id=1, source_target_pairs={{0,4},{4,0},{8,12},{12,8},{16,20},{20,16},{24,28},{28,24},{32,36},... | collective-permute-start | bytes 208904 | tf_op jit(solution)/shard_map/ppermute | solution.py:524
  112.9 0.9 collective-permute-done.6.got
  113.8 0.8 final.1
  (17 shorter events, 0.5 us)
Async XLA Ops:
  0.6 25.0 %copy-start = (bf16[32,4,4096]{2,1,0:T(4,128)(2,1)S(1)}, bf16[32,4,4096]{2,1,0:T(4,128)(2,1)}, u32[]{:S(2)}) copy-start(bf16[32,4,4096]{2,1,0:T(4,128)(2,1)} %param.19) | copy-start | bytes 3145732
  0.6 17.4 %copy-start.2 = (bf16[64,1024]{1,0:T(8,128)(2,1)S(1)}, bf16[64,1024]{1,0:T(8,128)(2,1)}, u32[]{:S(2)}) copy-start(bf16[64,1024]{1,0:T(8,128)(2,1)} %q.1) | copy-start | bytes 393220
  0.7 17.4 %copy-start.4 = (bf16[64,256]{1,0:T(8,128)(2,1)S(1)}, bf16[64,256]{1,0:T(8,128)(2,1)}, u32[]{:S(2)}) copy-start(bf16[64,256]{1,0:T(8,128)(2,1)} %v.1) | copy-start | bytes 98308
  2.9 15.1 %copy-start.1 = (bf16[336,256]{1,0:T(8,128)(2,1)S(1)}, bf16[336,256]{1,0:T(8,128)(2,1)}, u32[]{:S(2)}) copy-start(bf16[336,256]{1,0:T(8,128)(2,1)} %get-tuple-element.18.x0) | copy-start | bytes 516100
  2.9 12.3 %collective-permute-start = (bf16[336,256]{1,0:T(8,128)(2,1)}, bf16[336,256]{1,0:T(8,128)(2,1)S(1)}, u32[]{:S(2)}, u32[]{:S(2)}) collective-permute-start(bf16[336,256]{1,0:T(8,128)(2,1)} %get-tuple-element.19), channel_id=1, source_target_pairs={{0,1},{1,2},{2,3},{3,0},{4,5},{5,6},{6,7},{7,4},{8,9},{9,10},{10,1... | collective-permute-start | bytes 516104 | tf_op jit(solution)/shard_map/ppermute | solution.py:546
  7.0 9.1 %collective-permute-start.1 = (bf16[336,256]{1,0:T(8,128)(2,1)}, bf16[336,256]{1,0:T(8,128)(2,1)S(1)}, u32[]{:S(2)}, u32[]{:S(2)}) collective-permute-start(bf16[336,256]{1,0:T(8,128)(2,1)} %get-tuple-element.20), channel_id=1, source_target_pairs={{0,2},{1,3},{2,0},{3,1},{4,6},{5,7},{6,4},{7,5},{8,10},{9,11},{10,... | collective-permute-start | bytes 516104 | tf_op jit(solution)/shard_map/ppermute | solution.py:546
  11.4 6.7 %collective-permute-start.2 = (bf16[336,256]{1,0:T(8,128)(2,1)}, bf16[336,256]{1,0:T(8,128)(2,1)S(1)}, u32[]{:S(2)}, u32[]{:S(2)}) collective-permute-start(bf16[336,256]{1,0:T(8,128)(2,1)} %get-tuple-element.21), channel_id=1, source_target_pairs={{0,3},{1,0},{2,1},{3,2},{4,7},{5,4},{6,5},{7,6},{8,11},{9,8},{10,9... | collective-permute-start | bytes 516104 | tf_op jit(solution)/shard_map/ppermute | solution.py:546
  15.2 2.9 %copy-start.3 = (bf16[64,256]{1,0:T(8,128)(2,1)S(1)}, bf16[64,256]{1,0:T(8,128)(2,1)}, u32[]{:S(2)}) copy-start(bf16[64,256]{1,0:T(8,128)(2,1)} %k.1) | copy-start | bytes 98308
  18.3 8.2 %collective-permute-start.3 = (bf16[400,128]{1,0:T(8,128)(2,1)S(1)}, bf16[400,128]{1,0:T(8,128)(2,1)S(1)}, u32[]{:S(2)}, u32[]{:S(2)}) collective-permute-start(bf16[400,128]{1,0:T(8,128)(2,1)S(1)} %get-tuple-element.23), channel_id=1, source_target_pairs={{0,4},{4,0},{8,12},{12,8},{16,20},{20,16},{24,28},{28,24},{32,36},... | collective-permute-start | bytes 307208 | tf_op jit(solution)/shard_map/ppermute | solution.py:524
  50.1 5.2 %collective-permute-start.4 = (bf16[96,128]{1,0:T(8,128)(2,1)S(1)}, bf16[96,128]{1,0:T(8,128)(2,1)S(1)}, u32[]{:S(2)}, u32[]{:S(2)}) collective-permute-start(bf16[96,128]{1,0:T(8,128)(2,1)S(1)} %get-tuple-element.26.mine), channel_id=1, source_target_pairs={{0,8},{8,0},{16,24},{24,16},{32,40},{40,32},{48,56},{56,48},{64,72... | collective-permute-start | bytes 73736 | tf_op jit(solution)/shard_map/ppermute | solution.py:578
  56.3 23.8 %all-to-all-start.1 = ((bf16[4,560,128]{2,1,0:T(8,128)(2,1)}), bf16[4,560,128]{2,1,0:T(8,128)(2,1)S(1)}, u32[]{:S(2)}, u32[]{:S(2)}) async-start(bf16[4,560,128]{2,1,0:T(8,128)(2,1)} %queries.1), calls=%async_computation.1 | async-start | bytes 1146880 | tf_op jit(solution)/shard_map/all_to_all | solution.py:520
  65.7 14.5 %collective-permute-start.5 = (bf16[2048,128]{1,0:T(8,128)(2,1)S(1)}, bf16[2048,128]{1,0:T(8,128)(2,1)S(1)}, u32[]{:S(2)}, u32[]{:S(2)}) collective-permute-start(bf16[2048,128]{1,0:T(8,128)(2,1)S(1)} %get-tuple-element.30.near), channel_id=1, source_target_pairs={{0,8},{8,0},{16,24},{24,16},{32,40},{40,32},{48,56},{56,48},{64,72... | collective-permute-start | bytes 1572872 | tf_op jit(solution)/shard_map/ppermute | solution.py:580
  106.0 7.7 %collective-permute-start.6 = (bf16[272,128]{1,0:T(8,128)(2,1)S(1)}, bf16[272,128]{1,0:T(8,128)(2,1)S(1)}, u32[]{:S(2)}, u32[]{:S(2)}) collective-permute-start(bf16[272,128]{1,0:T(8,128)(2,1)S(1)} %get-tuple-element.33), channel_id=1, source_target_pairs={{0,4},{4,0},{8,12},{12,8},{16,20},{20,16},{24,28},{28,24},{32,36},... | collective-permute-start | bytes 208904 | tf_op jit(solution)/shard_map/ppermute | solution.py:524

commit v5 on v4

--- a/solution.py
+++ b/solution.py
@@ -37,7 +37,6 @@
 DEC_MSG = HEADS * PER + PER
 KV_DEC = 2 * BLK + META
 KV_MSG = KV_DEC + DEC_MSG
-CHUNK = 2 * KEYS
 PAGES = KEYS // PAGE
 LAST_MSG = 4 * TOK + 16
 QUAD = 4
@@ -102,14 +101,13 @@
 SMEM = pl.BlockSpec(memory_space=pltpu.SMEM)
 
 
-def pages_kernel(old_k, old_v, src_page, page_row, page_len, *rest):
-    outs, (src_s, row_s, len_s, sems) = rest[:NG], rest[NG:]
+def pages_kernel(old_k, old_v, src_page, page_row, page_len, out, src_s, row_s, len_s, sems):
     grp = spot()[1]
     pairs = [(src_page, src_s), (page_row, row_s), (page_len, len_s)]
     for d in range(NG):
-        cols = pl.ds(aligned(((grp + d) % NG) * TWO, TWO), TWO)
-        pairs.append((old_k.at[:, cols], outs[d].at[pl.ds(0, HALF), :]))
-        pairs.append((old_v.at[:, cols], outs[d].at[pl.ds(HALF, HALF), :]))
+        cols = pl.ds(d * TWO, TWO)
+        pairs.append((old_k.at[:, cols], out.at[d, pl.ds(0, HALF), :]))
+        pairs.append((old_v.at[:, cols], out.at[d, pl.ds(HALF, HALF), :]))
     copies = [pltpu.make_async_copy(a, b, sems.at[n]) for n, (a, b) in enumerate(pairs)]
     for copy in copies:
         copy.start()
@@ -126,12 +124,12 @@
         tile = jnp.where((sub == 8) & (lane == n), row_s[0, n].astype(F32), tile)
         tile = jnp.where((sub == 9) & (lane == n), len_s[0, n].astype(F32), tile)
     for d in range(NG):
-        outs[d][2 * HALF :, :] = tile.astype(BF16)
+        out[d, 2 * HALF :, :] = tile.astype(BF16)
     for copy in copies[3:]:
         copy.wait()
 
 
-def split_kernel(q, k, v, x0, x1, x2, x3, keep, send, sems):
+def split_kernel(q, k, v, xs, keep, send, sems):
     _, _, _, _, core, w, u = spot()
     pairs = []
     for dst, head in ((keep, core), (send, 1 - core)):
@@ -147,15 +145,15 @@
     fresh = (iota((META, 128), 0) < 4) & (iota((META, 128), 1) < NEWP)
     for dst, at in ((keep, w), (send, u)):
         tile = jnp.zeros((META, 128), F32)
-        for d, x in enumerate((x0, x1, x2, x3)):
-            part = jnp.where(fresh, x[2 * HALF :, :HEAD].astype(F32), 0.0)
+        for d in range(NG):
+            part = jnp.where(fresh, xs[d, 2 * HALF :, :HEAD].astype(F32), 0.0)
             tile = tile + pltpu.roll(part, at * 16 + core * 8 + d * NEWP, 1)
         dst[6 * TOK :, :] = tile.astype(BF16)
     for copy in copies:
         copy.wait()
 
 
-def local_kernel(keep, got, q, x0, x1, x2, x3, k_dec, v_dec, kv_send, q_blk, ks, vs, cs, kb):
+def local_kernel(keep, got, q, xs, k_dec, v_dec, kv_send, q_blk, ks, vs, cs, kb):
     seq, _, _, _, core, _, _ = spot()
     for src, start in ((keep, core * TOK), (got, (1 - core) * TOK)):
         kb[pl.ds(aligned(start, TOK), TOK), :] = src[:TOK, :].astype(F32)
@@ -170,10 +168,9 @@
     for n in range(1, SIDE):
         kv_send[n, :KV_DEC, :] = kv_send[0, :KV_DEC, :]
 
-    parts = (x0, x1, x2, x3)
-    for n, part in enumerate(parts):
-        ks[n * HALF : (n + 1) * HALF, :] = part[:HALF, :]
-        vs[n * HALF : (n + 1) * HALF, :] = part[HALF : 2 * HALF, :]
+    for n in range(NG):
+        ks[n * HALF : (n + 1) * HALF, :] = xs[n, :HALF, :]
+        vs[n * HALF : (n + 1) * HALF, :] = xs[n, HALF : 2 * HALF, :]
     ks[OLD_TOK:, :] = k_dec[...]
     vs[OLD_TOK:, :] = v_dec[...]
 
@@ -189,8 +186,8 @@
     at = (token & 15).astype(F32)
     page = (token >> 4) - iota((OLD_TOK, 128), 1)
     count = 0.0
-    for n, part in enumerate(parts):
-        numbers = part[2 * HALF :, :HEAD].astype(F32)
+    for n in range(NG):
+        numbers = xs[n, 2 * HALF :, :HEAD].astype(F32)
         owner, length = numbers[8:9, :], numbers[9:10, :]
         inside = (page == n * OLD) & (at < length)
         count = count + lax.dot_general(
@@ -220,12 +217,12 @@
     kv_send[:, KV_DEC + HEADS * PER :, :] = stats.astype(BF16).reshape(SIDE, PER, 128)
 
 
-def attend_kernel(qs, near, other, q_dec, out, *refs):
+def attend_kernel(qs, keys, keys_other, vals, vals_other, q_dec, out, *refs):
     vs, tri, sel = refs[:3]
     sides = (refs[3:8], refs[8:13])
     seq, _, z, y, core, w, u = spot()
     even = core == 0
-    chunks = ((near, u), (other, u ^ 1))
+    chunks = ((keys, u), (keys_other, u ^ 1))
     row, col = iota((BLK, BLK), 0), iota((BLK, BLK), 1)
     tri[...] = jnp.where(col > row, HIDE, 0.0)
     same = jnp.where(row == col, 1.0, 0.0).astype(BF16)
@@ -236,8 +233,8 @@
             for m in range(SIDE):
                 cols = slice(m * BLK, (m + 1) * BLK)
                 side[1 + c][:HEAD, cols] = chunk[m * BLK : (m + 1) * BLK, :]
-    for c, (chunk, _) in enumerate(chunks):
-        vs[c * KEYS : (c + 1) * KEYS, :HEAD] = chunk[KEYS:, :]
+    vs[:KEYS, :HEAD] = vals[...]
+    vs[KEYS:, :HEAD] = vals_other[...]
     vs[:, HEAD:] = jnp.where(iota((2 * KEYS, HEAD), 1) == 0, 1.0, 0.0).astype(BF16)
 
     def score(j, qx, kx_a, kx_b, s_a, s_b):
@@ -333,8 +330,8 @@
             one = jnp.sum(count[j * PAGE : (j + 1) * PAGE], axis=0, keepdims=True)
             terms = jnp.where(which == j, one, terms)
         terms = jnp.concatenate([terms] * 4, axis=0)
-        keys = sides[0][1 + c][:HEAD, :]
-        scores = EXP2_SCALE * jnp.dot(sel[...], keys, preferred_element_type=F32)
+        held = sides[0][1 + c][:HEAD, :]
+        scores = EXP2_SCALE * jnp.dot(sel[...], held, preferred_element_type=F32)
         all_scores.append(jnp.where(terms > 0.5, scores, NEG))
         all_terms.append(terms)
     top = jnp.max(jnp.maximum(*all_scores), axis=1, keepdims=True).astype(BF16).astype(F32)
@@ -388,11 +385,11 @@
     return tile
 
 
-def merge_kernel(got, chunk, send, keep):
+def merge_kernel(got, keys, vals, send, keep):
     send[:META, :] = sum(got[n, 2 * BLK : KV_DEC, :].astype(F32) for n in range(SIDE)).astype(BF16)
     for n in range(SIDE):
-        chunk[n * BLK : (n + 1) * BLK, :] = got[n, :BLK, :]
-        chunk[KEYS + n * BLK : KEYS + (n + 1) * BLK, :] = got[n, BLK : 2 * BLK, :]
+        keys[n * BLK : (n + 1) * BLK, :] = got[n, :BLK, :]
+        vals[n * BLK : (n + 1) * BLK, :] = got[n, BLK : 2 * BLK, :]
 
     def values(n):
         return lambda h: got[n, KV_DEC + h * PER : KV_DEC + (h + 1) * PER, :].astype(F32)
@@ -529,9 +526,9 @@
     core = seq & 1
     far = pl.BlockSpec(memory_space=pltpu.HBM)
     counts = page_row.shape[1]
-    xs = call(
+    (x_send,) = call(
         pages_kernel,
-        [((X_MSG, TWO), BF16)] * NG,
+        [((NG, X_MSG, TWO), BF16)],
         (old_k.reshape(HALF, -1), old_v.reshape(HALF, -1), src_page, page_row, page_len),
         scratch=(
             pltpu.SMEM(src_page.shape, jnp.int32),
@@ -542,13 +539,11 @@
         specs={n: far for n in range(5)},
         limit=60,
     )
-    xs = [xs[0]] + [
-        lax.ppermute(xs[d], "grp", [(n, (n + d) % NG) for n in range(NG)]) for d in range(1, NG)
-    ]
+    xs = lax.all_to_all(x_send, "grp", 0, 0, tiled=True)
     keep, send = call(
         split_kernel,
         [((PAIR_MSG, 128), BF16)] * 2,
-        (q_pre, k_pre, v_pre, *xs),
+        (q_pre, k_pre, v_pre, xs),
         scratch=(pltpu.SemaphoreType.DMA((12,)),),
         specs={n: far for n in range(3)},
     )
@@ -562,7 +557,7 @@
     kv_send, q_blk = call(
         local_kernel,
         [((SIDE, KV_MSG, 128), BF16), ((QROWS, 128), BF16)],
-        (keep, to_other_core(send), q_mine, *xs, own_tokens(dec_k), own_tokens(dec_v)),
+        (keep, to_other_core(send), q_mine, xs, own_tokens(dec_k), own_tokens(dec_v)),
         scratch=(
             pltpu.VMEM((DEC_TOK, TWO), BF16),
             pltpu.VMEM((DEC_TOK, TWO), BF16),
@@ -570,16 +565,19 @@
             pltpu.VMEM((BLK, HEAD), F32),
         ),
     )
-    near, small, keep_dec = call(
+    keys, vals, small, keep_dec = call(
         merge_kernel,
-        [((CHUNK, 128), BF16), ((PAIR_SMALL, 128), BF16), ((72, 128), F32)],
+        [((KEYS, 128), BF16), ((KEYS, 128), BF16), ((PAIR_SMALL, 128), BF16), ((72, 128), F32)],
         (exchange(kv_send, KEY_GROUPS),),
     )
     small_other = lax.ppermute(small, "seq", NEIGHBOURS)
-    near, small_other = lax.optimization_barrier((near, small_other))
-    other = lax.ppermute(near, "seq", NEIGHBOURS)
+    keys, vals, small_other = lax.optimization_barrier((keys, vals, small_other))
+    keys_other = lax.ppermute(keys, "seq", NEIGHBOURS)
+    vals_other = lax.ppermute(vals, "seq", NEIGHBOURS)
     (q_send,) = call(
-        queries_kernel, [((QUAD, Q_MSG, 128), BF16)], (q_blk, small, small_other, keep_dec)
+        queries_kernel,
+        [((QUAD, Q_MSG, 128), BF16)],
+        (q_blk, small, small_other, keep_dec),
     )
     qs = exchange(q_send, QUADS)
     work = QROWS * SIDE * KEYS
@@ -593,7 +591,7 @@
     (o_send,) = call(
         attend_kernel,
         [((QUAD, O_MSG, 128), BF16)],
-        (qs, near, other, q_mine),
+        (qs, keys, keys_other, vals, vals_other, q_mine),
         scratch=(
             pltpu.VMEM((2 * KEYS, TWO), BF16),
             pltpu.VMEM((BLK, BLK), F32),

time: 115 us -> 115 us (level)
  starting transfers between devices: 42 us -> 38.9 us
  waiting for transfers between devices: 17 us -> 19 us
    ppermute x4 -> x2, starting transfers between devices: 14.6 us -> 5.27 us  [the longest x1 3.08 us: body(): keys_other = lax.ppermute(keys, 'seq', NEIGHBOURS)]
    all_to_all x0 -> x1, waiting for transfers between devices: none -> 7.02 us  [body(): xs = lax.all_to_all(x_send, 'grp', 0, 0, tiled=True)]
    ppermute x4 -> x2, waiting for transfers between devices: 14.2 us -> 9.16 us  [the longest x1 6.35 us: body(): keys_other = lax.ppermute(keys, 'seq', NEIGHBOURS)]
    all_to_all x0 -> x1, starting transfers between devices: none -> 4.85 us  [body(): xs = lax.all_to_all(x_send, 'grp', 0, 0, tiled=True)]
    ppermute x2, starting transfers between devices: 14.1 us -> 15.4 us  [to_other_core(): return lax.ppermute(x, 'seq', [(n, n ^ 1) for n in range(2 * SIDE * SIDE)])]
  transfers between devices with their start and end apart: 8 -> 7, of which waited for: 6 -> 6; matrix products, arithmetic and copies ran while one was open for 1% -> 1% of each run, Pallas kernels for 0% -> 0%
where the time goes in v5:
time: 115 us; the launch traced here: 114 us
  starting transfers between devices  38.9 us (34%)
  blocking collectives  37.8 us (33%)
  waiting for transfers between devices  19 us (17%)
  Pallas kernels  16.7 us (15%)
    all_to_all x2, blocking collectives, exchange(): return lax.all_to_all(x, 'seq', 0, 0, axis_index_groups=groups, tiled=True)  37.8 us
    pallas_call x8, Pallas kernels, call(): pl.pallas_call(kernel, out_shape=[jax.ShapeDtypeStruct(s, t) for s, t in...  16.7 us
    ppermute x2, starting transfers between devices, to_other_core(): return lax.ppermute(x, 'seq', [(n, n ^ 1) for n in range(2 * SIDE * SIDE)])  15.4 us
    all_to_all x1, starting transfers between devices, exchange(): return lax.all_to_all(x, 'seq', 0, 0, axis_index_groups=groups, tiled=True)  9.38 us
    all_to_all x1, waiting for transfers between devices, body(): xs = lax.all_to_all(x_send, 'grp', 0, 0, tiled=True)  7.02 us
    ppermute x1, waiting for transfers between devices, body(): keys_other = lax.ppermute(keys, 'seq', NEIGHBOURS)  6.35 us
    all_to_all x1, starting transfers between devices, body(): xs = lax.all_to_all(x_send, 'grp', 0, 0, tiled=True)  4.85 us
    ppermute x1, starting transfers between devices, body(): small_other = lax.ppermute(small, 'seq', NEIGHBOURS)  4.01 us
  transfers between devices with their start and end apart: 7, of which 6 were waited for; matrix products, arithmetic and copies ran while one was open for 1% of the time, Pallas kernels for 0%

profile of v5, /device:TPU:1, one launch (start us, length us, event | category | flops | bytes accessed | tf_op | source)
XLA Modules:
  0.0 114.2 jit_solution(18128417771112496502)
XLA Ops:
  0.6 2.2 %pages.1 = bf16[4,336,256]{2,1,0:T(8,128)(2,1)} custom-call(bf16[160,1024]{1,0:T(8,128)(2,1)} %bitcast.6, bf16[160,1024]{1,0:T(8,128)(2,1)} %bitcast.7, s32[1,8]{1,0:T(1,128)} %src_page.1, s32[1,12]{1,0:T(1,128)} %page_row.1, s32[1,12]{1,0:T(1,128)} %page_len.1), custom_call_target="tpu_custom_call" | custom-call | tf_op jit(solution)/shard_map/pages/pallas_call | solution.py:88
  2.9 4.9 %all-to-all-start = ((bf16[4,336,256]{2,1,0:T(8,128)(2,1)}), bf16[4,336,256]{2,1,0:T(8,128)(2,1)S(1)}, u32[]{:S(2)}, u32[]{:S(2)}) async-start(bf16[4,336,256]{2,1,0:T(8,128)(2,1)} %pages.1), calls=%async_computation | async-start | bytes 1376256 | tf_op jit(solution)/shard_map/all_to_all | solution.py:542
  7.7 0.7 dynamic-slice_bitcast_fusion
  8.5 7.0 %all-to-all-done.xs = bf16[4,336,256]{2,1,0:T(8,128)(2,1)S(1)} async-done(((bf16[4,336,256]{2,1,0:T(8,128)(2,1)}), bf16[4,336,256]{2,1,0:T(8,128)(2,1)S(1)}, u32[]{:S(2)}, u32[]{:S(2)}) %all-to-all-start) | async-done | bytes 688160 | tf_op jit(solution)/shard_map/all_to_all | solution.py:542
  15.6 0.3 split.1
  15.9 8.6 %collective-permute-start = (bf16[400,128]{1,0:T(8,128)(2,1)S(1)}, bf16[400,128]{1,0:T(8,128)(2,1)S(1)}, u32[]{:S(2)}, u32[]{:S(2)}) collective-permute-start(bf16[400,128]{1,0:T(8,128)(2,1)S(1)} %get-tuple-element.17), channel_id=1, source_target_pairs={{0,4},{4,0},{8,12},{12,8},{16,20},{20,16},{24,28},{28,24},{32,36},... | collective-permute-start | bytes 307208 | tf_op jit(solution)/shard_map/ppermute | solution.py:521
  24.6 0.7 collective-permute-done.got
  25.3 4.1 %local.1 = (bf16[8,416,128]{2,1,0:T(8,128)(2,1)S(1)}, bf16[512,128]{1,0:T(8,128)(2,1)S(1)}) custom-call(bf16[400,128]{1,0:T(8,128)(2,1)S(1)} %get-tuple-element.16.keep, bf16[400,128]{1,0:T(8,128)(2,1)S(1)} %collective-permute-done.got, bf16[128,1024]{1,0:T(8,128)(2,1)S(1)} %reshape.15.q.q_dec, bf16[4,336,256]{2,1,0:T(8,128)(2,1)S(1)} %all-to-all-done.xs, ...), custom_call_target="tpu_custom_call" | custom-call | tf_op jit(solution)/shard_map/local/pallas_call | solution.py:88
  29.4 20.0 %all_to_all.20.got = bf16[8,416,128]{2,1,0:T(8,128)(2,1)S(1)} all-to-all(bf16[8,416,128]{2,1,0:T(8,128)(2,1)S(1)} %get-tuple-element.19), channel_id=1, replica_groups={{0,64,128,192,256,320,384,448},{8,72,136,200,264,328,392,456},{16,80,14..., dimensions={0} | all-to-all | bytes 1703936 | tf_op jit(solution)/shard_map/all_to_all | solution.py:517
  49.4 0.3 merge.1
  49.7 4.0 %collective-permute-start.1 = (bf16[96,128]{1,0:T(8,128)(2,1)S(1)}, bf16[96,128]{1,0:T(8,128)(2,1)S(1)}, u32[]{:S(2)}, u32[]{:S(2)}) collective-permute-start(bf16[96,128]{1,0:T(8,128)(2,1)S(1)} %get-tuple-element.20.mine), channel_id=1, source_target_pairs={{0,8},{8,0},{16,24},{24,16},{32,40},{40,32},{48,56},{56,48},{64,72... | collective-permute-start | bytes 73736 | tf_op jit(solution)/shard_map/ppermute | solution.py:573
  53.7 1.2 %collective-permute-done.1.other = bf16[96,128]{1,0:T(8,128)(2,1)S(1)} collective-permute-done((bf16[96,128]{1,0:T(8,128)(2,1)S(1)}, bf16[96,128]{1,0:T(8,128)(2,1)S(1)}, u32[]{:S(2)}, u32[]{:S(2)}) %collective-permute-start.1) | collective-permute-done | bytes 24608 | tf_op jit(solution)/shard_map/ppermute | solution.py:573
  54.9 1.0 queries.1
  55.9 9.4 %all-to-all-start.2 = ((bf16[4,560,128]{2,1,0:T(8,128)(2,1)}), bf16[4,560,128]{2,1,0:T(8,128)(2,1)S(1)}, u32[]{:S(2)}, u32[]{:S(2)}) async-start(bf16[4,560,128]{2,1,0:T(8,128)(2,1)} %queries.1), calls=%async_computation.2 | async-start | bytes 1146880 | tf_op jit(solution)/shard_map/all_to_all | solution.py:517
  65.3 3.1 %collective-permute-start.2 = (bf16[1024,128]{1,0:T(8,128)(2,1)S(1)}, bf16[1024,128]{1,0:T(8,128)(2,1)S(1)}, u32[]{:S(2)}, u32[]{:S(2)}) collective-permute-start(bf16[1024,128]{1,0:T(8,128)(2,1)S(1)} %get-tuple-element.25.keys), channel_id=1, source_target_pairs={{0,8},{8,0},{16,24},{24,16},{32,40},{40,32},{48,56},{56,48},{64,72... | collective-permute-start | bytes 786440 | tf_op jit(solution)/shard_map/ppermute | solution.py:575
  68.4 2.2 %collective-permute-start.3 = (bf16[1024,128]{1,0:T(8,128)(2,1)S(1)}, bf16[1024,128]{1,0:T(8,128)(2,1)S(1)}, u32[]{:S(2)}, u32[]{:S(2)}) collective-permute-start(bf16[1024,128]{1,0:T(8,128)(2,1)S(1)} %get-tuple-element.26.vals), channel_id=1, source_target_pairs={{0,8},{8,0},{16,24},{24,16},{32,40},{40,32},{48,56},{56,48},{64,72... | collective-permute-start | bytes 786440 | tf_op jit(solution)/shard_map/ppermute | solution.py:576
  70.6 6.4 %collective-permute-done.2.keys_other = bf16[1024,128]{1,0:T(8,128)(2,1)S(1)} collective-permute-done((bf16[1024,128]{1,0:T(8,128)(2,1)S(1)}, bf16[1024,128]{1,0:T(8,128)(2,1)S(1)}, u32[]{:S(2)}, u32[]{:S(2)}) %collective-permute-start.2) | collective-permute-done | bytes 262176 | tf_op jit(solution)/shard_map/ppermute | solution.py:575
  76.9 2.8 %collective-permute-done.3.vals_other = bf16[1024,128]{1,0:T(8,128)(2,1)S(1)} collective-permute-done((bf16[1024,128]{1,0:T(8,128)(2,1)S(1)}, bf16[1024,128]{1,0:T(8,128)(2,1)S(1)}, u32[]{:S(2)}, u32[]{:S(2)}) %collective-permute-start.3) | collective-permute-done | bytes 262176 | tf_op jit(solution)/shard_map/ppermute | solution.py:576
  79.7 7.2 %attend.1 = bf16[4,544,128]{2,1,0:T(8,128)(2,1)S(1)} custom-call(bf16[4,560,128]{2,1,0:T(8,128)(2,1)S(1)} %all-to-all-done.2.qs, bf16[1024,128]{1,0:T(8,128)(2,1)S(1)} %get-tuple-element.25.keys, bf16[1024,128]{1,0:T(8,128)(2,1)S(1)} %collective-permute-done.2.keys_other, bf16[1024,128]{1,0:T(8,128)(2,1)S(1)} %get-tuple-element.26.vals, ...), custom_call_target="tpu_custom_call" | custom-call | flops 2147483648 | bytes 4194304 | tf_op jit(solution)/shard_map/attend/pallas_call | solution.py:88
  87.0 17.8 %all_to_all.21.got = bf16[4,544,128]{2,1,0:T(8,128)(2,1)S(1)} all-to-all(bf16[4,544,128]{2,1,0:T(8,128)(2,1)S(1)} %attend.1), channel_id=1, replica_groups={{0,16,32,48},{8,24,40,56},{64,80,96,112},{72,88,104,120},{128,144,160,1..., dimensions={0} | all-to-all | bytes 1114112 | tf_op jit(solution)/shard_map/all_to_all | solution.py:517
  104.8 0.9 pair.1
  105.7 6.8 %collective-permute-start.4 = (bf16[272,128]{1,0:T(8,128)(2,1)S(1)}, bf16[272,128]{1,0:T(8,128)(2,1)S(1)}, u32[]{:S(2)}, u32[]{:S(2)}) collective-permute-start(bf16[272,128]{1,0:T(8,128)(2,1)S(1)} %get-tuple-element.29), channel_id=1, source_target_pairs={{0,4},{4,0},{8,12},{12,8},{16,20},{20,16},{24,28},{28,24},{32,36},... | collective-permute-start | bytes 208904 | tf_op jit(solution)/shard_map/ppermute | solution.py:521
  112.5 0.9 collective-permute-done.4.got
  113.4 0.8 final.1
  (13 shorter events, 0.2 us)
Async XLA Ops:
  0.6 23.8 %copy-start = (bf16[32,4,4096]{2,1,0:T(4,128)(2,1)S(1)}, bf16[32,4,4096]{2,1,0:T(4,128)(2,1)}, u32[]{:S(2)}) copy-start(bf16[32,4,4096]{2,1,0:T(4,128)(2,1)} %param.19) | copy-start | bytes 3145732
  2.9 12.7 %all-to-all-start = ((bf16[4,336,256]{2,1,0:T(8,128)(2,1)}), bf16[4,336,256]{2,1,0:T(8,128)(2,1)S(1)}, u32[]{:S(2)}, u32[]{:S(2)}) async-start(bf16[4,336,256]{2,1,0:T(8,128)(2,1)} %pages.1), calls=%async_computation | async-start | bytes 1376256 | tf_op jit(solution)/shard_map/all_to_all | solution.py:542
  7.7 7.8 %copy-start.1 = (bf16[64,1024]{1,0:T(8,128)(2,1)S(1)}, bf16[64,1024]{1,0:T(8,128)(2,1)}, u32[]{:S(2)}) copy-start(bf16[64,1024]{1,0:T(8,128)(2,1)} %q.1) | copy-start | bytes 393220
  8.5 7.1 %copy-start.2 = (bf16[64,256]{1,0:T(8,128)(2,1)S(1)}, bf16[64,256]{1,0:T(8,128)(2,1)}, u32[]{:S(2)}) copy-start(bf16[64,256]{1,0:T(8,128)(2,1)} %k.1) | copy-start | bytes 98308
  8.5 7.1 %copy-start.3 = (bf16[64,256]{1,0:T(8,128)(2,1)S(1)}, bf16[64,256]{1,0:T(8,128)(2,1)}, u32[]{:S(2)}) copy-start(bf16[64,256]{1,0:T(8,128)(2,1)} %v.1) | copy-start | bytes 98308
  15.9 9.5 %collective-permute-start = (bf16[400,128]{1,0:T(8,128)(2,1)S(1)}, bf16[400,128]{1,0:T(8,128)(2,1)S(1)}, u32[]{:S(2)}, u32[]{:S(2)}) collective-permute-start(bf16[400,128]{1,0:T(8,128)(2,1)S(1)} %get-tuple-element.17), channel_id=1, source_target_pairs={{0,4},{4,0},{8,12},{12,8},{16,20},{20,16},{24,28},{28,24},{32,36},... | collective-permute-start | bytes 307208 | tf_op jit(solution)/shard_map/ppermute | solution.py:521
  49.7 5.2 %collective-permute-start.1 = (bf16[96,128]{1,0:T(8,128)(2,1)S(1)}, bf16[96,128]{1,0:T(8,128)(2,1)S(1)}, u32[]{:S(2)}, u32[]{:S(2)}) collective-permute-start(bf16[96,128]{1,0:T(8,128)(2,1)S(1)} %get-tuple-element.20.mine), channel_id=1, source_target_pairs={{0,8},{8,0},{16,24},{24,16},{32,40},{40,32},{48,56},{56,48},{64,72... | collective-permute-start | bytes 73736 | tf_op jit(solution)/shard_map/ppermute | solution.py:573
  55.9 23.8 %all-to-all-start.2 = ((bf16[4,560,128]{2,1,0:T(8,128)(2,1)}), bf16[4,560,128]{2,1,0:T(8,128)(2,1)S(1)}, u32[]{:S(2)}, u32[]{:S(2)}) async-start(bf16[4,560,128]{2,1,0:T(8,128)(2,1)} %queries.1), calls=%async_computation.2 | async-start | bytes 1146880 | tf_op jit(solution)/shard_map/all_to_all | solution.py:517
  65.3 11.6 %collective-permute-start.2 = (bf16[1024,128]{1,0:T(8,128)(2,1)S(1)}, bf16[1024,128]{1,0:T(8,128)(2,1)S(1)}, u32[]{:S(2)}, u32[]{:S(2)}) collective-permute-start(bf16[1024,128]{1,0:T(8,128)(2,1)S(1)} %get-tuple-element.25.keys), channel_id=1, source_target_pairs={{0,8},{8,0},{16,24},{24,16},{32,40},{40,32},{48,56},{56,48},{64,72... | collective-permute-start | bytes 786440 | tf_op jit(solution)/shard_map/ppermute | solution.py:575
  68.4 11.4 %collective-permute-start.3 = (bf16[1024,128]{1,0:T(8,128)(2,1)S(1)}, bf16[1024,128]{1,0:T(8,128)(2,1)S(1)}, u32[]{:S(2)}, u32[]{:S(2)}) collective-permute-start(bf16[1024,128]{1,0:T(8,128)(2,1)S(1)} %get-tuple-element.26.vals), channel_id=1, source_target_pairs={{0,8},{8,0},{16,24},{24,16},{32,40},{40,32},{48,56},{56,48},{64,72... | collective-permute-start | bytes 786440 | tf_op jit(solution)/shard_map/ppermute | solution.py:576
  105.7 7.7 %collective-permute-start.4 = (bf16[272,128]{1,0:T(8,128)(2,1)S(1)}, bf16[272,128]{1,0:T(8,128)(2,1)S(1)}, u32[]{:S(2)}, u32[]{:S(2)}) collective-permute-start(bf16[272,128]{1,0:T(8,128)(2,1)S(1)} %get-tuple-element.29), channel_id=1, source_target_pairs={{0,4},{4,0},{8,12},{12,8},{16,20},{20,16},{24,28},{28,24},{32,36},... | collective-permute-start | bytes 208904 | tf_op jit(solution)/shard_map/ppermute | solution.py:521

commit v6 on v5

--- a/solution.py
+++ b/solution.py
@@ -101,7 +101,7 @@
 SMEM = pl.BlockSpec(memory_space=pltpu.SMEM)
 
 
-def pages_kernel(old_k, old_v, src_page, page_row, page_len, out, src_s, row_s, len_s, sems):
+def pages_kernel(old_k, old_v, src_page, page_row, page_len, out, src_s, row_s, len_s, tiles, sems):
     grp = spot()[1]
     pairs = [(src_page, src_s), (page_row, row_s), (page_len, len_s)]
     for d in range(NG):
@@ -123,9 +123,14 @@
     for n in range(OLD):
         tile = jnp.where((sub == 8) & (lane == n), row_s[0, n].astype(F32), tile)
         tile = jnp.where((sub == 9) & (lane == n), len_s[0, n].astype(F32), tile)
-    for d in range(NG):
-        out[d, 2 * HALF :, :] = tile.astype(BF16)
-    for copy in copies[3:]:
+    tiles[...] = tile.astype(BF16)
+    last = [
+        pltpu.make_async_copy(tiles, out.at[d, pl.ds(2 * HALF, META), :], sems.at[len(pairs) + d])
+        for d in range(NG)
+    ]
+    for copy in last:
+        copy.start()
+    for copy in copies[3:] + last:
         copy.wait()
 
 
@@ -534,9 +539,11 @@
             pltpu.SMEM(src_page.shape, jnp.int32),
             pltpu.SMEM((1, counts), jnp.int32),
             pltpu.SMEM((1, counts), jnp.int32),
-            pltpu.SemaphoreType.DMA((3 + 2 * NG,)),
+            pltpu.VMEM((META, TWO), BF16),
+            pltpu.SemaphoreType.DMA((3 + 3 * NG,)),
         ),
         specs={n: far for n in range(5)},
+        out_specs=[far],
         limit=60,
     )
     xs = lax.all_to_all(x_send, "grp", 0, 0, tiled=True)

time: 115 us -> 133 us (1.16)
  Pallas kernels: 16.7 us -> 35.6 us
    pallas_call x8, Pallas kernels: 16.7 us -> 35.6 us  [call(): pl.pallas_call(kernel, out_shape=[jax.ShapeDtypeStruct(s, t) for s, t in...]
where the time goes in v6:
time: 133 us
  starting transfers between devices  38.9 us (29%)
  blocking collectives  37.8 us (28%)
  Pallas kernels  35.6 us (27%)
  waiting for transfers between devices  19 us (14%)
    all_to_all x2, blocking collectives, exchange(): return lax.all_to_all(x, 'seq', 0, 0, axis_index_groups=groups, tiled=True)  37.8 us
    pallas_call x8, Pallas kernels, call(): pl.pallas_call(kernel, out_shape=[jax.ShapeDtypeStruct(s, t) for s, t in...  35.6 us
    ppermute x2, starting transfers between devices, to_other_core(): return lax.ppermute(x, 'seq', [(n, n ^ 1) for n in range(2 * SIDE * SIDE)])  15.4 us
    all_to_all x1, starting transfers between devices, exchange(): return lax.all_to_all(x, 'seq', 0, 0, axis_index_groups=groups, tiled=True)  9.39 us
    all_to_all x1, waiting for transfers between devices, body(): xs = lax.all_to_all(x_send, 'grp', 0, 0, tiled=True)  7.02 us
    ppermute x1, waiting for transfers between devices, body(): keys_other = lax.ppermute(keys, 'seq', NEIGHBOURS)  6.35 us
    all_to_all x1, starting transfers between devices, body(): xs = lax.all_to_all(x_send, 'grp', 0, 0, tiled=True)  4.85 us
    ppermute x1, starting transfers between devices, body(): small_other = lax.ppermute(small, 'seq', NEIGHBOURS)  4.01 us
  transfers between devices with their start and end apart: 7, of which 6 were waited for; matrix products, arithmetic and copies ran while one was open for 1% of the time, Pallas kernels for 0%

profile of v6, /device:TPU:1, one launch (start us, length us, event | category | flops | bytes accessed | tf_op | source)
XLA Modules:
  0.0 133.0 jit_solution(1691730976708668173)
XLA Ops:
  0.6 21.1 %pages.1 = bf16[4,336,256]{2,1,0:T(8,128)(2,1)} custom-call(bf16[160,1024]{1,0:T(8,128)(2,1)} %bitcast.6, bf16[160,1024]{1,0:T(8,128)(2,1)} %bitcast.7, s32[1,8]{1,0:T(1,128)} %src_page.1, s32[1,12]{1,0:T(1,128)} %page_row.1, s32[1,12]{1,0:T(1,128)} %page_len.1), custom_call_target="tpu_custom_call" | custom-call | tf_op jit(solution)/shard_map/pages/pallas_call | solution.py:88
  21.8 4.9 %all-to-all-start = ((bf16[4,336,256]{2,1,0:T(8,128)(2,1)}), bf16[4,336,256]{2,1,0:T(8,128)(2,1)S(1)}, u32[]{:S(2)}, u32[]{:S(2)}) async-start(bf16[4,336,256]{2,1,0:T(8,128)(2,1)} %pages.1), calls=%async_computation | async-start | bytes 1376256 | tf_op jit(solution)/shard_map/all_to_all | solution.py:549
  26.6 0.7 dynamic-slice_bitcast_fusion
  27.4 7.0 %all-to-all-done.xs = bf16[4,336,256]{2,1,0:T(8,128)(2,1)S(1)} async-done(((bf16[4,336,256]{2,1,0:T(8,128)(2,1)}), bf16[4,336,256]{2,1,0:T(8,128)(2,1)S(1)}, u32[]{:S(2)}, u32[]{:S(2)}) %all-to-all-start) | async-done | bytes 688160 | tf_op jit(solution)/shard_map/all_to_all | solution.py:549
  34.4 0.3 split.1
  34.7 8.6 %collective-permute-start = (bf16[400,128]{1,0:T(8,128)(2,1)S(1)}, bf16[400,128]{1,0:T(8,128)(2,1)S(1)}, u32[]{:S(2)}, u32[]{:S(2)}) collective-permute-start(bf16[400,128]{1,0:T(8,128)(2,1)S(1)} %get-tuple-element.17), channel_id=1, source_target_pairs={{0,4},{4,0},{8,12},{12,8},{16,20},{20,16},{24,28},{28,24},{32,36},... | collective-permute-start | bytes 307208 | tf_op jit(solution)/shard_map/ppermute | solution.py:526
  43.5 0.7 collective-permute-done.got
  44.2 4.1 %local.1 = (bf16[8,416,128]{2,1,0:T(8,128)(2,1)S(1)}, bf16[512,128]{1,0:T(8,128)(2,1)S(1)}) custom-call(bf16[400,128]{1,0:T(8,128)(2,1)S(1)} %get-tuple-element.16.keep, bf16[400,128]{1,0:T(8,128)(2,1)S(1)} %collective-permute-done.got, bf16[128,1024]{1,0:T(8,128)(2,1)S(1)} %reshape.15.q.q_dec, bf16[4,336,256]{2,1,0:T(8,128)(2,1)S(1)} %all-to-all-done.xs, ...), custom_call_target="tpu_custom_call" | custom-call | tf_op jit(solution)/shard_map/local/pallas_call | solution.py:88
  48.3 20.0 %all_to_all.20.got = bf16[8,416,128]{2,1,0:T(8,128)(2,1)S(1)} all-to-all(bf16[8,416,128]{2,1,0:T(8,128)(2,1)S(1)} %get-tuple-element.19), channel_id=1, replica_groups={{0,64,128,192,256,320,384,448},{8,72,136,200,264,328,392,456},{16,80,14..., dimensions={0} | all-to-all | bytes 1703936 | tf_op jit(solution)/shard_map/all_to_all | solution.py:522
  68.3 0.3 merge.1
  68.6 4.0 %collective-permute-start.1 = (bf16[96,128]{1,0:T(8,128)(2,1)S(1)}, bf16[96,128]{1,0:T(8,128)(2,1)S(1)}, u32[]{:S(2)}, u32[]{:S(2)}) collective-permute-start(bf16[96,128]{1,0:T(8,128)(2,1)S(1)} %get-tuple-element.20.mine), channel_id=1, source_target_pairs={{0,8},{8,0},{16,24},{24,16},{32,40},{40,32},{48,56},{56,48},{64,72... | collective-permute-start | bytes 73736 | tf_op jit(solution)/shard_map/ppermute | solution.py:580
  72.6 1.2 collective-permute-done.1.other
  73.8 1.0 queries.1
  74.8 9.4 %all-to-all-start.2 = ((bf16[4,560,128]{2,1,0:T(8,128)(2,1)}), bf16[4,560,128]{2,1,0:T(8,128)(2,1)S(1)}, u32[]{:S(2)}, u32[]{:S(2)}) async-start(bf16[4,560,128]{2,1,0:T(8,128)(2,1)} %queries.1), calls=%async_computation.2 | async-start | bytes 1146880 | tf_op jit(solution)/shard_map/all_to_all | solution.py:522
  84.2 3.1 %collective-permute-start.2 = (bf16[1024,128]{1,0:T(8,128)(2,1)S(1)}, bf16[1024,128]{1,0:T(8,128)(2,1)S(1)}, u32[]{:S(2)}, u32[]{:S(2)}) collective-permute-start(bf16[1024,128]{1,0:T(8,128)(2,1)S(1)} %get-tuple-element.25.keys), channel_id=1, source_target_pairs={{0,8},{8,0},{16,24},{24,16},{32,40},{40,32},{48,56},{56,48},{64,72... | collective-permute-start | bytes 786440 | tf_op jit(solution)/shard_map/ppermute | solution.py:582
  87.3 2.2 %collective-permute-start.3 = (bf16[1024,128]{1,0:T(8,128)(2,1)S(1)}, bf16[1024,128]{1,0:T(8,128)(2,1)S(1)}, u32[]{:S(2)}, u32[]{:S(2)}) collective-permute-start(bf16[1024,128]{1,0:T(8,128)(2,1)S(1)} %get-tuple-element.26.vals), channel_id=1, source_target_pairs={{0,8},{8,0},{16,24},{24,16},{32,40},{40,32},{48,56},{56,48},{64,72... | collective-permute-start | bytes 786440 | tf_op jit(solution)/shard_map/ppermute | solution.py:583
  89.5 6.4 %collective-permute-done.2.keys_other = bf16[1024,128]{1,0:T(8,128)(2,1)S(1)} collective-permute-done((bf16[1024,128]{1,0:T(8,128)(2,1)S(1)}, bf16[1024,128]{1,0:T(8,128)(2,1)S(1)}, u32[]{:S(2)}, u32[]{:S(2)}) %collective-permute-start.2) | collective-permute-done | bytes 262176 | tf_op jit(solution)/shard_map/ppermute | solution.py:582
  95.8 2.8 %collective-permute-done.3.vals_other = bf16[1024,128]{1,0:T(8,128)(2,1)S(1)} collective-permute-done((bf16[1024,128]{1,0:T(8,128)(2,1)S(1)}, bf16[1024,128]{1,0:T(8,128)(2,1)S(1)}, u32[]{:S(2)}, u32[]{:S(2)}) %collective-permute-start.3) | collective-permute-done | bytes 262176 | tf_op jit(solution)/shard_map/ppermute | solution.py:583
  98.6 7.2 %attend.1 = bf16[4,544,128]{2,1,0:T(8,128)(2,1)S(1)} custom-call(bf16[4,560,128]{2,1,0:T(8,128)(2,1)S(1)} %all-to-all-done.2.qs, bf16[1024,128]{1,0:T(8,128)(2,1)S(1)} %get-tuple-element.25.keys, bf16[1024,128]{1,0:T(8,128)(2,1)S(1)} %collective-permute-done.2.keys_other, bf16[1024,128]{1,0:T(8,128)(2,1)S(1)} %get-tuple-element.26.vals, ...), custom_call_target="tpu_custom_call" | custom-call | flops 2147483648 | bytes 4194304 | tf_op jit(solution)/shard_map/attend/pallas_call | solution.py:88
  105.8 17.8 %all_to_all.21.got = bf16[4,544,128]{2,1,0:T(8,128)(2,1)S(1)} all-to-all(bf16[4,544,128]{2,1,0:T(8,128)(2,1)S(1)} %attend.1), channel_id=1, replica_groups={{0,16,32,48},{8,24,40,56},{64,80,96,112},{72,88,104,120},{128,144,160,1..., dimensions={0} | all-to-all | bytes 1114112 | tf_op jit(solution)/shard_map/all_to_all | solution.py:522
  123.7 0.9 pair.1
  124.5 6.8 %collective-permute-start.4 = (bf16[272,128]{1,0:T(8,128)(2,1)S(1)}, bf16[272,128]{1,0:T(8,128)(2,1)S(1)}, u32[]{:S(2)}, u32[]{:S(2)}) collective-permute-start(bf16[272,128]{1,0:T(8,128)(2,1)S(1)} %get-tuple-element.29), channel_id=1, source_target_pairs={{0,4},{4,0},{8,12},{12,8},{16,20},{20,16},{24,28},{28,24},{32,36},... | collective-permute-start | bytes 208904 | tf_op jit(solution)/shard_map/ppermute | solution.py:526
  131.4 0.9 collective-permute-done.4.got
  132.3 0.8 final.1
  (13 shorter events, 0.2 us)
Async XLA Ops:
  0.6 42.7 %copy-start = (bf16[32,4,4096]{2,1,0:T(4,128)(2,1)S(1)}, bf16[32,4,4096]{2,1,0:T(4,128)(2,1)}, u32[]{:S(2)}) copy-start(bf16[32,4,4096]{2,1,0:T(4,128)(2,1)} %param.19) | copy-start | bytes 3145732
  21.8 12.7 %all-to-all-start = ((bf16[4,336,256]{2,1,0:T(8,128)(2,1)}), bf16[4,336,256]{2,1,0:T(8,128)(2,1)S(1)}, u32[]{:S(2)}, u32[]{:S(2)}) async-start(bf16[4,336,256]{2,1,0:T(8,128)(2,1)} %pages.1), calls=%async_computation | async-start | bytes 1376256 | tf_op jit(solution)/shard_map/all_to_all | solution.py:549
  26.6 7.8 %copy-start.1 = (bf16[64,1024]{1,0:T(8,128)(2,1)S(1)}, bf16[64,1024]{1,0:T(8,128)(2,1)}, u32[]{:S(2)}) copy-start(bf16[64,1024]{1,0:T(8,128)(2,1)} %q.1) | copy-start | bytes 393220
  27.4 7.1 %copy-start.2 = (bf16[64,256]{1,0:T(8,128)(2,1)S(1)}, bf16[64,256]{1,0:T(8,128)(2,1)}, u32[]{:S(2)}) copy-start(bf16[64,256]{1,0:T(8,128)(2,1)} %k.1) | copy-start | bytes 98308
  27.4 7.1 %copy-start.3 = (bf16[64,256]{1,0:T(8,128)(2,1)S(1)}, bf16[64,256]{1,0:T(8,128)(2,1)}, u32[]{:S(2)}) copy-start(bf16[64,256]{1,0:T(8,128)(2,1)} %v.1) | copy-start | bytes 98308
  34.7 9.5 %collective-permute-start = (bf16[400,128]{1,0:T(8,128)(2,1)S(1)}, bf16[400,128]{1,0:T(8,128)(2,1)S(1)}, u32[]{:S(2)}, u32[]{:S(2)}) collective-permute-start(bf16[400,128]{1,0:T(8,128)(2,1)S(1)} %get-tuple-element.17), channel_id=1, source_target_pairs={{0,4},{4,0},{8,12},{12,8},{16,20},{20,16},{24,28},{28,24},{32,36},... | collective-permute-start | bytes 307208 | tf_op jit(solution)/shard_map/ppermute | solution.py:526
  68.6 5.2 %collective-permute-start.1 = (bf16[96,128]{1,0:T(8,128)(2,1)S(1)}, bf16[96,128]{1,0:T(8,128)(2,1)S(1)}, u32[]{:S(2)}, u32[]{:S(2)}) collective-permute-start(bf16[96,128]{1,0:T(8,128)(2,1)S(1)} %get-tuple-element.20.mine), channel_id=1, source_target_pairs={{0,8},{8,0},{16,24},{24,16},{32,40},{40,32},{48,56},{56,48},{64,72... | collective-permute-start | bytes 73736 | tf_op jit(solution)/shard_map/ppermute | solution.py:580
  74.8 23.8 %all-to-all-start.2 = ((bf16[4,560,128]{2,1,0:T(8,128)(2,1)}), bf16[4,560,128]{2,1,0:T(8,128)(2,1)S(1)}, u32[]{:S(2)}, u32[]{:S(2)}) async-start(bf16[4,560,128]{2,1,0:T(8,128)(2,1)} %queries.1), calls=%async_computation.2 | async-start | bytes 1146880 | tf_op jit(solution)/shard_map/all_to_all | solution.py:522
  84.2 11.6 %collective-permute-start.2 = (bf16[1024,128]{1,0:T(8,128)(2,1)S(1)}, bf16[1024,128]{1,0:T(8,128)(2,1)S(1)}, u32[]{:S(2)}, u32[]{:S(2)}) collective-permute-start(bf16[1024,128]{1,0:T(8,128)(2,1)S(1)} %get-tuple-element.25.keys), channel_id=1, source_target_pairs={{0,8},{8,0},{16,24},{24,16},{32,40},{40,32},{48,56},{56,48},{64,72... | collective-permute-start | bytes 786440 | tf_op jit(solution)/shard_map/ppermute | solution.py:582
  87.3 11.4 %collective-permute-start.3 = (bf16[1024,128]{1,0:T(8,128)(2,1)S(1)}, bf16[1024,128]{1,0:T(8,128)(2,1)S(1)}, u32[]{:S(2)}, u32[]{:S(2)}) collective-permute-start(bf16[1024,128]{1,0:T(8,128)(2,1)S(1)} %get-tuple-element.26.vals), channel_id=1, source_target_pairs={{0,8},{8,0},{16,24},{24,16},{32,40},{40,32},{48,56},{56,48},{64,72... | collective-permute-start | bytes 786440 | tf_op jit(solution)/shard_map/ppermute | solution.py:583
  124.5 7.7 %collective-permute-start.4 = (bf16[272,128]{1,0:T(8,128)(2,1)S(1)}, bf16[272,128]{1,0:T(8,128)(2,1)S(1)}, u32[]{:S(2)}, u32[]{:S(2)}) collective-permute-start(bf16[272,128]{1,0:T(8,128)(2,1)S(1)} %get-tuple-element.29), channel_id=1, source_target_pairs={{0,4},{4,0},{8,12},{12,8},{16,20},{20,16},{24,28},{28,24},{32,36},... | collective-permute-start | bytes 208904 | tf_op jit(solution)/shard_map/ppermute | solution.py:526

commit v7 on v5

--- a/solution.py
+++ b/solution.py
@@ -153,6 +153,18 @@
         copy.wait()
 
 
+def item_order(core):
+    i = iota((ITEMS, 128), 0)
+    swapped = ((i >> 1) & 7) * 16 + (i >> 4) * 2 + (i & 1)
+    return jnp.where(core == 0, i, swapped)
+
+
+def order_kernel(q, out):
+    flag = item_order(spot()[4]) == iota((ITEMS, 128), 1)
+    order = jnp.where(flag, 1.0, 0.0).astype(BF16)
+    out[...] = jnp.dot(order, q[...], preferred_element_type=F32).astype(BF16)
+
+
 def local_kernel(keep, got, q, xs, k_dec, v_dec, kv_send, q_blk, ks, vs, cs, kb):
     seq, _, _, _, core, _, _ = spot()
     for src, start in ((keep, core * TOK), (got, (1 - core) * TOK)):
@@ -177,9 +189,7 @@
     def hot(flag):
         return jnp.where(flag, 1.0, 0.0).astype(BF16)
 
-    i = iota((ITEMS, 128), 0)
-    swapped = ((i >> 1) & 7) * 16 + (i >> 4) * 2 + (i & 1)
-    which = jnp.where(core == 0, i, swapped)
+    which = item_order(core)
     lane = iota((ITEMS, 128), 1)
     row = (which >> 2).astype(F32)
     token = iota((OLD_TOK, 128), 0)
@@ -196,11 +206,10 @@
     cs[:, :OLD_TOK] = count
     cs[:, OLD_TOK:] = jnp.where((which == seq) & (lane <= (seq & 3)), 1.0, 0.0)
 
-    order = hot(which == lane)
     stats = jnp.zeros((ITEMS, 128), F32)
     for h in range(HEADS):
         kv = slice(h // 4 * HEAD, (h // 4 + 1) * HEAD)
-        query = jnp.dot(order, q[:, h * HEAD : (h + 1) * HEAD], preferred_element_type=F32).astype(BF16)
+        query = q[:, h * HEAD : (h + 1) * HEAD]
         scores = EXP2_SCALE * lax.dot_general(query, ks[:, kv], NT, preferred_element_type=F32)
         terms = cs[...]
         scores = jnp.where(terms > 0.5, scores, NEG)
@@ -550,6 +559,8 @@
     q_mine = lax.dynamic_slice_in_dim(q_dec, grp * HEADS * HEAD, HEADS * HEAD, 2)
     q_mine = q_mine.reshape(ITEMS, HEADS * HEAD)
 
+    (q_ordered,) = call(order_kernel, [((ITEMS, HEADS * HEAD), BF16)], (q_mine,))
+
     def own_tokens(x):
         part = lax.dynamic_slice(x, (seq // STEPS, 0, grp * TWO), (1, STEPS, TWO))[0]
         return jnp.pad(part, ((0, 128 - STEPS), (0, 0)))
@@ -557,7 +568,7 @@
     kv_send, q_blk = call(
         local_kernel,
         [((SIDE, KV_MSG, 128), BF16), ((QROWS, 128), BF16)],
-        (keep, to_other_core(send), q_mine, xs, own_tokens(dec_k), own_tokens(dec_v)),
+        (keep, to_other_core(send), q_ordered, xs, own_tokens(dec_k), own_tokens(dec_v)),
         scratch=(
             pltpu.VMEM((DEC_TOK, TWO), BF16),
             pltpu.VMEM((DEC_TOK, TWO), BF16),

time: 115 us -> 114 us (level)
    pallas_call x8 -> x9, Pallas kernels: 16.7 us -> 15.9 us  [call(): pl.pallas_call(kernel, out_shape=[jax.ShapeDtypeStruct(s, t) for s, t in...]
where the time goes in v7:
time: 114 us; the launch traced here: 113 us
  starting transfers between devices  38.9 us (34%)
  blocking collectives  37.8 us (33%)
  waiting for transfers between devices  18.8 us (16%)
  Pallas kernels  15.9 us (14%)
    all_to_all x2, blocking collectives, exchange(): return lax.all_to_all(x, 'seq', 0, 0, axis_index_groups=groups, tiled=True)  37.8 us
    pallas_call x9, Pallas kernels, call(): pl.pallas_call(kernel, out_shape=[jax.ShapeDtypeStruct(s, t) for s, t in...  15.9 us
    ppermute x2, starting transfers between devices, to_other_core(): return lax.ppermute(x, 'seq', [(n, n ^ 1) for n in range(2 * SIDE * SIDE)])  15.4 us
    all_to_all x1, starting transfers between devices, exchange(): return lax.all_to_all(x, 'seq', 0, 0, axis_index_groups=groups, tiled=True)  9.38 us
    all_to_all x1, waiting for transfers between devices, body(): xs = lax.all_to_all(x_send, 'grp', 0, 0, tiled=True)  7.02 us
    ppermute x1, waiting for transfers between devices, body(): keys_other = lax.ppermute(keys, 'seq', NEIGHBOURS)  6.36 us
    all_to_all x1, starting transfers between devices, body(): xs = lax.all_to_all(x_send, 'grp', 0, 0, tiled=True)  4.85 us
    ppermute x1, starting transfers between devices, body(): small_other = lax.ppermute(small, 'seq', NEIGHBOURS)  4 us
  transfers between devices with their start and end apart: 7, of which 6 were waited for; matrix products, arithmetic and copies ran while one was open for 1% of the time, Pallas kernels for 0%

profile of v7, /device:TPU:1, one launch (start us, length us, event | category | flops | bytes accessed | tf_op | source)
XLA Modules:
  0.0 113.2 jit_solution(5438088800512628375)
XLA Ops:
  0.6 2.2 %pages.1 = bf16[4,336,256]{2,1,0:T(8,128)(2,1)} custom-call(bf16[160,1024]{1,0:T(8,128)(2,1)} %bitcast.6, bf16[160,1024]{1,0:T(8,128)(2,1)} %bitcast.7, s32[1,8]{1,0:T(1,128)} %src_page.1, s32[1,12]{1,0:T(1,128)} %page_row.1, s32[1,12]{1,0:T(1,128)} %page_len.1), custom_call_target="tpu_custom_call" | custom-call | tf_op jit(solution)/shard_map/pages/pallas_call | solution.py:88
  2.9 4.9 %all-to-all-start = ((bf16[4,336,256]{2,1,0:T(8,128)(2,1)}), bf16[4,336,256]{2,1,0:T(8,128)(2,1)S(1)}, u32[]{:S(2)}, u32[]{:S(2)}) async-start(bf16[4,336,256]{2,1,0:T(8,128)(2,1)} %pages.1), calls=%async_computation | async-start | bytes 1376256 | tf_op jit(solution)/shard_map/all_to_all | solution.py:551
  7.7 0.7 dynamic-slice_bitcast_fusion
  8.5 7.0 %all-to-all-done.xs = bf16[4,336,256]{2,1,0:T(8,128)(2,1)S(1)} async-done(((bf16[4,336,256]{2,1,0:T(8,128)(2,1)}), bf16[4,336,256]{2,1,0:T(8,128)(2,1)S(1)}, u32[]{:S(2)}, u32[]{:S(2)}) %all-to-all-start) | async-done | bytes 688160 | tf_op jit(solution)/shard_map/all_to_all | solution.py:551
  15.6 0.3 split.1
  15.9 8.6 %collective-permute-start = (bf16[400,128]{1,0:T(8,128)(2,1)S(1)}, bf16[400,128]{1,0:T(8,128)(2,1)S(1)}, u32[]{:S(2)}, u32[]{:S(2)}) collective-permute-start(bf16[400,128]{1,0:T(8,128)(2,1)S(1)} %get-tuple-element.17), channel_id=1, source_target_pairs={{0,4},{4,0},{8,12},{12,8},{16,20},{20,16},{24,28},{28,24},{32,36},... | collective-permute-start | bytes 307208 | tf_op jit(solution)/shard_map/ppermute | solution.py:530
  24.8 0.5 collective-permute-done.got
  25.3 3.1 %local.1 = (bf16[8,416,128]{2,1,0:T(8,128)(2,1)S(1)}, bf16[512,128]{1,0:T(8,128)(2,1)S(1)}) custom-call(bf16[400,128]{1,0:T(8,128)(2,1)S(1)} %get-tuple-element.16.keep, bf16[400,128]{1,0:T(8,128)(2,1)S(1)} %collective-permute-done.got, bf16[128,1024]{1,0:T(8,128)(2,1)S(1)} %order.1.q, bf16[4,336,256]{2,1,0:T(8,128)(2,1)S(1)} %all-to-all-done.xs, ...), custom_call_target="tpu_custom_call" | custom-call | tf_op jit(solution)/shard_map/local/pallas_call | solution.py:88
  28.4 20.0 %all_to_all.20.got = bf16[8,416,128]{2,1,0:T(8,128)(2,1)S(1)} all-to-all(bf16[8,416,128]{2,1,0:T(8,128)(2,1)S(1)} %get-tuple-element.19), channel_id=1, replica_groups={{0,64,128,192,256,320,384,448},{8,72,136,200,264,328,392,456},{16,80,14..., dimensions={0} | all-to-all | bytes 1703936 | tf_op jit(solution)/shard_map/all_to_all | solution.py:526
  48.4 0.3 merge.1
  48.7 4.0 %collective-permute-start.1 = (bf16[96,128]{1,0:T(8,128)(2,1)S(1)}, bf16[96,128]{1,0:T(8,128)(2,1)S(1)}, u32[]{:S(2)}, u32[]{:S(2)}) collective-permute-start(bf16[96,128]{1,0:T(8,128)(2,1)S(1)} %get-tuple-element.20.mine), channel_id=1, source_target_pairs={{0,8},{8,0},{16,24},{24,16},{32,40},{40,32},{48,56},{56,48},{64,72... | collective-permute-start | bytes 73736 | tf_op jit(solution)/shard_map/ppermute | solution.py:584
  52.7 1.2 %collective-permute-done.1.other = bf16[96,128]{1,0:T(8,128)(2,1)S(1)} collective-permute-done((bf16[96,128]{1,0:T(8,128)(2,1)S(1)}, bf16[96,128]{1,0:T(8,128)(2,1)S(1)}, u32[]{:S(2)}, u32[]{:S(2)}) %collective-permute-start.1) | collective-permute-done | bytes 24608 | tf_op jit(solution)/shard_map/ppermute | solution.py:584
  53.9 1.0 queries.1
  54.9 9.4 %all-to-all-start.2 = ((bf16[4,560,128]{2,1,0:T(8,128)(2,1)}), bf16[4,560,128]{2,1,0:T(8,128)(2,1)S(1)}, u32[]{:S(2)}, u32[]{:S(2)}) async-start(bf16[4,560,128]{2,1,0:T(8,128)(2,1)} %queries.1), calls=%async_computation.2 | async-start | bytes 1146880 | tf_op jit(solution)/shard_map/all_to_all | solution.py:526
  64.3 3.1 %collective-permute-start.2 = (bf16[1024,128]{1,0:T(8,128)(2,1)S(1)}, bf16[1024,128]{1,0:T(8,128)(2,1)S(1)}, u32[]{:S(2)}, u32[]{:S(2)}) collective-permute-start(bf16[1024,128]{1,0:T(8,128)(2,1)S(1)} %get-tuple-element.25.keys), channel_id=1, source_target_pairs={{0,8},{8,0},{16,24},{24,16},{32,40},{40,32},{48,56},{56,48},{64,72... | collective-permute-start | bytes 786440 | tf_op jit(solution)/shard_map/ppermute | solution.py:586
  67.4 2.2 %collective-permute-start.3 = (bf16[1024,128]{1,0:T(8,128)(2,1)S(1)}, bf16[1024,128]{1,0:T(8,128)(2,1)S(1)}, u32[]{:S(2)}, u32[]{:S(2)}) collective-permute-start(bf16[1024,128]{1,0:T(8,128)(2,1)S(1)} %get-tuple-element.26.vals), channel_id=1, source_target_pairs={{0,8},{8,0},{16,24},{24,16},{32,40},{40,32},{48,56},{56,48},{64,72... | collective-permute-start | bytes 786440 | tf_op jit(solution)/shard_map/ppermute | solution.py:587
  69.6 6.4 %collective-permute-done.2.keys_other = bf16[1024,128]{1,0:T(8,128)(2,1)S(1)} collective-permute-done((bf16[1024,128]{1,0:T(8,128)(2,1)S(1)}, bf16[1024,128]{1,0:T(8,128)(2,1)S(1)}, u32[]{:S(2)}, u32[]{:S(2)}) %collective-permute-start.2) | collective-permute-done | bytes 262176 | tf_op jit(solution)/shard_map/ppermute | solution.py:586
  75.9 2.8 %collective-permute-done.3.vals_other = bf16[1024,128]{1,0:T(8,128)(2,1)S(1)} collective-permute-done((bf16[1024,128]{1,0:T(8,128)(2,1)S(1)}, bf16[1024,128]{1,0:T(8,128)(2,1)S(1)}, u32[]{:S(2)}, u32[]{:S(2)}) %collective-permute-start.3) | collective-permute-done | bytes 262176 | tf_op jit(solution)/shard_map/ppermute | solution.py:587
  78.7 7.2 %attend.1 = bf16[4,544,128]{2,1,0:T(8,128)(2,1)S(1)} custom-call(bf16[4,560,128]{2,1,0:T(8,128)(2,1)S(1)} %all-to-all-done.2.qs, bf16[1024,128]{1,0:T(8,128)(2,1)S(1)} %get-tuple-element.25.keys, bf16[1024,128]{1,0:T(8,128)(2,1)S(1)} %collective-permute-done.2.keys_other, bf16[1024,128]{1,0:T(8,128)(2,1)S(1)} %get-tuple-element.26.vals, ...), custom_call_target="tpu_custom_call" | custom-call | flops 2147483648 | bytes 4194304 | tf_op jit(solution)/shard_map/attend/pallas_call | solution.py:88
  85.9 17.8 %all_to_all.21.got = bf16[4,544,128]{2,1,0:T(8,128)(2,1)S(1)} all-to-all(bf16[4,544,128]{2,1,0:T(8,128)(2,1)S(1)} %attend.1), channel_id=1, replica_groups={{0,16,32,48},{8,24,40,56},{64,80,96,112},{72,88,104,120},{128,144,160,1..., dimensions={0} | all-to-all | bytes 1114112 | tf_op jit(solution)/shard_map/all_to_all | solution.py:526
  103.8 0.9 pair.1
  104.6 6.8 %collective-permute-start.4 = (bf16[272,128]{1,0:T(8,128)(2,1)S(1)}, bf16[272,128]{1,0:T(8,128)(2,1)S(1)}, u32[]{:S(2)}, u32[]{:S(2)}) collective-permute-start(bf16[272,128]{1,0:T(8,128)(2,1)S(1)} %get-tuple-element.29), channel_id=1, source_target_pairs={{0,4},{4,0},{8,12},{12,8},{16,20},{20,16},{24,28},{28,24},{32,36},... | collective-permute-start | bytes 208904 | tf_op jit(solution)/shard_map/ppermute | solution.py:530
  111.5 0.9 collective-permute-done.4.got
  112.4 0.8 final.1
  (14 shorter events, 0.4 us)
Async XLA Ops:
  0.6 23.8 %copy-start = (bf16[32,4,4096]{2,1,0:T(4,128)(2,1)S(1)}, bf16[32,4,4096]{2,1,0:T(4,128)(2,1)}, u32[]{:S(2)}) copy-start(bf16[32,4,4096]{2,1,0:T(4,128)(2,1)} %param.19) | copy-start | bytes 3145732
  2.9 12.7 %all-to-all-start = ((bf16[4,336,256]{2,1,0:T(8,128)(2,1)}), bf16[4,336,256]{2,1,0:T(8,128)(2,1)S(1)}, u32[]{:S(2)}, u32[]{:S(2)}) async-start(bf16[4,336,256]{2,1,0:T(8,128)(2,1)} %pages.1), calls=%async_computation | async-start | bytes 1376256 | tf_op jit(solution)/shard_map/all_to_all | solution.py:551
  7.7 7.8 %copy-start.1 = (bf16[64,1024]{1,0:T(8,128)(2,1)S(1)}, bf16[64,1024]{1,0:T(8,128)(2,1)}, u32[]{:S(2)}) copy-start(bf16[64,1024]{1,0:T(8,128)(2,1)} %q.1) | copy-start | bytes 393220
  8.5 7.1 %copy-start.2 = (bf16[64,256]{1,0:T(8,128)(2,1)S(1)}, bf16[64,256]{1,0:T(8,128)(2,1)}, u32[]{:S(2)}) copy-start(bf16[64,256]{1,0:T(8,128)(2,1)} %k.1) | copy-start | bytes 98308
  8.5 7.1 %copy-start.3 = (bf16[64,256]{1,0:T(8,128)(2,1)S(1)}, bf16[64,256]{1,0:T(8,128)(2,1)}, u32[]{:S(2)}) copy-start(bf16[64,256]{1,0:T(8,128)(2,1)} %v.1) | copy-start | bytes 98308
  15.9 9.5 %collective-permute-start = (bf16[400,128]{1,0:T(8,128)(2,1)S(1)}, bf16[400,128]{1,0:T(8,128)(2,1)S(1)}, u32[]{:S(2)}, u32[]{:S(2)}) collective-permute-start(bf16[400,128]{1,0:T(8,128)(2,1)S(1)} %get-tuple-element.17), channel_id=1, source_target_pairs={{0,4},{4,0},{8,12},{12,8},{16,20},{20,16},{24,28},{28,24},{32,36},... | collective-permute-start | bytes 307208 | tf_op jit(solution)/shard_map/ppermute | solution.py:530
  48.7 5.2 %collective-permute-start.1 = (bf16[96,128]{1,0:T(8,128)(2,1)S(1)}, bf16[96,128]{1,0:T(8,128)(2,1)S(1)}, u32[]{:S(2)}, u32[]{:S(2)}) collective-permute-start(bf16[96,128]{1,0:T(8,128)(2,1)S(1)} %get-tuple-element.20.mine), channel_id=1, source_target_pairs={{0,8},{8,0},{16,24},{24,16},{32,40},{40,32},{48,56},{56,48},{64,72... | collective-permute-start | bytes 73736 | tf_op jit(solution)/shard_map/ppermute | solution.py:584
  54.9 23.8 %all-to-all-start.2 = ((bf16[4,560,128]{2,1,0:T(8,128)(2,1)}), bf16[4,560,128]{2,1,0:T(8,128)(2,1)S(1)}, u32[]{:S(2)}, u32[]{:S(2)}) async-start(bf16[4,560,128]{2,1,0:T(8,128)(2,1)} %queries.1), calls=%async_computation.2 | async-start | bytes 1146880 | tf_op jit(solution)/shard_map/all_to_all | solution.py:526
  64.3 11.6 %collective-permute-start.2 = (bf16[1024,128]{1,0:T(8,128)(2,1)S(1)}, bf16[1024,128]{1,0:T(8,128)(2,1)S(1)}, u32[]{:S(2)}, u32[]{:S(2)}) collective-permute-start(bf16[1024,128]{1,0:T(8,128)(2,1)S(1)} %get-tuple-element.25.keys), channel_id=1, source_target_pairs={{0,8},{8,0},{16,24},{24,16},{32,40},{40,32},{48,56},{56,48},{64,72... | collective-permute-start | bytes 786440 | tf_op jit(solution)/shard_map/ppermute | solution.py:586
  67.4 11.4 %collective-permute-start.3 = (bf16[1024,128]{1,0:T(8,128)(2,1)S(1)}, bf16[1024,128]{1,0:T(8,128)(2,1)S(1)}, u32[]{:S(2)}, u32[]{:S(2)}) collective-permute-start(bf16[1024,128]{1,0:T(8,128)(2,1)S(1)} %get-tuple-element.26.vals), channel_id=1, source_target_pairs={{0,8},{8,0},{16,24},{24,16},{32,40},{40,32},{48,56},{56,48},{64,72... | collective-permute-start | bytes 786440 | tf_op jit(solution)/shard_map/ppermute | solution.py:587
  104.6 7.7 %collective-permute-start.4 = (bf16[272,128]{1,0:T(8,128)(2,1)S(1)}, bf16[272,128]{1,0:T(8,128)(2,1)S(1)}, u32[]{:S(2)}, u32[]{:S(2)}) collective-permute-start(bf16[272,128]{1,0:T(8,128)(2,1)S(1)} %get-tuple-element.29), channel_id=1, source_target_pairs={{0,4},{4,0},{8,12},{12,8},{16,20},{20,16},{24,28},{28,24},{32,36},... | collective-permute-start | bytes 208904 | tf_op jit(solution)/shard_map/ppermute | solution.py:530
